TPU v7x, 32 devices: a whole 2x2x4 slice. The times are simulated.
32 devices in a mesh: img: 8 (over z, y), ty: 2 (over x), tx: 2 (over core).
Axes of the slice: x: 2, y: 2, z: 4, core: 2. Of those that a mesh axis runs over, the one named last changes fastest.
Arguments:
- tokens: bfloat16 [8, 32, 32, 1152], P('img', 'ty', 'tx'), may hold values from -6 to 6
- cond: bfloat16 [8, 1152], P('img'), may hold values from -6 to 6
- live_count: int32 [8], P('img'), may hold values from 1 to 1, as said below
- w_qkv: bfloat16 [1152, 3456], P('img'), may hold values from -0.1875 to 0.1875
- w_out: bfloat16 [1152, 1152], P('img'), may hold values from -0.75 to 0.75
- w_gu: bfloat16 [1152, 6144], P('img'), may hold values from -0.1875 to 0.1875
- w_down: bfloat16 [3072, 1152], P('img'), may hold values from -0.109375 to 0.109375
- w_ada: bfloat16 [1152, 6912], P('img'), may hold values from -0.1875 to 0.1875
- ada_bias: float32 [6912], replicated, may hold values from -3 to 3
- q_gain: float32 [72], replicated, may hold values from 0.8 to 1.6
- k_gain: float32 [72], replicated, may hold values from 0.8 to 1.6
- cotangent: bfloat16 [8, 32, 32, 1152], P('img', 'ty', 'tx'), may hold values from -6 to 6
Outputs:
- output: bfloat16 [8, 32, 32, 1152], P('img', 'ty', 'tx')
- grad_tokens: bfloat16 [8, 32, 32, 1152], P('img', 'ty', 'tx')
- grad_cond: bfloat16 [8, 1152], P('img')
- grad_w_qkv: float32 [1152, 3456], P('img', ('ty', 'tx'))
- grad_w_out: float32 [1152, 1152], P('img', ('ty', 'tx'))
- grad_w_gu: float32 [1152, 6144], P('img', ('ty', 'tx'))
- grad_w_down: float32 [3072, 1152], P('img', ('ty', 'tx'))
- grad_w_ada: float32 [1152, 6912], P('img', ('ty', 'tx'))
- grad_q_gain: float32 [72], replicated
- grad_k_gain: float32 [72], replicated
- grad_ada_bias: float32 [6912], replicated
Inputs may be any that keep to these rules, and one draw needn't show every extreme that they name: `live_count`: each index of img holds 1 to 1 live images, in its first slots; in every draw some index holds 1.
All inputs are finite; a program needn't handle non-finite values.
Results may differ from a plain program's by a relative error of at most 0.015.
Values may be sent and summed in bfloat16 or wider, within the bound.
No kernel may reach another device: no remote copies, remote signals or barrier semaphores. Data moves between devices by JAX's collectives and lax.ppermute only.
A program may use at most 320 MiB of HBM per device.

v0:
```python
import math

import jax
import jax.numpy as jnp
from jax import lax
from jax.sharding import PartitionSpec as P

HEADS = 16
HEAD = 72
FF = 3072


epsilon = 1e-06


def inverse_rms(values):
    return lax.rsqrt(jnp.mean(values * values, axis=-1, keepdims=True) + epsilon)


def rope_tables(row_pos, col_pos, quarter):
    freqs = 10000.0 ** (-jnp.arange(quarter, dtype=jnp.float32) / quarter)
    angles = jnp.stack([row_pos[:, None] * freqs, col_pos[:, None] * freqs], axis=1)
    return (jnp.cos(angles), jnp.sin(angles))


def rotate(values, cosine, sine):
    quarter = values.shape[-1] // 4
    shaped = values.reshape(values.shape[:-1] + (2, 2, quarter))
    first_half = shaped[..., 0, :]
    other_half = shaped[..., 1, :]
    cos_b = cosine[:, None]
    sin_b = sine[:, None]
    turned = jnp.stack(
        [first_half * cos_b - other_half * sin_b, first_half * sin_b + other_half * cos_b], axis=-2
    )
    return turned.reshape(values.shape)


def unrotate(values, cosine, sine):
    quarter = values.shape[-1] // 4
    shaped = values.reshape(values.shape[:-1] + (2, 2, quarter))
    first_half = shaped[..., 0, :]
    other_half = shaped[..., 1, :]
    cos_b = cosine[:, None]
    sin_b = sine[:, None]
    turned = jnp.stack(
        [first_half * cos_b + other_half * sin_b, other_half * cos_b - first_half * sin_b], axis=-2
    )
    return turned.reshape(values.shape)


def contract_rows(left, right):
    return lax.dot_general(
        left, right, (((0,), (0,)), ((), ())), preferred_element_type=jnp.float32
    )


def contract_cols(left, right):
    return lax.dot_general(
        left, right, (((1,), (1,)), ((), ())), preferred_element_type=jnp.float32
    )


def norm_back(grad_out, normed, inv_scale):
    return inv_scale * (grad_out - normed * jnp.mean(grad_out * normed, axis=-1, keepdims=True))


def attend_forward(queries, keys_all, values_all):
    logits = jnp.einsum(
        "qhd,khd->hqk", queries, keys_all, preferred_element_type=jnp.float32
    ) / math.sqrt(queries.shape[-1])
    row_max = jnp.max(logits, axis=-1, keepdims=True)
    exp_terms = jnp.exp(logits - row_max)
    exp_total = jnp.sum(exp_terms, axis=-1, keepdims=True)
    probs_low = (exp_terms / exp_total).astype(jnp.bfloat16)
    result = jnp.einsum("hqk,khd->qhd", probs_low, values_all, preferred_element_type=jnp.float32)
    return (result, row_max + jnp.log(exp_total))


def attend_backward(queries, keys_all, values_all, log_total, grad_mixed):
    root_head = math.sqrt(queries.shape[-1])
    logits = (
        jnp.einsum("qhd,khd->hqk", queries, keys_all, preferred_element_type=jnp.float32)
        / root_head
    )
    probs = jnp.exp(logits - log_total)
    grad_probs = jnp.einsum(
        "qhd,khd->hqk", grad_mixed, values_all, preferred_element_type=jnp.float32
    )
    row_dot = jnp.sum(probs * grad_probs, axis=-1, keepdims=True)
    grad_logits = (probs * (grad_probs - row_dot)).astype(jnp.bfloat16)
    grad_q = (
        jnp.einsum("hqk,khd->qhd", grad_logits, keys_all, preferred_element_type=jnp.float32)
        / root_head
    )
    grad_k = (
        jnp.einsum("hqk,qhd->khd", grad_logits, queries, preferred_element_type=jnp.float32)
        / root_head
    )
    grad_v = jnp.einsum(
        "hqk,qhd->khd", probs.astype(jnp.bfloat16), grad_mixed, preferred_element_type=jnp.float32
    )
    return (grad_q, grad_k, grad_v)


def body(
    tokens, cond, live_count, w_qkv, w_out, w_gu, w_down, w_ada, ada_bias, q_gain, k_gain, cotangent
):
    slots, tile_rows, tile_cols, width = tokens.shape
    per_slot = tile_rows * tile_cols
    row_total = slots * per_slot
    live_flags = (jnp.arange(slots) < live_count[0]).astype(jnp.float32)[:, None, None]
    full_qkv, full_out, full_gu, full_down, full_ada = (
        lax.all_gather(w_qkv, "img", axis=0, tiled=True),
        lax.all_gather(w_out, "img", axis=0, tiled=True),
        lax.all_gather(w_gu, "img", axis=0, tiled=True),
        lax.all_gather(w_down, "img", axis=0, tiled=True),
        lax.all_gather(w_ada, "img", axis=0, tiled=True),
    )
    cond_float = cond.astype(jnp.float32)
    silu_low = jax.nn.silu(cond_float).astype(jnp.bfloat16)
    modulation = jnp.dot(silu_low, full_ada, preferred_element_type=jnp.float32) + ada_bias
    shift_a, scale_a, gate_a, shift_b, scale_b, gate_b = [
        modulation[:, None, part_id * width : (part_id + 1) * width] for part_id in range(6)
    ]
    local_ids = jnp.arange(per_slot, dtype=jnp.int32)
    row_pos = (lax.axis_index("ty") * tile_rows + local_ids // tile_cols).astype(jnp.float32)
    col_pos = (lax.axis_index("tx") * tile_cols + local_ids % tile_cols).astype(jnp.float32)
    cosine, sine = rope_tables(row_pos, col_pos, HEAD // 4)
    x_tiles = tokens.reshape(slots, per_slot, width).astype(jnp.float32)
    inv_a = inverse_rms(x_tiles)
    normed_a = x_tiles * inv_a
    attn_in = (normed_a * (1.0 + scale_a) + shift_a).astype(jnp.bfloat16).reshape(row_total, width)
    qkv_proj = jnp.dot(attn_in, full_qkv, preferred_element_type=jnp.float32).reshape(
        slots, per_slot, 3, HEADS, HEAD
    )
    q_raw = qkv_proj[:, :, 0]
    k_raw = qkv_proj[:, :, 1]
    values_low = qkv_proj[:, :, 2].astype(jnp.bfloat16)
    inv_q = inverse_rms(q_raw)
    q_hat = q_raw * inv_q
    inv_k = inverse_rms(k_raw)
    k_hat = k_raw * inv_k
    queries = rotate(q_hat * q_gain, cosine, sine).astype(jnp.bfloat16)
    keys_low = rotate(k_hat * k_gain, cosine, sine).astype(jnp.bfloat16)
    keys_all, values_all = (
        lax.all_gather(keys_low.reshape(slots, per_slot, width), ("ty", "tx"), axis=1, tiled=True),
        lax.all_gather(
            values_low.reshape(slots, per_slot, width), ("ty", "tx"), axis=1, tiled=True
        ),
    )
    keys_all = keys_all.reshape(slots, -1, HEADS, HEAD)
    values_all = values_all.reshape(slots, -1, HEADS, HEAD)
    slot_id = 0
    result, log_total = attend_forward(queries[slot_id], keys_all[slot_id], values_all[slot_id])
    mixed_list = [result]
    lse_list = [log_total]
    mixed_low = jnp.stack(mixed_list).astype(jnp.bfloat16).reshape(row_total, width)
    attended = jnp.dot(mixed_low, full_out, preferred_element_type=jnp.float32).reshape(
        slots, per_slot, width
    )
    x_mid = x_tiles + gate_a * attended
    inv_b = inverse_rms(x_mid)
    normed_b = x_mid * inv_b
    mlp_in = (normed_b * (1.0 + scale_b) + shift_b).astype(jnp.bfloat16).reshape(row_total, width)
    gate_up = jnp.dot(mlp_in, full_gu, preferred_element_type=jnp.float32)
    gate_part = gate_up[:, :FF]
    up_part = gate_up[:, FF:]
    sigmoid_g = jax.nn.sigmoid(gate_part)
    silu_g = gate_part * sigmoid_g
    hidden_low = (silu_g * up_part).astype(jnp.bfloat16)
    branch = jnp.dot(hidden_low, full_down, preferred_element_type=jnp.float32).reshape(
        slots, per_slot, width
    )
    output = (live_flags * (x_mid + gate_b * branch)).astype(jnp.bfloat16).reshape(tokens.shape)
    grad_y = live_flags * cotangent.reshape(slots, per_slot, width).astype(jnp.float32)
    grad_gate_b = jnp.sum(grad_y * branch, axis=1)
    grad_branch_low = (gate_b * grad_y).astype(jnp.bfloat16).reshape(row_total, width)
    g_down = contract_rows(hidden_low, grad_branch_low)
    grad_hidden = contract_cols(grad_branch_low, full_down)
    grad_gate = grad_hidden * up_part * sigmoid_g * (1.0 + gate_part * (1.0 - sigmoid_g))
    grad_gu_low = jnp.concatenate([grad_gate, grad_hidden * silu_g], axis=-1).astype(jnp.bfloat16)
    g_gu = contract_rows(mlp_in, grad_gu_low)
    grad_mlp_in = contract_cols(grad_gu_low, full_gu).reshape(slots, per_slot, width)
    grad_scale_b = jnp.sum(grad_mlp_in * normed_b, axis=1)
    grad_shift_b = jnp.sum(grad_mlp_in, axis=1)
    grad_mid = grad_y + norm_back(grad_mlp_in * (1.0 + scale_b), normed_b, inv_b)
    grad_gate_a = jnp.sum(grad_mid * attended, axis=1)
    grad_att_low = (gate_a * grad_mid).astype(jnp.bfloat16).reshape(row_total, width)
    g_out = contract_rows(mixed_low, grad_att_low)
    grad_mixed_low = (
        contract_cols(grad_att_low, full_out)
        .astype(jnp.bfloat16)
        .reshape(slots, per_slot, HEADS, HEAD)
    )
    slot_id = 0
    grad_q, grad_k, grad_v = attend_backward(
        queries[slot_id],
        keys_all[slot_id],
        values_all[slot_id],
        lse_list[slot_id],
        grad_mixed_low[slot_id],
    )
    grad_q_list = [grad_q]
    grad_k_list = [grad_k.reshape(-1, width)]
    grad_v_list = [grad_v.reshape(-1, width)]
    own_keys, own_values = (
        lax.psum_scatter(
            jnp.stack(grad_k_list).astype(jnp.bfloat16),
            ("ty", "tx"),
            scatter_dimension=1,
            tiled=True,
        ).astype(jnp.float32),
        lax.psum_scatter(
            jnp.stack(grad_v_list).astype(jnp.bfloat16),
            ("ty", "tx"),
            scatter_dimension=1,
            tiled=True,
        ).astype(jnp.float32),
    )
    turned_q = unrotate(jnp.stack(grad_q_list), cosine, sine)
    turned_k = unrotate(own_keys.reshape(slots, per_slot, HEADS, HEAD), cosine, sine)
    gain_q_grad = jnp.sum(turned_q * q_hat, axis=(0, 1, 2))
    gain_k_grad = jnp.sum(turned_k * k_hat, axis=(0, 1, 2))
    grad_q_raw = norm_back(turned_q * q_gain, q_hat, inv_q)
    grad_k_raw = norm_back(turned_k * k_gain, k_hat, inv_k)
    grad_qkv_low = jnp.stack(
        [grad_q_raw, grad_k_raw, own_values.reshape(slots, per_slot, HEADS, HEAD)], axis=2
    )
    grad_qkv_low = grad_qkv_low.astype(jnp.bfloat16).reshape(row_total, 3 * width)
    g_qkv = contract_rows(attn_in, grad_qkv_low)
    grad_attn_in = contract_cols(grad_qkv_low, full_qkv).reshape(slots, per_slot, width)
    grad_scale_a = jnp.sum(grad_attn_in * normed_a, axis=1)
    grad_shift_a = jnp.sum(grad_attn_in, axis=1)
    grad_x = grad_mid + norm_back(grad_attn_in * (1.0 + scale_a), normed_a, inv_a)
    grad_tokens = grad_x.astype(jnp.bfloat16).reshape(tokens.shape)
    grad_mod = jnp.concatenate(
        [grad_shift_a, grad_scale_a, grad_gate_a, grad_shift_b, grad_scale_b, grad_gate_b], axis=-1
    )
    mod_tile = lax.psum(grad_mod, ("ty", "tx"))
    mod_low = mod_tile.astype(jnp.bfloat16)
    tile_count = lax.axis_size("ty") * lax.axis_size("tx")
    tile_index = lax.axis_index("ty") * lax.axis_size("tx") + lax.axis_index("tx")
    col_share = mod_low.shape[1] // tile_count
    mod_cols = lax.dynamic_slice_in_dim(mod_low, tile_index * col_share, col_share, 1)
    bias_term = jnp.where(tile_index == 0, jnp.sum(mod_low.astype(jnp.float32), axis=0), 0.0)
    gain_q_sum, gain_k_sum, bias_sum = lax.psum(
        (gain_q_grad, gain_k_grad, bias_term), ("img", "ty", "tx")
    )
    grad_silu = contract_cols(mod_low, full_ada)
    cols_qkv, cols_out, cols_gu, cols_down = (
        lax.psum_scatter(
            g_qkv.astype(jnp.bfloat16), ("ty", "tx"), scatter_dimension=1, tiled=True
        ).astype(jnp.float32),
        lax.psum_scatter(
            g_out.astype(jnp.bfloat16), ("ty", "tx"), scatter_dimension=1, tiled=True
        ).astype(jnp.float32),
        lax.psum_scatter(
            g_gu.astype(jnp.bfloat16), ("ty", "tx"), scatter_dimension=1, tiled=True
        ).astype(jnp.float32),
        lax.psum_scatter(
            g_down.astype(jnp.bfloat16), ("ty", "tx"), scatter_dimension=1, tiled=True
        ).astype(jnp.float32),
    )
    ada_cols = contract_rows(silu_low, mod_cols)
    sum_qkv, sum_out, sum_gu, sum_down, sum_ada = (
        lax.psum_scatter(cols_qkv, "img", scatter_dimension=0, tiled=True),
        lax.psum_scatter(cols_out, "img", scatter_dimension=0, tiled=True),
        lax.psum_scatter(cols_gu, "img", scatter_dimension=0, tiled=True),
        lax.psum_scatter(cols_down, "img", scatter_dimension=0, tiled=True),
        lax.psum_scatter(ada_cols, "img", scatter_dimension=0, tiled=True),
    )
    sigmoid_c = jax.nn.sigmoid(cond_float)
    grad_cond = (grad_silu * sigmoid_c * (1.0 + cond_float * (1.0 - sigmoid_c))).astype(
        jnp.bfloat16
    )
    return (
        output,
        grad_tokens,
        grad_cond,
        sum_qkv,
        sum_out,
        sum_gu,
        sum_down,
        sum_ada,
        gain_q_sum,
        gain_k_sum,
        bias_sum,
    )


def solution(mesh):
    in_specs = (
        P("img", "ty", "tx", None),
        P("img", None),
        P("img"),
        P("img", None),
        P("img", None),
        P("img", None),
        P("img", None),
        P("img", None),
        P(),
        P(),
        P(),
        P("img", "ty", "tx", None),
    )
    out_specs = (
        P("img", "ty", "tx", None),
        P("img", "ty", "tx", None),
        P("img", None),
        P("img", ("ty", "tx")),
        P("img", ("ty", "tx")),
        P("img", ("ty", "tx")),
        P("img", ("ty", "tx")),
        P("img", ("ty", "tx")),
        P(),
        P(),
        P(),
    )
    return jax.shard_map(body, mesh=mesh, in_specs=in_specs, out_specs=out_specs, check_vma=False)
```

profile of v0, /device:TPU:0, one launch (start us, length us, event | category | flops | bytes accessed | tf_op | source)
XLA Modules:
  0.0 1733.6 jit_solution(7799064384197622571)
XLA Ops:
  11.2 121.3 %all-gather.10.cloned.1.call-done = bf16[1152,3456]{1,0:T(8,128)(2,1)} async-done(((bf16[144,3456]{1,0:T(8,128)(2,1)}), bf16[1152,3456]{1,0:T(8,128)(2,1)}) %all-gather.10.cloned.1.call-update) | async-done | bytes 7962640 | tf_op jit(solution)/shard_map/all_gather | solution.py:114
  132.6 11.7 copy.45
  144.3 205.9 %all-gather.8.cloned.1.call-done = bf16[1152,6912]{1,0:T(8,128)(2,1)} async-done(((bf16[144,6912]{1,0:T(8,128)(2,1)}), bf16[1152,6912]{1,0:T(8,128)(2,1)}) %all-gather.8.cloned.1.call-update) | async-done | bytes 15925264 | tf_op jit(solution)/shard_map/all_gather | solution.py:118
  373.8 17.7 %all-gather.14.cloned.1.call-done = bf16[1,1024,1152]{1,2,0:T(8,128)(2,1)} async-done(((bf16[1,256,1152]{1,2,0:T(8,128)(2,1)}), bf16[1,1024,1152]{1,2,0:T(8,128)(2,1)}) %all-gather.14.cloned.1.call-update) | async-done | bytes 2359312 | tf_op jit(solution)/shard_map/all_gather | solution.py:147
  405.7 12.1 all-gather.12.cloned.1.call-done
  426.4 48.5 %all-gather.16.cloned.1.call-done = bf16[1152,1152]{1,0:T(8,128)(2,1)} async-done(((bf16[144,1152]{1,0:T(8,128)(2,1)}), bf16[1152,1152]{1,0:T(8,128)(2,1)}) %all-gather.16.cloned.1.call-update) | async-done | bytes 2654224 | tf_op jit(solution)/shard_map/all_gather | solution.py:115
  478.8 192.3 %all-gather.18.cloned.1.call-done = bf16[1152,6144]{1,0:T(8,128)(2,1)} async-done(((bf16[144,6144]{1,0:T(8,128)(2,1)}), bf16[1152,6144]{1,0:T(8,128)(2,1)}) %all-gather.18.cloned.1.call-update) | async-done | bytes 14155792 | tf_op jit(solution)/shard_map/all_gather | solution.py:116
  671.2 11.3 fusion.53
  682.5 97.8 %all-gather.20.cloned.1.call-done = bf16[3072,1152]{1,0:T(8,128)(2,1)} async-done(((bf16[384,1152]{1,0:T(8,128)(2,1)}), bf16[3072,1152]{1,0:T(8,128)(2,1)}) %all-gather.20.cloned.1.call-update) | async-done | bytes 7077904 | tf_op jit(solution)/shard_map/all_gather | solution.py:117
  791.1 12.0 multiply_reduce_fusion.4
  812.9 12.8 multiply_reduce_fusion
  825.7 11.9 multiply_convert_fusion
  875.1 47.9 %reshape_bitcast_fusion = bf16[1,256,1152]{0,2,1:T(8,128)(2,1)} fusion(bf16[256,1152]{1,0:T(8,128)(2,1)} %reduce-scatter.34.cloned.1.call-done), kind=kLoop, calls=%fused_computation | loop fusion | bytes 1179648
  922.9 67.7 %copy.64 = bf16[1,256,1152]{1,0,2:T(2,128)(2,1)S(1)} copy(bf16[1,256,1152]{0,2,1:T(8,128)(2,1)} %reshape_bitcast_fusion) | data formatting | bytes 1179648
  1006.2 11.3 convolution_convert_fusion
  1028.4 12.8 psum.28
  1049.1 37.2 %reduce-scatter.20.cloned.1.call-done = bf16[1152,864]{0,1:T(8,128)(2,1)} async-done(((bf16[1152,3456]{0,1:T(8,128)(2,1)}), bf16[1152,864]{0,1:T(8,128)(2,1)}) %reduce-scatter.20.cloned.1.call-update) | async-done | bytes 1990672 | tf_op jit(solution)/shard_map/reduce_scatter | solution.py:252
  1090.8 107.8 %reduce-scatter.24.cloned.1.call-done = bf16[1152,1536]{1,0:T(8,128)(2,1)} async-done(((bf16[1152,6144]{1,0:T(8,128)(2,1)}), bf16[1152,1536]{1,0:T(8,128)(2,1)}) %reduce-scatter.24.cloned.1.call-update) | async-done | bytes 3538960 | tf_op jit(solution)/shard_map/reduce_scatter | solution.py:258
  1204.5 41.0 %all-reduce = (f32[72]{0:T(128)}, f32[72]{0:T(128)}, f32[6912]{0:T(1024)}) all-reduce(f32[72]{0:T(128)S(1)} %get-tuple-element.49, f32[72]{0:T(128)S(1)} %get-tuple-element.44, f32[6912]{0:T(1024)S(1)} %fusion.36), channel_id=1, replica_groups=mesh['img'=8,'ty'=2,'tx'=2] {'img','ty','tx'}, use_global_device_ids=true, to_apply=%region_30.31 | all-reduce | flops 7056 | bytes 56448 | tf_op jit(solution)/shard_map/psum | solution.py:247
  1257.1 11.7 reduce-scatter.38.cloned.1.call-done
  1268.8 150.3 %reduce-scatter.32.cloned.1.call-done = f32[144,1728]{1,0:T(8,128)} async-done(((f32[1152,1728]{1,0:T(8,128)}), f32[144,1728]{1,0:T(8,128)}) %reduce-scatter.32.cloned.1.call-update) | async-done | bytes 995344 | tf_op jit(solution)/shard_map/reduce_scatter | solution.py:271
  1419.1 82.6 %reduce-scatter.30.cloned.1.call-done = f32[384,288]{0,1:T(8,128)} async-done(((f32[3072,288]{0,1:T(8,128)}), f32[384,288]{0,1:T(8,128)}) %reduce-scatter.30.cloned.1.call-update) | async-done | bytes 442384 | tf_op jit(solution)/shard_map/reduce_scatter | solution.py:270
  1501.7 91.7 %reduce-scatter.36.cloned.1.call-done = f32[144,864]{1,0:T(8,128)} async-done(((f32[1152,864]{1,0:T(8,128)}), f32[144,864]{1,0:T(8,128)}) %reduce-scatter.36.cloned.1.call-update) | async-done | bytes 497680
  1593.4 132.9 %reduce-scatter.26.cloned.1.call-done = f32[144,1536]{1,0:T(8,128)} async-done(((f32[1152,1536]{1,0:T(8,128)}), f32[144,1536]{1,0:T(8,128)}) %reduce-scatter.26.cloned.1.call-update) | async-done | bytes 884752 | tf_op jit(solution)/shard_map/reduce_scatter | solution.py:269
  (246 shorter events, 167.1 us)
Async XLA Ops:
  7.2 125.3 %all-gather.10.cloned.1.call-start = ((), (), s32[]{:S(2)}) async-start(), calls=%async_computation.12 | async-start | bytes 8957952 | tf_op jit(solution)/shard_map/all_gather | solution.py:114
  7.9 342.2 %all-gather.8.cloned.1.call-start = ((), (), s32[]{:S(2)}) async-start(), calls=%async_computation.11 | async-start | bytes 17915904 | tf_op jit(solution)/shard_map/all_gather | solution.py:118
  8.7 382.8 %all-gather.14.cloned.1.call-start = ((), (), s32[]{:S(2)}) async-start(), calls=%async_computation.14 | async-start | bytes 2949120 | tf_op jit(solution)/shard_map/all_gather | solution.py:147
  11.2 347.5 %copy-start.45 = (f32[16,16]{1,0:T(8,128)}, f32[16,16]{1,0:T(8,128)S(1)}, u32[]{:S(2)}) copy-start(f32[16,16]{1,0:T(8,128)S(1)} %add_rsqrt_fusion.2) | copy-start | bytes 3076
  132.6 217.6 %copy-start.49 = (bf16[1,1152]{1,0:T(2,128)(2,1)S(1)}, bf16[1,1152]{1,0:T(2,128)(2,1)}, u32[]{:S(2)}) copy-start(bf16[1,1152]{1,0:T(2,128)(2,1)} %param.13) | copy-start | bytes 6916
  144.3 213.7 %copy-start.52 = (f32[6912]{0:T(1024)S(1)}, f32[6912]{0:T(1024)}, u32[]{:S(2)}) copy-start(f32[6912]{0:T(1024)} %param.20) | copy-start | bytes 82948
  368.8 49.1 %all-gather.12.cloned.1.call-start = ((), (), s32[]{:S(2)}) async-start(), calls=%async_computation.13 | async-start | bytes 2949120 | tf_op jit(solution)/shard_map/all_gather | solution.py:148
  369.7 105.2 %all-gather.16.cloned.1.call-start = ((), (), s32[]{:S(2)}) async-start(), calls=%async_computation.15 | async-start | bytes 2985984 | tf_op jit(solution)/shard_map/all_gather | solution.py:115
  370.3 300.9 %all-gather.18.cloned.1.call-start = ((), (), s32[]{:S(2)}) async-start(), calls=%async_computation.16 | async-start | bytes 15925248 | tf_op jit(solution)/shard_map/all_gather | solution.py:116
  370.9 409.5 %all-gather.20.cloned.1.call-start = ((), (), s32[]{:S(2)}) async-start(), calls=%async_computation.17 | async-start | bytes 7962624 | tf_op jit(solution)/shard_map/all_gather | solution.py:117
  371.7 503.4 %reduce-scatter.34.cloned.1.call-start = ((), (), s32[]{:S(2)}) async-start(), calls=%async_computation.26 | async-start | bytes 2949120
  373.8 406.6 %copy-start.19 = (bf16[256,1152]{1,0:T(8,128)(2,1)}, bf16[256,1152]{1,0:T(8,128)(2,1)S(1)}, u32[]{:S(2)}) copy-start(bf16[256,1152]{1,0:T(8,128)(2,1)S(1)} %fusion.16) | copy-start | bytes 1769476
  478.8 324.4 %copy-start.8 = (f32[256,1152]{1,0:T(8,128)}, f32[256,1152]{1,0:T(8,128)S(1)}, u32[]{:S(2)}) copy-start(f32[256,1152]{1,0:T(8,128)S(1)} %get-tuple-element.70) | copy-start | bytes 3538948
  478.8 312.3 %copy-start.53 = (f32[256]{0:T(256)}, f32[256]{0:T(256)S(1)}, u32[]{:S(2)}) copy-start(f32[256]{0:T(256)S(1)} %add_rsqrt_fusion.3) | copy-start | bytes 3076
  843.7 154.8 %reduce-scatter.18.cloned.1.call-start = ((), (), s32[]{:S(2)}) async-start(), calls=%async_computation.18 | async-start | bytes 2949120 | tf_op jit(solution)/shard_map/reduce_scatter | solution.py:214
  855.2 170.1 %reduce-scatter.22.cloned.1.call-start = ((), (), s32[]{:S(2)}) async-start(), calls=%async_computation.20 | async-start | bytes 3317760 | tf_op jit(solution)/shard_map/reduce_scatter | solution.py:255
  859.0 186.3 %reduce-scatter.28.cloned.1.call-start = ((), (), s32[]{:S(2)}) async-start(), calls=%async_computation.23 | async-start | bytes 8847360 | tf_op jit(solution)/shard_map/reduce_scatter | solution.py:261
  865.5 220.8 %reduce-scatter.20.cloned.1.call-start = ((), (), s32[]{:S(2)}) async-start(), calls=%async_computation.19 | async-start | bytes 9953280 | tf_op jit(solution)/shard_map/reduce_scatter | solution.py:252
  1005.5 193.0 %reduce-scatter.24.cloned.1.call-start = ((), (), s32[]{:S(2)}) async-start(), calls=%async_computation.21 | async-start | bytes 17694720 | tf_op jit(solution)/shard_map/reduce_scatter | solution.py:258
  1017.5 251.2 %reduce-scatter.38.cloned.1.call-start = ((), (), s32[]{:S(2)}) async-start(), calls=%async_computation.28 | async-start | bytes 1990656
  1028.3 390.8 %reduce-scatter.32.cloned.1.call-start = ((), (), s32[]{:S(2)}) async-start(), calls=%async_computation.25 | async-start | bytes 9289728 | tf_op jit(solution)/shard_map/reduce_scatter | solution.py:271
  1045.3 456.4 %reduce-scatter.30.cloned.1.call-start = ((), (), s32[]{:S(2)}) async-start(), calls=%async_computation.24 | async-start | bytes 3981312 | tf_op jit(solution)/shard_map/reduce_scatter | solution.py:270
  1049.1 544.3 %reduce-scatter.36.cloned.1.call-start = ((), (), s32[]{:S(2)}) async-start(), calls=%async_computation.27 | async-start | bytes 4644864
  1090.7 635.5 %reduce-scatter.26.cloned.1.call-start = ((), (), s32[]{:S(2)}) async-start(), calls=%async_computation.22 | async-start | bytes 7962624 | tf_op jit(solution)/shard_map/reduce_scatter | solution.py:269
  (59 other events, 602.8 us)
Sparse Core Ops, SparseCore 0:
  10.2 122.2 all-gather.9
  134.7 215.3 all-gather.7
  368.9 22.5 all-gather.13
  393.4 24.3 all-gather.11
  419.8 55.0 all-gather.15
  477.0 194.1 all-gather.17
  673.4 106.9 all-gather.19
  843.8 31.2 reduce-scatter.33
  877.8 33.0 reduce-scatter.17
  913.3 34.8 reduce-scatter.21
  950.9 63.7 reduce-scatter.27
  1017.1 69.1 reduce-scatter.19
  1088.9 109.5 reduce-scatter.23
  1202.4 66.3 reduce-scatter.37
  1273.3 145.6 reduce-scatter.31
  1423.6 78.0 reduce-scatter.29
  1506.1 87.2 reduce-scatter.35
  1597.5 128.7 reduce-scatter.25
where the time goes:
time: 1740 us; the launch traced here: 1730 us
  waiting for transfers between devices  1310 us (75%)
  local copies, waits for them, and re-layouts  163 us (9%)
  matrix products  144 us (8%)
  blocking collectives  53.9 us (3%)
  other arithmetic  40.7 us (2%)
    all_gather x1, waiting for transfers between devices, body(): lax.all_gather(w_ada, 'img', axis=0, tiled=True)  206 us
    all_gather x1, waiting for transfers between devices, body(): lax.all_gather(w_gu, 'img', axis=0, tiled=True)  192 us
    reduce_scatter x1, waiting for transfers between devices, body(): lax.psum_scatter(ada_cols, 'img', scatter_dimension=0, tiled=True)  150 us
    unnamed x140, local copies, waits for them, and re-layouts  144 us
    reduce_scatter x1, waiting for transfers between devices, body(): lax.psum_scatter(cols_gu, 'img', scatter_dimension=0, tiled=True)  133 us
    all_gather x1, waiting for transfers between devices, body(): lax.all_gather(w_qkv, 'img', axis=0, tiled=True)  121 us
    unnamed x21, waiting for transfers between devices  108 us
    reduce_scatter x1, waiting for transfers between devices, body(): lax.psum_scatter(g_gu.astype(jnp.bfloat16), ('ty', 'tx'), scatter_dimensi...  108 us
  transfers between devices with their start and end apart: 18, of which 15 were waited for; matrix products, arithmetic and copies ran while one was open for 14% of the time, Pallas kernels for 0%

commit v1 on v0

v1 whole, which is shorter than its diff:
```python
import functools
import math

import jax
import jax.numpy as jnp
import numpy as np
from jax import lax
from jax.experimental import pallas as pl
from jax.experimental.pallas import tpu as pltpu
from jax.sharding import PartitionSpec as P

HEADS = 16
HEAD = 72
FF = 3072
TILES = 4
OWN = HEADS // TILES
LANES = 128
COLS = OWN * HEAD
PADDED = OWN * LANES
WINDOW = 384
QUARTER = HEAD // 4
EPSILON = 1e-06
LOG2E = math.log2(math.e)
LN2 = math.log(2.0)
BF16 = jnp.bfloat16
F32 = jnp.float32


def head_lane(index):
    part, half, freq = index // 36, (index % 36) // QUARTER, index % QUARTER
    return half * 64 + part * QUARTER + freq


def spread_matrices():
    spread = np.zeros((4, WINDOW, PADDED), np.float32)
    for which in range(4):
        base = (COLS - 256) * which if which < 3 else 0
        for head in range(OWN):
            for index in range(HEAD):
                lane = index if which >= 2 else head_lane(index)
                spread[which, base + HEAD * head + index, LANES * head + lane] = 1.0
    return spread


def dot(left, right):
    return jnp.dot(left, right, preferred_element_type=F32)


def dot_nt(left, right):
    return lax.dot_general(left, right, (((1,), (1,)), ((), ())), preferred_element_type=F32)


def dot_tn(left, right):
    return lax.dot_general(left, right, (((0,), (0,)), ((), ())), preferred_element_type=F32)


def inverse_rms(values):
    return lax.rsqrt(jnp.mean(values * values, axis=-1, keepdims=True) + EPSILON)


def norm_back(grad_out, normed, inv_scale):
    return inv_scale * (grad_out - normed * jnp.mean(grad_out * normed, axis=-1, keepdims=True))


def swap(values, axis):
    return lax.ppermute(values, axis, [(0, 1), (1, 0)])


def gather_rows(values):
    pair = jnp.concatenate([values, swap(values, "ty")])
    return jnp.concatenate([pair, swap(pair, "tx")])


def scatter_rows(partial):
    half = partial.shape[0] // 2
    low = partial.astype(BF16)
    pair = partial[:half].astype(F32) + swap(low[half:], "tx").astype(F32)
    cut = half // 2
    return pair[:cut] + swap(pair[cut:].astype(BF16), "ty").astype(F32)


def sum_tiles(values):
    values = values + swap(values, "tx")
    return values + swap(values, "ty")


def absolute(pieces):
    ty, tx = lax.axis_index("ty"), lax.axis_index("tx")
    turned = [jnp.where(tx == 1, pieces[j ^ 2], pieces[j]) for j in range(4)]
    turned = [jnp.where(ty == 1, turned[j ^ 1], turned[j]) for j in range(4)]
    return [turned[((a & 1) << 1) | (a >> 1)] for a in range(4)]


def tile_at(j):
    return (lax.axis_index("ty") ^ (j & 1)) * 2 + (lax.axis_index("tx") ^ (j >> 1))


def exchange_tiles(piece_for):
    got = [piece_for(tile_at(0))]
    got.append(swap(piece_for(tile_at(1)), "ty"))
    got.append(swap(piece_for(tile_at(2)), "tx"))
    across = [(a * 2 + b, (1 - a) * 2 + 1 - b) for a in range(2) for b in range(2)]
    got.append(lax.ppermute(piece_for(tile_at(3)), ("ty", "tx"), across))
    return absolute(got)


def flip_perm(count, bit):
    return [(i, i ^ bit) for i in range(count)]


def flip_gather(values, count):
    bit = 1
    while bit < count:
        values = jnp.concatenate([values, lax.ppermute(values, "img", flip_perm(count, bit))])
        bit *= 2
    return values


def flip_scatter(values, count):
    bit = count // 2
    while bit >= 1:
        values = values[:bit] + lax.ppermute(values[bit:], "img", flip_perm(count, bit))
        bit //= 2
    return values


def tree_sum(values):
    while values.shape[0] > 1:
        values = values[0::2] + values[1::2]
    return values


def ring_order(count):
    return list(range(0, count, 2)) + list(range(count - 1, 0, -2))


def ring_perm(count, step):
    order = ring_order(count)
    return [(order[i], order[(i + step) % count]) for i in range(count)]


def ring_place(count):
    order = ring_order(count)
    places = np.argsort(np.array(order)).astype(np.int32)
    return jnp.asarray(places)[lax.axis_index("img")], jnp.asarray(np.array(order, np.int32))


def use_ring(count, rows):
    return 2 < count <= 16 and count % 2 == 0 and rows % 16 == 0


def split_rows(rows):
    return (rows // 2 + 15) // 16 * 16


def assemble_kernel(count, rows, cut, index_ref, *refs):
    own, pieces_a, pieces_b = refs[0], refs[1:count], refs[count : 2 * count - 1]
    out_ref, sems = refs[-2], refs[-1]
    copies = [(own, 0, rows)]
    copies += [(piece, 0, cut) for piece in pieces_a]
    copies += [(piece, cut, rows - cut) for piece in pieces_b]
    started = []
    for k, (src, offset, size) in enumerate(copies):
        start = pl.multiple_of(index_ref[k] * rows + offset, 16)
        copy = pltpu.make_async_copy(src, out_ref.at[pl.ds(start, size)], sems.at[k])
        copy.start()
        started.append(copy)
    for copy in started:
        copy.wait()


def gather_weight(own, count):
    rows = own.shape[0]
    if not use_ring(count, rows):
        return lax.all_gather(own, "img", axis=0, tiled=True)
    cut = split_rows(rows)
    a, b = own[:cut], own[cut:]
    pieces_a, pieces_b = [], []
    for _ in range(count - 1):
        a = lax.ppermute(a, "img", ring_perm(count, 1))
        b = lax.ppermute(b, "img", ring_perm(count, -1))
        pieces_a.append(a)
        pieces_b.append(b)
    place, order = ring_place(count)
    steps = jnp.arange(1, count, dtype=jnp.int32)
    index = jnp.concatenate(
        [
            lax.axis_index("img")[None],
            order[(place - steps) % count],
            order[(place + steps) % count],
        ]
    ).astype(jnp.int32)
    copies = 2 * count - 1
    return pl.pallas_call(
        functools.partial(assemble_kernel, count, rows, cut),
        out_shape=jax.ShapeDtypeStruct((count * rows, own.shape[1]), own.dtype),
        in_specs=[pl.BlockSpec(memory_space=pltpu.SMEM)]
        + [pl.BlockSpec(memory_space=pl.ANY)] * copies,
        out_specs=vmem(),
        scratch_shapes=[pltpu.SemaphoreType.DMA((copies,))],
        name="assemble",
    )(index, own, *pieces_a, *pieces_b)


def scatter_weight(grad, count, kind):
    rows = grad.shape[0] // count
    if kind == "call" or not use_ring(count, rows):
        return lax.psum_scatter(grad, "img", scatter_dimension=0, tiled=True).astype(F32)
    cut = split_rows(rows)
    place, order = ring_place(count)
    outs = []
    for sign, offset, size in ((1, 0, cut), (-1, cut, rows - cut)):

        def part(step, offset=offset, size=size, sign=sign):
            owner = order[(place - sign * step) % count]
            return lax.dynamic_slice_in_dim(grad, owner * rows + offset, size, 0)

        total = part(1)
        for step in range(2, count + 1):
            total = lax.ppermute(total, "img", ring_perm(count, sign))
            total = total.astype(F32) + part(step).astype(F32)
            if step < count:
                total = total.astype(BF16)
        outs.append(total)
    return jnp.concatenate(outs)


def vmem():
    return pl.BlockSpec(memory_space=pltpu.VMEM)


def lane_ids(rows):
    return lax.broadcasted_iota(jnp.int32, (rows, LANES), 1)


def three_parts(column):
    high = column.astype(BF16)
    rest = column - high.astype(F32)
    mid = rest.astype(BF16)
    return high, mid, (rest - mid.astype(F32)).astype(BF16)


def put_lanes(values, first, parts):
    lanes = lane_ids(values.shape[0])
    for k, part in enumerate(parts):
        values = jnp.where(lanes == first + k, part.astype(values.dtype), values)
    return values


QK_SPARE = 100
V_SPARE = HEAD


def attention_kernel(
    x_ref, shift_ref, scale_ref, w_ref, cos_ref, sin_ref, gq_ref, gk_ref, spread_ref,
    attn_ref, qraw_ref, kraw_ref, q_ref, k_ref, v_ref, mixedp_ref, mixed_ref, wpad_ref,
):
    tokens = x_ref.shape[0]
    block = 256
    factor = LOG2E / math.sqrt(HEAD)

    @pl.loop(0, w_ref.shape[0] // 128)
    def _(i):
        rows = pl.ds(pl.multiple_of(i * 128, 128), 128)
        for w in range(3):
            wpad_ref[rows, PADDED * w : PADDED * (w + 1)] = dot(
                w_ref[rows, 256 * w : 256 * w + WINDOW], spread_ref[w]
            ).astype(BF16)

    @pl.loop(0, tokens // block)
    def _(i):
        rows = pl.ds(pl.multiple_of(i * block, block), block)
        x = x_ref[rows, :].astype(F32)
        normed = x * inverse_rms(x)
        attn_in = (normed * (1.0 + scale_ref[...]) + shift_ref[...]).astype(BF16)
        attn_ref[rows, :] = attn_in
        cos, sin = cos_ref[rows, :], sin_ref[rows, :]
        lanes = lane_ids(block)
        spare = (lanes >= QK_SPARE) & (lanes < QK_SPARE + 3)
        for which, raw_ref, out_ref, gain_ref in (
            (0, qraw_ref, q_ref, gq_ref),
            (1, kraw_ref, k_ref, gk_ref),
        ):
            raw = dot(attn_in, wpad_ref[:, PADDED * which : PADDED * (which + 1)])
            raw_ref[rows, :] = raw
            for head in range(OWN):
                at = slice(LANES * head, LANES * (head + 1))
                part = raw[:, at]
                inv = lax.rsqrt(jnp.sum(part * part, axis=-1, keepdims=True) / HEAD + EPSILON)
                scaled = part * inv * gain_ref[...]
                turned = scaled * cos + pltpu.roll(scaled, 64, 1) * sin
                if which == 0:
                    out_ref[rows, at] = (turned * factor).astype(BF16)
                else:
                    out_ref[rows, at] = jnp.where(spare, 1.0, turned).astype(BF16)
        value = dot(attn_in, wpad_ref[:, PADDED * 2 : PADDED * 3])
        ones = (lanes >= V_SPARE) & (lanes < V_SPARE + 3)
        for head in range(OWN):
            at = slice(LANES * head, LANES * (head + 1))
            v_ref[rows, at] = jnp.where(ones, 1.0, value[:, at]).astype(BF16)

    @pl.loop(0, tokens // block)
    def _(i):
        rows = pl.ds(pl.multiple_of(i * block, block), block)
        for head in range(OWN):
            at = slice(LANES * head, LANES * (head + 1))
            query = q_ref[rows, at]
            logits = dot_nt(query, k_ref[:, at])
            terms = jnp.exp2(logits).astype(BF16)
            result = dot(terms, v_ref[:, at])
            total = result[:, V_SPARE : V_SPARE + 1]
            mixedp_ref[rows, at] = (result * (1.0 / total)).astype(BF16)
            q_ref[rows, at] = put_lanes(query, QK_SPARE, three_parts(-jnp.log2(total)))
        mixed_ref[rows, :] = dot_nt(mixedp_ref[rows, :], spread_ref[3]).astype(BF16)[:, :COLS]


def attention_forward(x, shift, scale, w, cos, sin, gq, gk, spread):
    tokens, width = x.shape
    return pl.pallas_call(
        attention_kernel,
        out_shape=[
            jax.ShapeDtypeStruct((tokens, width), BF16),
            jax.ShapeDtypeStruct((tokens, PADDED), F32),
            jax.ShapeDtypeStruct((tokens, PADDED), F32),
            jax.ShapeDtypeStruct((tokens, PADDED), BF16),
            jax.ShapeDtypeStruct((tokens, PADDED), BF16),
            jax.ShapeDtypeStruct((tokens, PADDED), BF16),
            jax.ShapeDtypeStruct((tokens, PADDED), BF16),
            jax.ShapeDtypeStruct((tokens, COLS), BF16),
        ],
        in_specs=[vmem()] * 9,
        out_specs=[vmem()] * 8,
        scratch_shapes=[pltpu.VMEM((width, 3 * PADDED), BF16)],
        compiler_params=pltpu.CompilerParams(vmem_limit_bytes=56 * 1024 * 1024),
        name="attention_forward",
    )(x, shift, scale, w, cos, sin, gq, gk, spread)


def attention_back_kernel(
    grad_ref, qraw_ref, kraw_ref, q_ref, k_ref, v_ref, mixedp_ref, cos_ref, sin_ref, gq_ref, gk_ref,
    spread_ref, out_ref, gains_ref, do_ref, dq_ref, dk_ref, pad_ref,
):
    tokens = grad_ref.shape[0]
    block = 256
    root = 1.0 / math.sqrt(HEAD)

    @pl.loop(0, tokens // block)
    def _(i):
        rows = pl.ds(pl.multiple_of(i * block, block), block)
        wide = dot(grad_ref[rows, :], spread_ref[3, :COLS, :])
        for head in range(OWN):
            at = slice(LANES * head, LANES * (head + 1))
            part = wide[:, at]
            row_dot = jnp.sum(part * mixedp_ref[rows, at].astype(F32), axis=-1, keepdims=True)
            do_ref[rows, at] = put_lanes(part.astype(BF16), V_SPARE, three_parts(-row_dot))

    for head in range(OWN):
        at = slice(LANES * head, LANES * (head + 1))
        dq_ref[at, :] = jnp.zeros((LANES, tokens), F32)

        @pl.loop(0, tokens // block)
        def _(i):
            rows = pl.ds(pl.multiple_of(i * block, block), block)
            query, grad = q_ref[:, at], do_ref[:, at]
            key = k_ref[rows, at]
            probs = jnp.exp2(dot_nt(key, query))
            slope = (probs * dot_nt(v_ref[rows, at], grad)).astype(BF16)
            pad_ref[rows, 2 * PADDED + LANES * head : 2 * PADDED + LANES * (head + 1)] = dot(
                probs.astype(BF16), grad
            ).astype(BF16)
            dk_ref[rows, at] = dot(slope, query) * LN2
            dq_ref[at, :] += dot(key.astype(F32).T.astype(BF16), slope)

    gains_ref[...] = jnp.zeros_like(gains_ref)

    @pl.loop(0, tokens // block)
    def _(i):
        rows = pl.ds(pl.multiple_of(i * block, block), block)
        cos, sin = cos_ref[rows, :], sin_ref[rows, :]
        for which, raw_ref, gain_ref in ((0, qraw_ref, gq_ref), (1, kraw_ref, gk_ref)):
            gained = jnp.zeros((1, LANES), F32)
            for head in range(OWN):
                at = slice(LANES * head, LANES * (head + 1))
                raw = raw_ref[rows, at]
                inv = lax.rsqrt(jnp.sum(raw * raw, axis=-1, keepdims=True) / HEAD + EPSILON)
                hat = raw * inv
                if which == 0:
                    grad = dq_ref[at, rows].T * root
                else:
                    grad = dk_ref[rows, at]
                turned = grad * cos - pltpu.roll(grad, 64, 1) * sin
                product = turned * hat
                gained += jnp.sum(product, axis=0, keepdims=True)
                mean = jnp.sum(product * gain_ref[...], axis=-1, keepdims=True) / HEAD
                pad_ref[rows, PADDED * which + LANES * head : PADDED * which + LANES * (head + 1)] = (
                    inv * (turned * gain_ref[...] - hat * mean)
                ).astype(BF16)
            gains_ref[which : which + 1, :] += gained
        compact = [
            dot_nt(pad_ref[rows, PADDED * w : PADDED * (w + 1)], spread_ref[w]).astype(BF16)
            for w in range(3)
        ]
        out_ref[rows, :] = jnp.concatenate(
            [
                compact[0][:, :256],
                compact[0][:, 256:] + compact[1][:, :128],
                compact[1][:, 128:256],
                compact[1][:, 256:] + compact[2][:, :128],
                compact[2][:, 128:],
            ],
            axis=1,
        )[:, : 3 * COLS]


def attention_backward(grad, qraw, kraw, q, k, v, mixedp, cos, sin, gq, gk, spread):
    tokens = grad.shape[0]
    return pl.pallas_call(
        attention_back_kernel,
        out_shape=[
            jax.ShapeDtypeStruct((tokens, 3 * COLS), BF16),
            jax.ShapeDtypeStruct((8, LANES), F32),
        ],
        in_specs=[vmem()] * 12,
        out_specs=[vmem()] * 2,
        scratch_shapes=[
            pltpu.VMEM((tokens, PADDED), BF16),
            pltpu.VMEM((PADDED, tokens), F32),
            pltpu.VMEM((tokens, PADDED), F32),
            pltpu.VMEM((tokens, 3 * PADDED), BF16),
        ],
        compiler_params=pltpu.CompilerParams(vmem_limit_bytes=56 * 1024 * 1024),
        name="attention_backward",
    )(grad, qraw, kraw, q, k, v, mixedp, cos, sin, gq, gk, spread)


def rope_lanes(tile_rows, tile_cols):
    freq = np.zeros((LANES,), np.float32)
    part = np.zeros((LANES,), np.int32)
    sign = np.zeros((LANES,), np.float32)
    for index in range(HEAD):
        lane = head_lane(index)
        part[lane] = index // 36
        sign[lane] = 1.0 if lane >= 64 else -1.0
    freqs = 10000.0 ** (-jnp.arange(QUARTER, dtype=F32) / QUARTER)
    half = jnp.concatenate([freqs, freqs, jnp.zeros((64 - 2 * QUARTER,), F32)])
    freq = jnp.concatenate([half, half])
    ids = np.arange(tile_rows * tile_cols)
    rows, cols = [], []
    for j in range(4):
        ty, tx = lax.axis_index("ty") ^ (j & 1), lax.axis_index("tx") ^ (j >> 1)
        rows.append(ty * tile_rows + jnp.asarray(ids // tile_cols, jnp.int32))
        cols.append(tx * tile_cols + jnp.asarray(ids % tile_cols, jnp.int32))
    rows = jnp.concatenate(rows).astype(F32)[:, None]
    cols = jnp.concatenate(cols).astype(F32)[:, None]
    angle = jnp.where(jnp.asarray(part)[None] == 0, rows, cols) * freq[None]
    live = jnp.asarray((sign != 0).astype(np.float32))[None]
    return jnp.cos(angle) * live, jnp.sin(angle) * jnp.asarray(sign)[None]


def gain_lanes(gain):
    parts = gain.reshape(2, 2, QUARTER).transpose(1, 0, 2).reshape(2, 2 * QUARTER)
    return jnp.pad(parts, ((0, 0), (0, 64 - 2 * QUARTER))).reshape(1, LANES)


def gain_back(lanes):
    parts = lanes.reshape(2, 64)[:, : 2 * QUARTER].reshape(2, 2, QUARTER)
    return parts.transpose(1, 0, 2).reshape(HEAD)


def body(
    count, tokens, cond, live_count, w_qkv, w_out, w_gu, w_down, w_ada, ada_bias, q_gain, k_gain, cotangent
):
    _, tile_rows, tile_cols, width = tokens.shape
    per_tile = tile_rows * tile_cols
    img, ty, tx = lax.axis_index("img"), lax.axis_index("ty"), lax.axis_index("tx")
    tile = ty * 2 + tx
    live = (live_count[0] > 0).astype(F32)
    shard = width // count
    ff_shard = FF // count
    ff_own = ff_shard // TILES
    hidden_own = FF // TILES
    spread = jnp.asarray(spread_matrices(), BF16)

    first = jnp.concatenate(
        [lax.dynamic_slice_in_dim(w_qkv, p * width + tile * COLS, COLS, 1) for p in range(3)]
        + [lax.dynamic_slice_in_dim(w_out, tile * (width // TILES), width // TILES, 1)],
        axis=1,
    )
    full_first = gather_weight(first, count)
    gu_own = lax.dynamic_slice_in_dim(w_gu.reshape(shard, 2 * count, ff_shard), tile * ff_own, ff_own, 2)
    full_gu = gather_weight(gu_own.reshape(shard, 2 * hidden_own), count)
    full_down = gather_weight(lax.dynamic_slice_in_dim(w_down, tile * ff_own, ff_own, 0), count)

    x_all = gather_rows(tokens.reshape(per_tile, width))
    dy_all = gather_rows(cotangent.reshape(per_tile, width))

    cond_float = cond.astype(F32)
    silu_all = flip_gather(jax.nn.silu(cond_float).astype(BF16), count)
    silu_rows = lax.dynamic_slice_in_dim(silu_all, img * shard, shard, 1)
    modulation = flip_scatter(dot(silu_rows, w_ada), count) + ada_bias
    shift_a, scale_a, gate_a, shift_b, scale_b, gate_b = [
        modulation[:, k * width : (k + 1) * width] for k in range(6)
    ]

    cos, sin = rope_lanes(tile_rows, tile_cols)
    gq, gk = gain_lanes(q_gain), gain_lanes(k_gain)
    attn_in, qraw, kraw, queries, keys, values, mixedp, mixed = attention_forward(
        x_all, shift_a, scale_a, full_first, cos, sin, gq, gk, spread
    )

    def turn(v, flip):
        blocks = [v[per_tile * b : per_tile * (b + 1)] for b in range(4)]
        return jnp.concatenate([blocks[b ^ flip] for b in range(4)])

    mixed_pair = jnp.concatenate([mixed, turn(swap(mixed, "ty"), 1)], axis=1)
    mixed_all = jnp.concatenate([mixed_pair, turn(swap(mixed_pair, "tx"), 2)], axis=1)

    out_cols = full_first[:, 3 * COLS :]
    out_pair = swap(out_cols, "ty")
    pieces = [out_cols, out_pair, swap(out_cols, "tx"), swap(out_pair, "tx")]
    out_abs = jnp.concatenate(absolute(pieces), axis=1)
    full_out = jnp.concatenate(
        [lax.dynamic_slice_in_dim(out_abs, tile_at(j) * COLS, COLS, 0) for j in range(4)]
    )

    x_float = x_all.astype(F32)
    attended = dot(mixed_all, full_out)
    x_mid = x_float + gate_a * attended
    inv_b = inverse_rms(x_mid)
    normed_b = x_mid * inv_b
    mlp_in = (normed_b * (1.0 + scale_b) + shift_b).astype(BF16)
    gate_up = dot(mlp_in, full_gu)
    gate, up = gate_up[:, :hidden_own], gate_up[:, hidden_own:]
    sigmoid = jax.nn.sigmoid(gate)
    silu_g = gate * sigmoid
    hidden = (silu_g * up).astype(BF16)
    branch = scatter_rows(dot(hidden, full_down))
    x_mid_own = x_mid[:per_tile]
    output = (live * (x_mid_own + gate_b * branch)).astype(BF16)

    dy = live * dy_all.astype(F32)
    dy_own = dy[:per_tile]
    grad_gate_b = jnp.sum(dy_own * branch, axis=0, keepdims=True)
    grad_branch = (gate_b * dy).astype(BF16)
    g_down = dot_tn(hidden, grad_branch).astype(BF16)
    grad_hidden = dot_nt(grad_branch, full_down)
    grad_gu = jnp.concatenate(
        [grad_hidden * up * sigmoid * (1.0 + gate * (1.0 - sigmoid)), grad_hidden * silu_g], axis=1
    ).astype(BF16)
    g_gu = dot_tn(mlp_in, grad_gu).astype(BF16)
    grad_mlp_in = scatter_rows(dot_nt(grad_gu, full_gu))
    normed_own = normed_b[:per_tile]
    grad_scale_b = jnp.sum(grad_mlp_in * normed_own, axis=0, keepdims=True)
    grad_shift_b = jnp.sum(grad_mlp_in, axis=0, keepdims=True)
    grad_mid = dy_own + norm_back(grad_mlp_in * (1.0 + scale_b), normed_own, inv_b[:per_tile])
    grad_gate_a = jnp.sum(grad_mid * attended[:per_tile], axis=0, keepdims=True)
    grad_att = gather_rows((gate_a * grad_mid).astype(BF16))

    out_width = width // TILES
    g_out = dot_tn(mixed_all, lax.dynamic_slice_in_dim(grad_att, tile * out_width, out_width, 1))
    g_out = jnp.concatenate(
        absolute([g_out[COLS * j : COLS * (j + 1)].astype(BF16) for j in range(4)])
    )
    grad_mixed = dot_nt(grad_att, full_out[:COLS]).astype(BF16)
    grad_qkv, gains = attention_backward(
        grad_mixed, qraw, kraw, queries, keys, values, mixedp, cos, sin, gq, gk, spread
    )
    g_qkv = dot_tn(attn_in, grad_qkv).astype(BF16)
    grad_attn_in = scatter_rows(dot_nt(grad_qkv, full_first[:, : 3 * COLS]))
    x_own = x_float[:per_tile]
    inv_a = inverse_rms(x_own)
    normed_a = x_own * inv_a
    grad_scale_a = jnp.sum(grad_attn_in * normed_a, axis=0, keepdims=True)
    grad_shift_a = jnp.sum(grad_attn_in, axis=0, keepdims=True)
    grad_tokens = (grad_mid + norm_back(grad_attn_in * (1.0 + scale_a), normed_a, inv_a)).astype(BF16)

    grad_mod = jnp.concatenate(
        [grad_shift_a, grad_scale_a, grad_gate_a, grad_shift_b, grad_scale_b, grad_gate_b], axis=1
    )
    grad_mod = sum_tiles(grad_mod)
    gain_sums = sum_tiles(gains[:2])
    gain_sums = tree_sum(flip_gather(gain_sums.reshape(1, 2 * LANES), count))
    mod_all = flip_gather(grad_mod.astype(BF16), count)
    grad_bias = tree_sum(mod_all.astype(F32)).reshape(-1)
    ada_cols = mod_all.shape[1] // TILES
    grad_ada = dot_tn(silu_rows, lax.dynamic_slice_in_dim(mod_all, tile * ada_cols, ada_cols, 1))
    grad_silu = flip_gather(dot_nt(mod_all, w_ada).reshape(1, count * shard), count)
    grad_silu = grad_silu.reshape(count, count, shard)
    flips = jnp.arange(count) ^ img
    grad_silu = grad_silu[flips, flips].reshape(1, width)
    sigmoid_c = jax.nn.sigmoid(cond_float)
    grad_cond = (grad_silu * sigmoid_c * (1.0 + cond_float * (1.0 - sigmoid_c))).astype(BF16)

    s_down = scatter_weight(g_down, count, "ring").astype(BF16)
    s_gu = scatter_weight(g_gu, count, "ring").astype(BF16)
    s_out = scatter_weight(g_out, count, "ring")
    s_qkv = scatter_weight(g_qkv, count, "ring").astype(BF16)

    down_cols = width // TILES
    grad_down = jnp.concatenate(
        exchange_tiles(lambda t: lax.dynamic_slice_in_dim(s_down, t * down_cols, down_cols, 1))
    ).astype(F32)
    gu_cols = 2 * hidden_own // TILES
    got = exchange_tiles(lambda t: lax.dynamic_slice_in_dim(s_gu, t * gu_cols, gu_cols, 1))
    groups = gu_cols // ff_own
    grad_w_gu = jnp.concatenate(
        [got[s][:, ff_own * g : ff_own * (g + 1)] for g in range(groups) for s in range(4)], axis=1
    ).astype(F32)
    units = jnp.stack([s_qkv[:, COLS * p : COLS * (p + 1)] for p in range(3)])

    def unit(table):
        return lax.dynamic_index_in_dim(units, jnp.asarray(table, jnp.int32)[tile], 0, keepdims=False)

    kept = unit([0, 1, 1, 2])
    from_tx = swap(unit([1, 0, 2, 1]), "tx")
    from_ty = swap(unit([2, 2, 0, 0]), "ty")
    slots = jnp.stack([kept, from_tx, from_ty])
    places = jnp.asarray([[0, 1, 2], [2, 1, 0], [0, 1, 2], [2, 1, 0]], jnp.int32)[tile]
    grad_w_qkv = jnp.concatenate(
        [lax.dynamic_index_in_dim(slots, places[k], 0, keepdims=False) for k in range(3)], axis=1
    ).astype(F32)

    return (
        output.reshape(tokens.shape),
        grad_tokens.reshape(tokens.shape),
        grad_cond,
        grad_w_qkv,
        s_out,
        grad_w_gu,
        grad_down,
        grad_ada,
        gain_back(gain_sums[0, :LANES]),
        gain_back(gain_sums[0, LANES:]),
        grad_bias,
    )


def solution(mesh):
    tiled = P("img", "ty", "tx", None)
    rows = P("img", None)
    cut = P("img", ("ty", "tx"))
    in_specs = (tiled, rows, P("img"), rows, rows, rows, rows, rows, P(), P(), P(), tiled)
    out_specs = (tiled, tiled, rows, cut, cut, cut, cut, cut, P(), P(), P())
    return jax.shard_map(
        functools.partial(body, mesh.shape["img"]),
        mesh=mesh,
        in_specs=in_specs,
        out_specs=out_specs,
        check_vma=False,
    )
```

time: 1740 us -> 653 us (0.38)
  waiting for transfers between devices: 1310 us -> 143 us
  starting transfers between devices: 1.19 us -> 147 us
  matrix products: 144 us -> 51.8 us
  Pallas kernels: 0 us -> 64.5 us
  local copies, waits for them, and re-layouts: 163 us -> 105 us
  blocking collectives: 53.9 us -> 0 us
  other arithmetic: 40.7 us -> 85.4 us
  between operations: 16.3 us -> 46.1 us
    all_gather x7 -> x0, waiting for transfers between devices: 696 us -> none  [the longest x1 206 us: body(): lax.all_gather(w_ada, 'img', axis=0, tiled=True)]
    reduce_scatter x8 -> x0, waiting for transfers between devices: 511 us -> none  [the longest x1 150 us: body(): lax.psum_scatter(ada_cols, 'img', scatter_dimension=0, tiled=True)]
    ppermute x0 -> x142, starting transfers between devices: none -> 147 us  [the longest x56 59.6 us: scatter_weight(): total = lax.ppermute(total, 'img', ring_perm(count, sign))]
    ppermute x0 -> x142, waiting for transfers between devices: none -> 143 us  [the longest x56 70.1 us: scatter_weight(): total = lax.ppermute(total, 'img', ring_perm(count, sign))]
    unnamed x140 -> x208, local copies, waits for them, and re-layouts: 144 us -> 16.3 us
    unnamed x21 -> x0, waiting for transfers between devices: 108 us -> none
    dot_general x20 -> x14, matrix products: 144 us -> 51.8 us  [the longest x5 20.2 us: dot_nt(): lax.dot_general(left, right, (((1,), (1,)), ((), ())), preferred_element_...]
    pallas_call x0 -> x5, Pallas kernels: none -> 64.5 us  [the longest x1 31.2 us: attention_backward(): pl.pallas_call(attention_back_kernel, out_shape=[jax.ShapeDtypeStruct((to...]
  transfers between devices with their start and end apart: 18 -> 142, of which waited for: 15 -> 57; matrix products, arithmetic and copies ran while one was open for 14% -> 27% of each run, Pallas kernels for 0% -> 5%
where the time goes in v1:
time: 653 us; the launch traced here: 642 us
  starting transfers between devices  147 us (23%)
  waiting for transfers between devices  143 us (22%)
  local copies, waits for them, and re-layouts  105 us (16%)
  other arithmetic  85.4 us (13%)
  Pallas kernels  64.5 us (10%)
  matrix products  51.8 us (8%)
  between operations  46.1 us (7%)
    ppermute x56, waiting for transfers between devices, scatter_weight(): total = lax.ppermute(total, 'img', ring_perm(count, sign))  70.1 us
    ppermute x56, starting transfers between devices, scatter_weight(): total = lax.ppermute(total, 'img', ring_perm(count, sign))  59.6 us
    pallas_call x1, Pallas kernels, attention_backward(): pl.pallas_call(attention_back_kernel, out_shape=[jax.ShapeDtypeStruct((to...  31.2 us
    ppermute x27, waiting for transfers between devices, swap(): return lax.ppermute(values, axis, [(0, 1), (1, 0)])  31.1 us
    ppermute x21, starting transfers between devices, gather_weight(): b = lax.ppermute(b, 'img', ring_perm(count, -1))  24.9 us
    pallas_call x1, Pallas kernels, attention_forward(): pl.pallas_call(attention_kernel, out_shape=[jax.ShapeDtypeStruct((tokens,...  21 us
    ppermute x21, starting transfers between devices, gather_weight(): a = lax.ppermute(a, 'img', ring_perm(count, 1))  20.3 us
    dot_general x5, matrix products, dot_nt(): lax.dot_general(left, right, (((1,), (1,)), ((), ())), preferred_element_...  20.2 us
  transfers between devices with their start and end apart: 142, of which 57 were waited for; matrix products, arithmetic and copies ran while one was open for 27% of the time, Pallas kernels for 5%

profile of v1, /device:TPU:0, one launch (start us, length us, event | category | flops | bytes accessed | tf_op | source)
XLA Modules:
  0.0 642.2 jit_solution(10671672375467410001)
XLA Ops:
  44.3 6.3 collective-permute-done.48.refs_8_
  172.5 4.0 collective-permute-done.13.refs_6_
  185.5 4.0 assemble.3.w_ref
  193.6 4.7 assemble.4
  198.3 4.7 fusion.52
  203.1 21.0 %attention_forward.1 = (bf16[1024,1152]{1,0:T(8,128)(2,1)}, f32[1024,512]{1,0:T(8,128)}, f32[1024,512]{1,0:T(8,128)}, bf16[1024,512]{1,0:T(8,128)(2,1)}, bf16[10...) custom-call(bf16[1024,1152]{1,0:T(8,128)(2,1)} %get-tuple-element.111.x_r, ...), custom_call_target="tpu_custom_call" | custom-call | tf_op jit(solution)/shard_map/attention_forward/pallas_call | solution.py:319
  228.5 3.9 convert_multiply_fusion
  237.9 4.4 collective-permute-done.22
  254.4 4.2 broadcast_select_fusion.4
  258.6 6.1 concatenate.176
  268.5 8.0 %multiply_reduce_fusion = (f32[1024]{0:T(1024)S(1)}, f32[1024,1152]{1,0:T(8,128)S(1)}, f32[1024,1152]{1,0:T(8,128)}) fusion(f32[1152]{0:T(1024)S(1)} %get-tuple-element.85, bf16[512,1152]{1,0:T(8,128)(2,1)} %collective-permute-done.1, bf16[256,1152]{1,0:T(8,128)(2,1)} %collective-permute-done, bf16[256,1152]{1,0:T(8,128)(2,1)S(1)} %bitcast.133, ...), kind=kOutput, calls=%fused_computation.7 | convolution fusion | flops 2749758464 | bytes 16818688 | tf_op jit(solution)/shard_map/dot_general | solution.py:46
  281.1 4.2 fusion.17
  285.4 4.7 multiply_convert_fusion.2
  291.8 4.6 fusion.11
  296.4 8.0 %convolution_convert_fusion = bf16[1152,1536]{1,0:T(8,128)(2,1)S(1)} fusion(bf16[1024,768]{1,0:T(8,128)(2,1)} %copy-done.93, bf16[1024,768]{1,0:T(8,128)(2,1)} %copy-done.92, f32[1024,1152]{1,0:T(8,128)S(1)} %broadcast_multiply_fusion, f32[1152]{0:T(1024)S(1)} %get-tuple-element.82, f32[1152]{0:T(1024)S(1)} %get-tuple-element.83), kind=kOutput, calls=%fused_computation.3 | convolution fusion | flops 3635478528 | bytes 11412480 | tf_op jit(solution)/shard_map/dot_general | solution.py:54
  322.2 4.5 collective-permute-done.110
  398.3 4.1 collective-permute-done.109
  405.4 6.5 %collective-permute-done.60 = bf16[256,1152]{1,0:T(8,128)(2,1)S(1)} collective-permute-done((bf16[256,1152]{1,0:T(8,128)(2,1)S(1)}, bf16[256,1152]{1,0:T(8,128)(2,1)S(1)}, u32[]{:S(2)}, u32[]{:S(2)}) %collective-permute-start.60) | collective-permute-done | bytes 589856 | tf_op jit(solution)/shard_map/ppermute | solution.py:66
  418.6 8.4 %collective-permute-done.61 = bf16[256,1152]{1,0:T(8,128)(2,1)S(1)} collective-permute-done((bf16[256,1152]{1,0:T(8,128)(2,1)S(1)}, bf16[256,1152]{1,0:T(8,128)(2,1)S(1)}, u32[]{:S(2)}, u32[]{:S(2)}) %collective-permute-start.61) | collective-permute-done | bytes 589856 | tf_op jit(solution)/shard_map/ppermute | solution.py:66
  439.8 31.2 %attention_backward.1 = (bf16[1024,864]{1,0:T(8,128)(2,1)}, f32[8,128]{1,0:T(8,128)}) custom-call(bf16[1024,288]{1,0:T(8,128)(2,1)} %copy.122.grad_ref, f32[1024,512]{1,0:T(8,128)} %get-tuple-element.22.qraw_ref, f32[1024,512]{1,0:T(8,128)} %get-tuple-element.23.kraw_ref, bf16[1024,512]{1,0:T(8,128)(2,1)} %get-tuple-element.24.q_ref, ...), custom_call_target="tpu_custom_call" | custom-call | tf_op jit(solution)/shard_map/attention_backward/pallas_call | solution.py:417
  471.0 6.7 %fusion.9 = f32[1024,1152]{1,0:T(8,128)} fusion(bf16[1024,864]{1,0:T(8,128)(2,1)} %get-tuple-element.28, bf16[1152,1152]{1,0:T(8,128)(2,1)S(1)} %copy-done.2), kind=kOutput, calls=%fused_computation.36 | convolution fusion | flops 2038431744 | bytes 8552448 | tf_op jit(solution)/shard_map/dot_general | solution.py:50
  564.5 4.6 collective-permute-done.83
  571.5 4.9 collective-permute-done.84
  599.4 5.7 collective-permute-done.64
  (715 shorter events, 426.6 us)
Async XLA Ops:
  7.4 45.2 %collective-permute-start.8 = (bf16[80,1152]{1,0:T(8,128)(2,1)}, bf16[80,1152]{1,0:T(8,128)(2,1)}, u32[]{:S(2)}, u32[]{:S(2)}) collective-permute-start(bf16[80,1152]{1,0:T(8,128)(2,1)} %slice.398), channel_id=1, source_target_pairs={{0,8},{8,16},{16,24},{24,28},{28,20},{20,12},{12,4},{4,0},{1,9},{9... | collective-permute-start | bytes 552968 | tf_op jit(solution)/shard_map/ppermute | solution.py:180
  9.7 41.6 %collective-permute-start.15 = (bf16[64,1152]{1,0:T(8,128)(2,1)}, bf16[64,1152]{1,0:T(8,128)(2,1)}, u32[]{:S(2)}, u32[]{:S(2)}) collective-permute-start(bf16[64,1152]{1,0:T(8,128)(2,1)} %slice.399), channel_id=1, source_target_pairs={{0,4},{8,0},{16,8},{24,16},{28,24},{20,28},{12,20},{4,12},{1,5},{9... | collective-permute-start | bytes 442376 | tf_op jit(solution)/shard_map/ppermute | solution.py:181
  15.5 47.1 %collective-permute-start.27 = (bf16[80,1536]{1,0:T(8,128)(2,1)}, bf16[80,1536]{1,0:T(8,128)(2,1)}, u32[]{:S(2)}, u32[]{:S(2)}) collective-permute-start(bf16[80,1536]{1,0:T(8,128)(2,1)} %slice.315), channel_id=1, source_target_pairs={{0,8},{8,16},{16,24},{24,28},{28,20},{20,12},{12,4},{4,0},{1,9},{9... | collective-permute-start | bytes 737288 | tf_op jit(solution)/shard_map/ppermute | solution.py:180
  18.7 23.5 %collective-permute-start.41 = (bf16[48,1152]{1,0:T(8,128)(2,1)}, bf16[48,1152]{1,0:T(8,128)(2,1)}, u32[]{:S(2)}, u32[]{:S(2)}) collective-permute-start(bf16[48,1152]{1,0:T(8,128)(2,1)} %get-tuple-element.134), channel_id=1, source_target_pairs={{0,8},{8,16},{16,24},{24,28},{28,20},{20,12},{12,4},{4,0},{1,9},{9... | collective-permute-start | bytes 331784 | tf_op jit(solution)/shard_map/ppermute | solution.py:180
  74.0 75.7 %collective-permute-start = (bf16[256,1152]{1,0:T(8,128)(2,1)S(1)}, bf16[256,1152]{1,0:T(8,128)(2,1)}, u32[]{:S(2)}, u32[]{:S(2)}) collective-permute-start(bf16[256,1152]{1,0:T(8,128)(2,1)S(1)} %bitcast.130), channel_id=1, source_target_pairs={{0,2},{2,0},{1,3},{3,1},{4,6},{6,4},{5,7},{7,5},{8,10},{10,8},{9,1... | collective-permute-start | bytes 1769480 | tf_op jit(solution)/shard_map/ppermute | solution.py:66
  83.6 68.8 %collective-permute-start.57 = (bf16[256,1152]{1,0:T(8,128)(2,1)S(1)}, bf16[256,1152]{1,0:T(8,128)(2,1)}, u32[]{:S(2)}, u32[]{:S(2)}) collective-permute-start(bf16[256,1152]{1,0:T(8,128)(2,1)S(1)} %bitcast.134), channel_id=1, source_target_pairs={{0,2},{2,0},{1,3},{3,1},{4,6},{6,4},{5,7},{7,5},{8,10},{10,8},{9,1... | collective-permute-start | bytes 1769480 | tf_op jit(solution)/shard_map/ppermute | solution.py:66
  94.1 55.9 %collective-permute-start.36 = (bf16[64,1536]{1,0:T(8,128)(2,1)}, bf16[64,1536]{1,0:T(8,128)(2,1)}, u32[]{:S(2)}, u32[]{:S(2)}) collective-permute-start(bf16[64,1536]{1,0:T(8,128)(2,1)} %collective-permute-done.35.refs_9_), channel_id=1, source_target_pairs={{0,4},{8,0},{16,8},{24,16},{28,24},{20,28},{12,20},{4,12},{1,5},{9... | collective-permute-start | bytes 589832 | tf_op jit(solution)/shard_map/ppermute | solution.py:181
  95.9 60.8 %collective-permute-start.19 = (bf16[64,1152]{1,0:T(8,128)(2,1)}, bf16[64,1152]{1,0:T(8,128)(2,1)}, u32[]{:S(2)}, u32[]{:S(2)}) collective-permute-start(bf16[64,1152]{1,0:T(8,128)(2,1)} %collective-permute-done.18.refs_11_), channel_id=1, source_target_pairs={{0,4},{8,0},{16,8},{24,16},{28,24},{20,28},{12,20},{4,12},{1,5},{9... | collective-permute-start | bytes 442376 | tf_op jit(solution)/shard_map/ppermute | solution.py:181
  96.9 60.8 %collective-permute-start.30 = (bf16[80,1536]{1,0:T(8,128)(2,1)}, bf16[80,1536]{1,0:T(8,128)(2,1)}, u32[]{:S(2)}, u32[]{:S(2)}) collective-permute-start(bf16[80,1536]{1,0:T(8,128)(2,1)} %collective-permute-done.29.refs_3_), channel_id=1, source_target_pairs={{0,8},{8,16},{16,24},{24,28},{28,20},{20,12},{12,4},{4,0},{1,9},{9... | collective-permute-start | bytes 737288 | tf_op jit(solution)/shard_map/ppermute | solution.py:180
  168.4 29.9 %collective-permute-start.1 = (bf16[512,1152]{1,0:T(8,128)(2,1)}, bf16[512,1152]{1,0:T(8,128)(2,1)}, u32[]{:S(2)}, u32[]{:S(2)}) collective-permute-start(bf16[512,1152]{1,0:T(8,128)(2,1)} %pad_maximum_fusion.5), channel_id=1, source_target_pairs={{0,1},{1,0},{2,3},{3,2},{4,5},{5,4},{6,7},{7,6},{8,9},{9,8},{10,11... | collective-permute-start | bytes 3538952 | tf_op jit(solution)/shard_map/ppermute | solution.py:66
  168.5 60.0 %collective-permute-start.58 = (bf16[512,1152]{1,0:T(8,128)(2,1)}, bf16[512,1152]{1,0:T(8,128)(2,1)}, u32[]{:S(2)}, u32[]{:S(2)}) collective-permute-start(bf16[512,1152]{1,0:T(8,128)(2,1)} %pad_maximum_fusion.6), channel_id=1, source_target_pairs={{0,1},{1,0},{2,3},{3,2},{4,5},{5,4},{6,7},{7,6},{8,9},{9,8},{10,11... | collective-permute-start | bytes 3538952 | tf_op jit(solution)/shard_map/ppermute | solution.py:66
  192.3 40.1 %collective-permute-start.24 = (bf16[1152,288]{0,1:T(8,128)(2,1)}, bf16[1152,288]{0,1:T(8,128)(2,1)}, u32[]{:S(2)}, u32[]{:S(2)}) collective-permute-start(bf16[1152,288]{0,1:T(8,128)(2,1)} %copy.112), channel_id=1, source_target_pairs={{0,2},{2,0},{1,3},{3,1},{4,6},{6,4},{5,7},{7,5},{8,10},{10,8},{9,1... | collective-permute-start | bytes 1990664 | tf_op jit(solution)/shard_map/ppermute | solution.py:66
  193.6 41.9 %collective-permute-start.26 = (bf16[1152,288]{0,1:T(8,128)(2,1)}, bf16[1152,288]{0,1:T(8,128)(2,1)}, u32[]{:S(2)}, u32[]{:S(2)}) collective-permute-start(bf16[1152,288]{0,1:T(8,128)(2,1)} %copy.112), channel_id=1, source_target_pairs={{0,1},{1,0},{2,3},{3,2},{4,5},{5,4},{6,7},{7,6},{8,9},{9,8},{10,11... | collective-permute-start | bytes 1990664 | tf_op jit(solution)/shard_map/ppermute | solution.py:66
  307.9 73.7 %collective-permute-start.55 = (bf16[512,1152]{1,0:T(8,128)(2,1)}, bf16[512,1152]{1,0:T(8,128)(2,1)}, u32[]{:S(2)}, u32[]{:S(2)}) collective-permute-start(bf16[512,1152]{1,0:T(8,128)(2,1)} %slice.606), channel_id=1, source_target_pairs={{0,1},{1,0},{2,3},{3,2},{4,5},{5,4},{6,7},{7,6},{8,9},{9,8},{10,11... | collective-permute-start | bytes 3538952 | tf_op jit(solution)/shard_map/ppermute | solution.py:66
  309.6 74.4 %collective-permute-start.59 = (bf16[512,1152]{1,0:T(8,128)(2,1)}, bf16[512,1152]{1,0:T(8,128)(2,1)}, u32[]{:S(2)}, u32[]{:S(2)}) collective-permute-start(bf16[512,1152]{1,0:T(8,128)(2,1)} %slice.605), channel_id=1, source_target_pairs={{0,1},{1,0},{2,3},{3,2},{4,5},{5,4},{6,7},{7,6},{8,9},{9,8},{10,11... | collective-permute-start | bytes 3538952 | tf_op jit(solution)/shard_map/ppermute | solution.py:66
  310.0 23.1 %collective-permute-start.103 = (bf16[80,1536]{1,0:T(8,128)(2,1)S(1)}, bf16[80,1536]{1,0:T(8,128)(2,1)S(1)}, u32[]{:S(2)}, u32[]{:S(2)}) collective-permute-start(bf16[80,1536]{1,0:T(8,128)(2,1)S(1)} %constant_dynamic-slice_fusion.11), channel_id=1, source_target_pairs={{0,8},{8,16},{16,24},{24,28},{28,20},{20,12},{12,4},{4,0},{1,9},{9... | collective-permute-start | bytes 737288 | tf_op jit(solution)/shard_map/ppermute | solution.py:220
  383.9 29.0 %collective-permute-start.56 = (bf16[256,1152]{1,0:T(8,128)(2,1)S(1)}, bf16[256,1152]{1,0:T(8,128)(2,1)S(1)}, u32[]{:S(2)}, u32[]{:S(2)}) collective-permute-start(bf16[256,1152]{1,0:T(8,128)(2,1)S(1)} %slice.609), channel_id=1, source_target_pairs={{0,2},{2,0},{1,3},{3,1},{4,6},{6,4},{5,7},{7,5},{8,10},{10,8},{9,1... | collective-permute-start | bytes 1769480 | tf_op jit(solution)/shard_map/ppermute | solution.py:66
  385.8 26.1 %collective-permute-start.60 = (bf16[256,1152]{1,0:T(8,128)(2,1)S(1)}, bf16[256,1152]{1,0:T(8,128)(2,1)S(1)}, u32[]{:S(2)}, u32[]{:S(2)}) collective-permute-start(bf16[256,1152]{1,0:T(8,128)(2,1)S(1)} %slice.608), channel_id=1, source_target_pairs={{0,2},{2,0},{1,3},{3,1},{4,6},{6,4},{5,7},{7,5},{8,10},{10,8},{9,1... | collective-permute-start | bytes 1769480 | tf_op jit(solution)/shard_map/ppermute | solution.py:66
  403.5 24.8 %collective-permute-start.117 = (bf16[144,384]{1,0:T(8,128)(2,1)S(1)}, bf16[144,384]{1,0:T(8,128)(2,1)S(1)}, u32[]{:S(2)}, u32[]{:S(2)}) collective-permute-start(bf16[144,384]{1,0:T(8,128)(2,1)S(1)} %get-tuple-element.147), channel_id=1, source_target_pairs={{0,3},{1,2},{2,1},{3,0},{4,7},{5,6},{6,5},{7,4},{8,11},{9,10},{10,... | collective-permute-start | bytes 331784 | tf_op jit(solution)/shard_map/ppermute | solution.py:103
  403.6 24.7 %collective-permute-start.118 = (bf16[144,384]{1,0:T(8,128)(2,1)S(1)}, bf16[144,384]{1,0:T(8,128)(2,1)S(1)}, u32[]{:S(2)}, u32[]{:S(2)}) collective-permute-start(bf16[144,384]{1,0:T(8,128)(2,1)S(1)} %get-tuple-element.148), channel_id=1, source_target_pairs={{0,2},{2,0},{1,3},{3,1},{4,6},{6,4},{5,7},{7,5},{8,10},{10,8},{9,1... | collective-permute-start | bytes 331784 | tf_op jit(solution)/shard_map/ppermute | solution.py:66
  403.8 24.4 %collective-permute-start.119 = (bf16[144,384]{1,0:T(8,128)(2,1)S(1)}, bf16[144,384]{1,0:T(8,128)(2,1)S(1)}, u32[]{:S(2)}, u32[]{:S(2)}) collective-permute-start(bf16[144,384]{1,0:T(8,128)(2,1)S(1)} %get-tuple-element.146), channel_id=1, source_target_pairs={{0,1},{1,0},{2,3},{3,2},{4,5},{5,4},{6,7},{7,6},{8,9},{9,8},{10,11... | collective-permute-start | bytes 331784 | tf_op jit(solution)/shard_map/ppermute | solution.py:66
  502.6 90.3 %collective-permute-start.63 = (bf16[512,1152]{1,0:T(8,128)(2,1)}, bf16[512,1152]{1,0:T(8,128)(2,1)}, u32[]{:S(2)}, u32[]{:S(2)}) collective-permute-start(bf16[512,1152]{1,0:T(8,128)(2,1)} %slice.604), channel_id=1, source_target_pairs={{0,1},{1,0},{2,3},{3,2},{4,5},{5,4},{6,7},{7,6},{8,9},{9,8},{10,11... | collective-permute-start | bytes 3538952 | tf_op jit(solution)/shard_map/ppermute | solution.py:66
  502.6 39.3 %collective-permute-start.73 = (bf16[80,864]{0,1:T(8,128)(2,1)}, bf16[80,864]{0,1:T(8,128)(2,1)S(1)}, u32[]{:S(2)}, u32[]{:S(2)}) collective-permute-start(bf16[80,864]{0,1:T(8,128)(2,1)} %constant_dynamic-slice_fusion.19), channel_id=1, source_target_pairs={{0,8},{8,16},{16,24},{24,28},{28,20},{20,12},{12,4},{4,0},{1,9},{9... | collective-permute-start | bytes 414728 | tf_op jit(solution)/shard_map/ppermute | solution.py:220
  503.9 31.8 %collective-permute-start.80 = (bf16[64,864]{0,1:T(8,128)(2,1)}, bf16[64,864]{0,1:T(8,128)(2,1)}, u32[]{:S(2)}, u32[]{:S(2)}) collective-permute-start(bf16[64,864]{0,1:T(8,128)(2,1)} %constant_dynamic-slice_fusion.18), channel_id=1, source_target_pairs={{0,4},{8,0},{16,8},{24,16},{28,24},{20,28},{12,20},{4,12},{1,5},{9... | collective-permute-start | bytes 331784 | tf_op jit(solution)/shard_map/ppermute | solution.py:220
  (217 other events, 2955.9 us)

commit v2 on v1

v2 whole, which is shorter than its diff:
```python
import functools
import math

import jax
import jax.numpy as jnp
import numpy as np
from jax import lax
from jax.experimental import pallas as pl
from jax.experimental.pallas import tpu as pltpu
from jax.sharding import PartitionSpec as P

HEADS = 16
HEAD = 72
FF = 3072
TILES = 4
OWN = HEADS // TILES
LANES = 128
COLS = OWN * HEAD
PADDED = OWN * LANES
WINDOW = 384
QUARTER = HEAD // 4
EPSILON = 1e-06
LOG2E = math.log2(math.e)
LN2 = math.log(2.0)
BF16 = jnp.bfloat16
F32 = jnp.float32


def head_lane(index):
    part, half, freq = index // 36, (index % 36) // QUARTER, index % QUARTER
    return half * 64 + part * QUARTER + freq


def spread_matrices():
    spread = np.zeros((4, WINDOW, PADDED), np.float32)
    for which in range(4):
        base = (COLS - 256) * which if which < 3 else 0
        for head in range(OWN):
            for index in range(HEAD):
                lane = index if which >= 2 else head_lane(index)
                spread[which, base + HEAD * head + index, LANES * head + lane] = 1.0
    return spread


def dot(left, right):
    return jnp.dot(left, right, preferred_element_type=F32)


def dot_nt(left, right):
    return lax.dot_general(left, right, (((1,), (1,)), ((), ())), preferred_element_type=F32)


def dot_tn(left, right):
    return lax.dot_general(left, right, (((0,), (0,)), ((), ())), preferred_element_type=F32)


def inverse_rms(values):
    return lax.rsqrt(jnp.mean(values * values, axis=-1, keepdims=True) + EPSILON)


def norm_back(grad_out, normed, inv_scale):
    return inv_scale * (grad_out - normed * jnp.mean(grad_out * normed, axis=-1, keepdims=True))


def swap(values, axis):
    return lax.ppermute(values, axis, [(0, 1), (1, 0)])


FLIPS = (2, 3, 0, 1)


def tile_at(flip):
    return (lax.axis_index("ty") ^ (flip >> 1)) * 2 + (lax.axis_index("tx") ^ (flip & 1))


def gather_tiles(values):
    far = swap(values, "ty")
    return [far, swap(far, "tx"), values, swap(values, "tx")]


def sum_tiles(values):
    values = values + swap(values, "tx")
    return values + swap(values, "ty")


def absolute(pieces):
    ty, tx = lax.axis_index("ty"), lax.axis_index("tx")
    turned = [jnp.where(tx == 1, pieces[f ^ 1], pieces[f]) for f in range(4)]
    return [jnp.where(ty == 1, turned[f ^ 2], turned[f]) for f in range(4)]


def exchange_tiles(piece_for):
    across = [(a * 2 + b, (1 - a) * 2 + 1 - b) for a in range(2) for b in range(2)]
    return absolute(
        [
            piece_for(tile_at(0)),
            swap(piece_for(tile_at(1)), "tx"),
            swap(piece_for(tile_at(2)), "ty"),
            lax.ppermute(piece_for(tile_at(3)), ("ty", "tx"), across),
        ]
    )


def flip_perm(count, bit):
    return [(i, i ^ bit) for i in range(count)]


def flip_exchange(values, count, bits):
    rows = [values[k : k + 1] for k in range(count)]
    for bit in bits:
        sent = jnp.concatenate([rows[k] for k in range(count) if k & bit])
        got = lax.ppermute(sent, "img", flip_perm(count, bit))
        moved = [k for k in range(count) if k & bit]
        for place, k in enumerate(moved):
            rows[k] = got[place : place + 1]
    return jnp.concatenate(rows)


def ring_perm(count, step):
    order = list(range(0, count, 2)) + list(range(count - 1, 0, -2))
    return [(order[i], order[(i + step) % count]) for i in range(count)]


def ring_place(count):
    index = lax.axis_index("img")
    return jnp.where(index % 2 == 0, index // 2, count - 1 - index // 2)


def ring_owner(count, place):
    place = (place + count) % count
    return jnp.where(place < count // 2, 2 * place, 2 * (count - 1 - place) + 1)


def use_ring(count, rows):
    return 2 < count <= 16 and count % 2 == 0 and rows % 16 == 0


def split_rows(rows):
    return (rows // 2 + 15) // 16 * 16


def out_share(pick, first):
    return dot_nt(pick, first[:, first.shape[1] - WINDOW :]).astype(BF16)


def ring_gather(own, count, beside):
    cut = split_rows(own.shape[0])
    a, b = own[:cut], own[cut:]
    pieces, value = [], None
    for hop in range(count - 1):
        a = lax.ppermute(a, "img", ring_perm(count, 1))
        b = lax.ppermute(b, "img", ring_perm(count, -1))
        if hop < len(beside):
            value = beside[hop](value)
            a, b, value = lax.optimization_barrier((a, b, value))
        pieces.append((a, b))
    for step in beside[count - 1 :]:
        value = step(value)
    return pieces, value


def assemble_kernel(count, total, plan, shared, index_ref, pick_ref, *refs):
    cut = split_rows(total)
    own, pieces_a, pieces_b = refs[0], refs[1:count], refs[count : 2 * count - 1]
    outs, sems = refs[2 * count - 1 : -1], refs[-1]
    started = []
    for k, (src, first, size) in enumerate(
        [(own, 0, total)]
        + [(piece, 0, cut) for piece in pieces_a]
        + [(piece, cut, total - cut) for piece in pieces_b]
    ):
        for out, rows, base, count_rows, to_row, from_lane, to_lane, lanes in plan:
            low, high = max(first, base), min(first + size, base + count_rows)
            if low < high:
                start = pl.multiple_of(index_ref[k] * rows + to_row + low - base, 16)
                copy = pltpu.make_async_copy(
                    src.at[pl.ds(low - first, high - low), pl.ds(from_lane, lanes)],
                    outs[out].at[pl.ds(start, high - low), pl.ds(to_lane, lanes)],
                    sems.at[len(started)],
                )
                copy.start()
                started.append(copy)
    for copy in started:
        copy.wait()
    if shared:
        outs[-1][...] = out_share(pick_ref[...], outs[0])


def assemble(own, pieces, shapes, plan, count, shared):
    place = ring_place(count)
    steps = jnp.asarray([0] + [-k for k in range(1, count)] + list(range(1, count)), jnp.int32)
    index = ring_owner(count, place + steps).astype(jnp.int32)
    copies = 2 * count - 1
    shapes = [jax.ShapeDtypeStruct(shape, own.dtype) for shape in shapes]
    return pl.pallas_call(
        functools.partial(assemble_kernel, count, own.shape[0], plan, shared),
        out_shape=shapes,
        in_specs=[smem(), vmem()] + [pl.BlockSpec(memory_space=pltpu.HBM)] * copies,
        out_specs=[vmem() for _ in shapes],
        scratch_shapes=[pltpu.SemaphoreType.DMA((2 * len(plan) * copies,))],
        compiler_params=limit(58),
        cost_estimate=cost(5),
        name="assemble_first" if shared else "assemble_gu",
    )(index, out_pick(), own, *[a for a, _ in pieces], *[b for _, b in pieces])


def out_pick():
    pick = np.zeros((COLS, WINDOW), np.float32)
    pick[np.arange(COLS), WINDOW - COLS + np.arange(COLS)] = 1.0
    return jnp.asarray(pick, BF16)


def after(value, *others):
    return lax.optimization_barrier((value, others))[0]


def ring_scatter(grads, count, beside):
    sizes = [grad.shape[0] // count for grad in grads]
    total = sum(sizes)
    cut = split_rows(total)
    place = ring_place(count)
    value = None

    def part(sign, step):
        owner = ring_owner(count, place - sign * step)
        first, last = (0, cut) if sign > 0 else (cut, total)
        found, base = [], 0
        for grad, rows in zip(grads, sizes):
            low, high = max(first, base), min(last, base + rows)
            if low < high:
                found.append(lax.dynamic_slice_in_dim(grad, owner * rows + low - base, high - low, 0))
            base += rows
        return jnp.concatenate(found)

    sums = [part(1, 1), part(-1, 1)]
    for step in range(2, count + 1):
        kind = BF16 if step < count else F32
        got = [lax.ppermute(sums[k], "img", ring_perm(count, sign)) for k, sign in enumerate((1, -1))]
        if step - 2 < len(beside) and beside[step - 2]:
            value = beside[step - 2](value)
            got, value = lax.optimization_barrier((got, value))
        for k, sign in enumerate((1, -1)):
            sums[k] = (got[k].astype(F32) + part(sign, step).astype(F32)).astype(kind)
    for step in beside[count - 1 :]:
        value = step(value)
    return sums, value


def vmem():
    return pl.BlockSpec(memory_space=pltpu.VMEM)


def limit(megabytes):
    return pltpu.CompilerParams(vmem_limit_bytes=megabytes * 1024 * 1024)


def cost(microseconds):
    return pl.CostEstimate(
        flops=int(microseconds * 1.1e9), bytes_accessed=int(microseconds * 3e6), transcendentals=0
    )


def lane_ids(rows):
    return lax.broadcasted_iota(jnp.int32, (rows, LANES), 1)


def three_parts(column):
    high = column.astype(BF16)
    rest = column - high.astype(F32)
    mid = rest.astype(BF16)
    return high, mid, (rest - mid.astype(F32)).astype(BF16)


def put_lanes(values, first, parts):
    lanes = lane_ids(values.shape[0])
    for k, part in enumerate(parts):
        values = jnp.where(lanes == first + k, part.astype(values.dtype), values)
    return values


QK_SPARE = 100
V_SPARE = HEAD


PAIRS = OWN // 2
PAIR = 2 * LANES
PAIR_COLS = 2 * HEAD


def project_kernel(
    x0_ref, x1_ref, x2_ref, x3_ref, mod_ref, w_ref, cos_ref, sin_ref, gq_ref, gk_ref, spread_ref,
    attn_ref, qraw_ref, kraw_ref, q0_ref, q1_ref, k0_ref, k1_ref, v0_ref, v1_ref, wpad_ref,
):
    block = x0_ref.shape[0]
    tokens = 4 * block
    factor = LOG2E / math.sqrt(HEAD)

    for place, x_ref in enumerate((x0_ref, x1_ref, x2_ref, x3_ref)):
        x = x_ref[...].astype(F32)
        normed = x * inverse_rms(x)
        attn_ref[block * place : block * (place + 1), :] = (
            normed * (1.0 + mod_ref[1:2, :]) + mod_ref[0:1, :]
        ).astype(BF16)

    @pl.loop(0, w_ref.shape[0] // 128)
    def _(i):
        rows = pl.ds(pl.multiple_of(i * 128, 128), 128)
        for w in range(3):
            wpad_ref[rows, PADDED * w : PADDED * (w + 1)] = dot(
                w_ref[rows, 256 * w : 256 * w + WINDOW], spread_ref[w]
            ).astype(BF16)

    @pl.loop(0, tokens // block)
    def _(i):
        rows = pl.ds(pl.multiple_of(i * block, block), block)
        attn_in = attn_ref[rows, :]
        cos, sin = cos_ref[rows, :], sin_ref[rows, :]
        lanes = lane_ids(block)
        spare = (lanes >= QK_SPARE) & (lanes < QK_SPARE + 3)
        for which, raw_ref, out_refs, gain_ref in (
            (0, qraw_ref, (q0_ref, q1_ref), gq_ref),
            (1, kraw_ref, (k0_ref, k1_ref), gk_ref),
        ):
            raw = dot(attn_in, wpad_ref[:, PADDED * which : PADDED * (which + 1)])
            raw_ref[rows, :] = raw
            for head in range(OWN):
                part = raw[:, LANES * head : LANES * (head + 1)]
                inv = lax.rsqrt(jnp.sum(part * part, axis=-1, keepdims=True) / HEAD + EPSILON)
                scaled = part * inv * gain_ref[...]
                turned = scaled * cos + pltpu.roll(scaled, 64, 1) * sin
                turned = turned * factor if which == 0 else jnp.where(spare, 1.0, turned)
                at = slice(LANES * (head % 2), LANES * (head % 2 + 1))
                out_refs[head // 2][rows, at] = turned.astype(BF16)
        value = dot(attn_in, wpad_ref[:, PADDED * 2 : PADDED * 3])
        ones = (lanes >= V_SPARE) & (lanes < V_SPARE + 3)
        for head in range(OWN):
            at = slice(LANES * (head % 2), LANES * (head % 2 + 1))
            part = value[:, LANES * head : LANES * (head + 1)]
            (v0_ref, v1_ref)[head // 2][rows, at] = jnp.where(ones, 1.0, part).astype(BF16)


def project(x_tiles, mod, w, cos, sin, gq, gk, spread):
    width = w.shape[0]
    tokens = cos.shape[0]
    return pl.pallas_call(
        project_kernel,
        out_shape=[
            jax.ShapeDtypeStruct((tokens, width), BF16),
            jax.ShapeDtypeStruct((tokens, PADDED), F32),
            jax.ShapeDtypeStruct((tokens, PADDED), F32),
        ]
        + [jax.ShapeDtypeStruct((tokens, PAIR), BF16)] * 6,
        in_specs=[vmem()] * 11,
        out_specs=[vmem()] * 9,
        scratch_shapes=[pltpu.VMEM((width, 3 * PADDED), BF16)],
        cost_estimate=cost(16),
        compiler_params=limit(34),
        name="project",
    )(*x_tiles, mod, w, cos, sin, gq, gk, spread)


def attend_kernel(qin_ref, k_ref, v_ref, spread_ref, q_ref, mixedp_ref, mixed_ref):
    tokens = qin_ref.shape[0]
    block = 256

    @pl.loop(0, tokens // block)
    def _(i):
        rows = pl.ds(pl.multiple_of(i * block, block), block)
        for head in range(2):
            at = slice(LANES * head, LANES * (head + 1))
            query = qin_ref[rows, at]
            terms = jnp.exp2(dot_nt(query, k_ref[:, at])).astype(BF16)
            result = dot(terms, v_ref[:, at])
            total = result[:, V_SPARE : V_SPARE + 1]
            mixedp_ref[rows, at] = (result * (1.0 / total)).astype(BF16)
            q_ref[rows, at] = put_lanes(query, QK_SPARE, three_parts(-jnp.log2(total)))
        mixed_ref[:, rows] = dot_nt(spread_ref[3, :PAIR_COLS, :PAIR], mixedp_ref[rows, :]).astype(BF16)


def attend(q, k, v, spread):
    tokens = q.shape[0]
    return pl.pallas_call(
        attend_kernel,
        out_shape=[
            jax.ShapeDtypeStruct((tokens, PAIR), BF16),
            jax.ShapeDtypeStruct((tokens, PAIR), BF16),
            jax.ShapeDtypeStruct((PAIR_COLS, tokens), BF16),
        ],
        in_specs=[vmem()] * 4,
        out_specs=[vmem()] * 3,
        cost_estimate=cost(4.1),
        compiler_params=limit(20),
        name="attend",
    )(q, k, v, spread)


def attention_back_kernel(
    g0_ref, g1_ref, g2_ref, g3_ref, wout_ref, qraw_ref, kraw_ref, q0_ref, q1_ref, k0_ref, k1_ref, v0_ref, v1_ref,
    m0_ref, m1_ref, cos_ref, sin_ref, gq_ref, gk_ref, spread_ref, out_ref, gains_ref, do_ref, dq_ref, dk_ref, pad_ref,
):
    block = g0_ref.shape[0]
    tokens = 4 * block
    root = 1.0 / math.sqrt(HEAD)

    for place, g_ref in enumerate((g0_ref, g1_ref, g2_ref, g3_ref)):
        rows = slice(block * place, block * (place + 1))
        grad_mixed = dot(g_ref[...], wout_ref[...]).astype(BF16)
        wide = dot(grad_mixed, spread_ref[3, :COLS, :])
        for head in range(OWN):
            at = slice(LANES * head, LANES * (head + 1))
            part = wide[:, at]
            pair_at = slice(LANES * (head % 2), LANES * (head % 2 + 1))
            mixed = (m0_ref, m1_ref)[head // 2][rows, pair_at].astype(F32)
            row_dot = jnp.sum(part * mixed, axis=-1, keepdims=True)
            do_ref[rows, at] = put_lanes(part.astype(BF16), V_SPARE, three_parts(-row_dot))

    for head in range(OWN):
        at = slice(LANES * head, LANES * (head + 1))
        pair_at = slice(LANES * (head % 2), LANES * (head % 2 + 1))
        q_ref, k_ref, v_ref = ((q0_ref, k0_ref, v0_ref), (q1_ref, k1_ref, v1_ref))[head // 2]
        dq_ref[at, :] = jnp.zeros((LANES, tokens), F32)

        @pl.loop(0, tokens // block)
        def _(i, at=at, pair_at=pair_at, q_ref=q_ref, k_ref=k_ref, v_ref=v_ref, head=head):
            rows = pl.ds(pl.multiple_of(i * block, block), block)
            query, grad = q_ref[:, pair_at], do_ref[:, at]
            key = k_ref[rows, pair_at]
            probs = jnp.exp2(dot_nt(key, query))
            slope = (probs * dot_nt(v_ref[rows, pair_at], grad)).astype(BF16)
            pad_ref[rows, 2 * PADDED + LANES * head : 2 * PADDED + LANES * (head + 1)] = dot(
                probs.astype(BF16), grad
            ).astype(BF16)
            dk_ref[rows, at] = dot(slope, query) * LN2
            dq_ref[at, :] += dot(key.astype(F32).T.astype(BF16), slope)

    gains_ref[...] = jnp.zeros_like(gains_ref)

    @pl.loop(0, tokens // block)
    def _(i):
        rows = pl.ds(pl.multiple_of(i * block, block), block)
        cos, sin = cos_ref[rows, :], sin_ref[rows, :]
        for which, raw_ref, gain_ref in ((0, qraw_ref, gq_ref), (1, kraw_ref, gk_ref)):
            gained = jnp.zeros((1, LANES), F32)
            for head in range(OWN):
                at = slice(LANES * head, LANES * (head + 1))
                raw = raw_ref[rows, at]
                inv = lax.rsqrt(jnp.sum(raw * raw, axis=-1, keepdims=True) / HEAD + EPSILON)
                hat = raw * inv
                if which == 0:
                    grad = dq_ref[at, rows].T * root
                else:
                    grad = dk_ref[rows, at]
                turned = grad * cos - pltpu.roll(grad, 64, 1) * sin
                product = turned * hat
                gained += jnp.sum(product, axis=0, keepdims=True)
                mean = jnp.sum(product * gain_ref[...], axis=-1, keepdims=True) / HEAD
                pad_ref[rows, PADDED * which + LANES * head : PADDED * which + LANES * (head + 1)] = (
                    inv * (turned * gain_ref[...] - hat * mean)
                ).astype(BF16)
            gains_ref[which : which + 1, :] += gained
        compact = [
            dot_nt(pad_ref[rows, PADDED * w : PADDED * (w + 1)], spread_ref[w]).astype(BF16)
            for w in range(3)
        ]
        out_ref[rows, :] = jnp.concatenate(
            [
                compact[0][:, :256],
                compact[0][:, 256:] + compact[1][:, :128],
                compact[1][:, 128:256],
                compact[1][:, 256:] + compact[2][:, :128],
                compact[2][:, 128:],
            ],
            axis=1,
        )[:, : 3 * COLS]


def attention_backward(grads, w_rows, qraw, kraw, q, k, v, mixedp, cos, sin, gq, gk, spread):
    tokens = cos.shape[0]
    return pl.pallas_call(
        attention_back_kernel,
        out_shape=[
            jax.ShapeDtypeStruct((tokens, 3 * COLS), BF16),
            jax.ShapeDtypeStruct((8, LANES), F32),
        ],
        in_specs=[vmem()] * 20,
        out_specs=[vmem()] * 2,
        scratch_shapes=[
            pltpu.VMEM((tokens, PADDED), BF16),
            pltpu.VMEM((PADDED, tokens), F32),
            pltpu.VMEM((tokens, PADDED), F32),
            pltpu.VMEM((tokens, 3 * PADDED), BF16),
        ],
        cost_estimate=cost(32),
        compiler_params=limit(58),
        name="attention_backward",
    )(*grads, w_rows, qraw, kraw, *q, *k, *v, *mixedp, cos, sin, gq, gk, spread)


def smem():
    return pl.BlockSpec(memory_space=pltpu.SMEM)


def out_weight_kernel(tile_ref, p0_ref, p1_ref, p2_ref, p3_ref, out_ref, own_ref):
    for place, piece in enumerate((p0_ref, p1_ref, p2_ref, p3_ref)):
        start = pl.multiple_of((tile_ref[0] ^ FLIPS[place]) * COLS, 16)
        out_ref[pl.ds(start, COLS), :] = piece[...]
    for tile in range(4):

        @pl.when(tile_ref[0] == tile)
        def _(tile=tile):
            own_ref[...] = out_ref[:, COLS * tile : COLS * (tile + 1)]


def out_weight(tile, pieces):
    width = pieces[0].shape[1]
    return pl.pallas_call(
        out_weight_kernel,
        out_shape=[
            jax.ShapeDtypeStruct((width, width), BF16),
            jax.ShapeDtypeStruct((width, COLS), BF16),
        ],
        in_specs=[smem()] + [vmem()] * 4,
        out_specs=[vmem()] * 2,
        cost_estimate=cost(3.8),
        compiler_params=limit(12),
        name="out_weight",
    )(tile, *pieces)


def mlp_kernel(places, tile_ref, mod_ref, wout_ref, wgu_ref, wdown_ref, *refs):
    number = len(places)
    x_refs, dy_refs, mixed_refs = refs[:number], refs[number : 2 * number], refs[2 * number : 2 * number + 4 * PAIRS]
    refs = refs[-(4 + 2 * number + (2 in places) + 1) :]
    mlp_ref, hidden_ref, ggu_ref, gbranch_ref = refs[:4]
    branch_refs, gmlp_refs, mixed_ref = refs[4 : 4 + number], refs[4 + number : 4 + 2 * number], refs[-1]
    block = x_refs[0].shape[0]
    half = wgu_ref.shape[1] // 2
    for k, m_ref in enumerate(mixed_refs):
        pair, source = k // 4, k % 4
        start = pl.multiple_of((tile_ref[0] ^ FLIPS[source]) * COLS + PAIR_COLS * pair, 16)
        for n, place in enumerate(places):
            at = block * (place ^ FLIPS[source])
            mixed_ref[pl.ds(start, PAIR_COLS), block * n : block * (n + 1)] = m_ref[:, at : at + block]
    for n, (place, x_ref, dy_ref, branch_ref, gmlp_ref) in enumerate(
        zip(places, x_refs, dy_refs, branch_refs, gmlp_refs)
    ):
        here = slice(block * n, block * (n + 1))
        attended = lax.dot_general(
            mixed_ref[:, here], wout_ref[...], (((0,), (1,)), ((), ())), preferred_element_type=F32
        )
        if place == 2:
            refs[-2][...] = attended
        x_mid = x_ref[...].astype(F32) + mod_ref[2:3, :] * attended
        normed = x_mid * inverse_rms(x_mid)
        mlp_in = (normed * (1.0 + mod_ref[4:5, :]) + mod_ref[3:4, :]).astype(BF16)
        mlp_ref[here, :] = mlp_in
        grad_branch = (mod_ref[5:6, :] * (mod_ref[6:7, :] * dy_ref[...].astype(F32))).astype(BF16)
        gbranch_ref[here, :] = grad_branch
        gate = dot(mlp_in, wgu_ref[:, :half])
        up = dot(mlp_in, wgu_ref[:, half:])
        grad_hidden = dot_nt(grad_branch, wdown_ref[...])
        sigmoid = jax.nn.sigmoid(gate)
        silu = gate * sigmoid
        hidden = (silu * up).astype(BF16)
        hidden_ref[here, :] = hidden
        branch_ref[...] = dot(hidden, wdown_ref[...]).astype(BF16)
        grad_gate = (grad_hidden * up * (sigmoid * (1.0 + gate * (1.0 - sigmoid)))).astype(BF16)
        grad_up = (grad_hidden * silu).astype(BF16)
        ggu_ref[here, :half] = grad_gate
        ggu_ref[here, half:] = grad_up
        gmlp_ref[...] = (
            dot_nt(grad_gate, wgu_ref[:, :half]) + dot_nt(grad_up, wgu_ref[:, half:])
        ).astype(BF16)


def mlp(places, tile, mod, w_out, w_gu, w_down, x_tiles, dy_tiles, mixed, kept):
    number = len(places)
    block, width = x_tiles[0].shape
    hidden = w_down.shape[0]
    one = pl.Buffered(1)
    row_block = lambda cols: pl.BlockSpec(
        (number * block, cols), lambda i: (places[0] // number, 0), pipeline_mode=one
    )
    whole = lambda rows, cols: pl.BlockSpec((rows, cols), lambda i: (0, 0), pipeline_mode=one)
    args = [mod, w_out, w_gu, w_down]
    args += [x_tiles[p] for p in places] + [dy_tiles[p] for p in places] + list(mixed)
    in_specs = [smem()] + [whole(*arg.shape) for arg in args]
    args = [tile] + args
    aliases = {}
    for k, array in enumerate(kept):
        aliases[len(args)] = k
        args.append(array)
        in_specs.append(pl.BlockSpec(memory_space=pl.ANY))
    shapes = [(4 * block, width), (4 * block, hidden), (4 * block, 2 * hidden), (4 * block, width)]
    attended = [jax.ShapeDtypeStruct((block, width), F32)] if 2 in places else []
    return pl.pallas_call(
        functools.partial(mlp_kernel, places),
        grid=(1,),
        out_shape=[jax.ShapeDtypeStruct(shape, BF16) for shape in shapes]
        + [jax.ShapeDtypeStruct((block, width), BF16)] * (2 * number)
        + attended,
        in_specs=in_specs,
        out_specs=[row_block(shape[1]) for shape in shapes]
        + [whole(block, width)] * (2 * number + len(attended)),
        scratch_shapes=[pltpu.VMEM((width, number * block), BF16)],
        input_output_aliases=aliases,
        compiler_params=limit(44),
        cost_estimate=cost(7 * number),
        name="mlp",
    )(*args)


def middle_kernel(a_ref, b_ref, c0_ref, c1_ref, attended_ref, x_ref, dy_ref, mod_ref, gatt_ref, gmid_ref, sums_ref):
    far = jnp.concatenate([c0_ref[...], c1_ref[...]]).astype(F32)
    grad_in = a_ref[...].astype(F32) + b_ref[...].astype(F32) + far
    attended = attended_ref[...]
    x_mid = x_ref[...].astype(F32) + mod_ref[2:3, :] * attended
    inv = inverse_rms(x_mid)
    normed = x_mid * inv
    product = grad_in * normed
    grad_mid = mod_ref[6:7, :] * dy_ref[...].astype(F32) + inv * (
        grad_in * (1.0 + mod_ref[4:5, :])
        - normed * jnp.mean(product * (1.0 + mod_ref[4:5, :]), axis=-1, keepdims=True)
    )
    gmid_ref[...] = grad_mid
    gatt_ref[...] = (mod_ref[2:3, :] * grad_mid).astype(BF16)
    sums_ref[...] = jnp.zeros_like(sums_ref)
    sums_ref[0:1, :] = jnp.sum(grad_mid * attended, axis=0, keepdims=True)
    sums_ref[1:2, :] = jnp.sum(grad_in, axis=0, keepdims=True)
    sums_ref[2:3, :] = jnp.sum(product, axis=0, keepdims=True)


def middle(parts, attended, x, dy, mod):
    block, width = x.shape
    return pl.pallas_call(
        middle_kernel,
        out_shape=[
            jax.ShapeDtypeStruct((block, width), BF16),
            jax.ShapeDtypeStruct((block, width), F32),
            jax.ShapeDtypeStruct((8, width), F32),
        ],
        in_specs=[vmem()] * 8,
        out_specs=[vmem()] * 3,
        cost_estimate=cost(4.6),
        compiler_params=limit(14),
        name="middle",
    )(*parts, attended, x, dy, mod)


def output_kernel(a_ref, b_ref, c_ref, attended_ref, x_ref, dy_ref, mod_ref, out_ref, sums_ref):
    branch = a_ref[...].astype(F32) + b_ref[...].astype(F32) + c_ref[...].astype(F32)
    x_mid = x_ref[...].astype(F32) + mod_ref[2:3, :] * attended_ref[...]
    live = mod_ref[6:7, :]
    out_ref[...] = (live * (x_mid + mod_ref[5:6, :] * branch)).astype(BF16)
    sums_ref[...] = jnp.zeros_like(sums_ref)
    sums_ref[0:1, :] = jnp.sum(live * dy_ref[...].astype(F32) * branch, axis=0, keepdims=True)


def output_tile(parts, attended, x, dy, mod):
    block, width = x.shape
    return pl.pallas_call(
        output_kernel,
        out_shape=[
            jax.ShapeDtypeStruct((block, width), BF16),
            jax.ShapeDtypeStruct((8, width), F32),
        ],
        in_specs=[vmem()] * 7,
        out_specs=[vmem()] * 2,
        cost_estimate=cost(3.5),
        compiler_params=limit(12),
        name="output_tile",
    )(*parts, attended, x, dy, mod)


def tokens_kernel(a_ref, b_ref, c_ref, x_ref, gmid_ref, mod_ref, out_ref, sums_ref):
    grad_in = a_ref[...].astype(F32) + b_ref[...].astype(F32) + c_ref[...].astype(F32)
    x = x_ref[...].astype(F32)
    inv = inverse_rms(x)
    normed = x * inv
    product = grad_in * normed
    scale = 1.0 + mod_ref[1:2, :]
    out_ref[...] = (
        gmid_ref[...] + inv * (grad_in * scale - normed * jnp.mean(product * scale, axis=-1, keepdims=True))
    ).astype(BF16)
    sums_ref[...] = jnp.zeros_like(sums_ref)
    sums_ref[0:1, :] = jnp.sum(grad_in, axis=0, keepdims=True)
    sums_ref[1:2, :] = jnp.sum(product, axis=0, keepdims=True)


def tokens_back(parts, x, grad_mid, mod):
    block, width = x.shape
    return pl.pallas_call(
        tokens_kernel,
        out_shape=[
            jax.ShapeDtypeStruct((block, width), BF16),
            jax.ShapeDtypeStruct((8, width), F32),
        ],
        in_specs=[vmem()] * 6,
        out_specs=[vmem()] * 2,
        cost_estimate=cost(3.6),
        compiler_params=limit(14),
        name="tokens_back",
    )(*parts, x, grad_mid, mod)


def first_grad_kernel(tile_ref, g0_ref, g1_ref, g2_ref, g3_ref, *refs):
    mixed_refs, (attn_ref, qkv_ref, out_ref, cols_ref) = refs[: 4 * PAIRS], refs[4 * PAIRS :]
    block = g0_ref.shape[0]
    wide = qkv_ref.shape[1]
    for tile in range(4):

        @pl.when(tile_ref[0] == tile)
        def _(tile=tile):
            for place, g_ref in enumerate((g0_ref, g1_ref, g2_ref, g3_ref)):
                cols_ref[block * place : block * (place + 1), :] = g_ref[:, COLS * tile : COLS * (tile + 1)]

    for k in range(attn_ref.shape[1] // LANES):
        at = slice(LANES * k, LANES * (k + 1))
        out_ref[at, :wide] = dot_tn(attn_ref[:, at], qkv_ref[...]).astype(BF16)
    for k, m_ref in enumerate(mixed_refs):
        pair, source = k // 4, k % 4
        total = None
        for place in range(4):
            at = block * (place ^ FLIPS[source])
            term = dot(m_ref[:, at : at + block], cols_ref[block * place : block * (place + 1), :])
            total = term if total is None else total + term
        start = pl.multiple_of((tile_ref[0] ^ FLIPS[source]) * COLS + PAIR_COLS * pair, 16)
        out_ref[pl.ds(start, PAIR_COLS), wide:] = total.astype(BF16)


def first_grad(tile, grads, mixed, attn_in, grad_qkv):
    width = attn_in.shape[1]
    return pl.pallas_call(
        first_grad_kernel,
        out_shape=jax.ShapeDtypeStruct((width, grad_qkv.shape[1] + COLS), BF16),
        in_specs=[smem()] + [vmem()] * (6 + 4 * PAIRS),
        out_specs=vmem(),
        scratch_shapes=[pltpu.VMEM((grad_qkv.shape[0], COLS), BF16)],
        compiler_params=limit(24),
        cost_estimate=cost(8),
        name="first_grad",
    )(tile, *grads, *mixed, attn_in, grad_qkv)


def weight_grad_kernel(left_ref, right_ref, out_ref):
    for k in range(left_ref.shape[1] // LANES):
        at = slice(LANES * k, LANES * (k + 1))
        out_ref[at, :] = dot_tn(left_ref[:, at], right_ref[...]).astype(BF16)


def weight_grad(left, right, microseconds):
    return pl.pallas_call(
        weight_grad_kernel,
        out_shape=jax.ShapeDtypeStruct((left.shape[1], right.shape[1]), BF16),
        in_specs=[vmem()] * 2,
        out_specs=vmem(),
        compiler_params=limit(24),
        cost_estimate=cost(microseconds),
        name="weight_grad",
    )(left, right)


GU_AFTER = 4
TO_TX = (1, 0, 2, 1)
TO_TY = (2, 2, 0, 0)
KEPT = (0, 1, 1, 2)
SLOTS = ((0, 1, 2), (2, 1, 0), (0, 1, 2), (2, 1, 0))


def pack_kernel(shard, ff_own, tile_ref, a_ref, b_ref, sgu_ref, tx_ref, ty_ref, gu_ref, down_ref, unit_ref, out_ref):
    cut = a_ref.shape[0]
    share = sgu_ref.shape[1] // 4

    def rows(first, last, lanes):
        pieces = []
        if first < cut:
            pieces.append(a_ref[first : min(last, cut), lanes])
        if last > cut:
            pieces.append(b_ref[max(first, cut) - cut : last - cut, lanes])
        return pieces[0] if len(pieces) == 1 else jnp.concatenate(pieces)

    def gu(tile):
        return sgu_ref[:, share * tile : share * (tile + 1)]

    def down(tile):
        return rows(shard, shard + ff_own, slice(COLS * tile, COLS * (tile + 1)))

    def unit(part):
        return rows(0, shard, slice(COLS * part, COLS * (part + 1)))

    out_ref[...] = unit(3)
    for tile in range(4):

        @pl.when(tile_ref[0] == tile)
        def _(tile=tile):
            at = 0
            for ref, pieces in (
                (tx_ref, (gu(tile ^ 1), gu(tile ^ 3), down(tile ^ 1), down(tile ^ 3), unit(TO_TX[tile]))),
                (ty_ref, (gu(tile ^ 2), down(tile ^ 2), unit(TO_TY[tile]))),
            ):
                at = 0
                for piece in pieces:
                    ref[at : at + piece.shape[0], : piece.shape[1]] = piece.astype(BF16)
                    at += piece.shape[0]
            gu_ref[...] = gu(tile).astype(F32)
            down_ref[...] = down(tile)
            unit_ref[...] = unit(KEPT[tile])


def pack(tile, sums, sum_gu, shard, ff_own):
    share = sum_gu.shape[1] // 4
    both = 3 * shard + 2 * ff_own
    one = 2 * shard + ff_own
    return pl.pallas_call(
        functools.partial(pack_kernel, shard, ff_own),
        out_shape=[
            jax.ShapeDtypeStruct((both, share), BF16),
            jax.ShapeDtypeStruct((one, share), BF16),
            jax.ShapeDtypeStruct((shard, share), F32),
            jax.ShapeDtypeStruct((ff_own, COLS), F32),
            jax.ShapeDtypeStruct((shard, COLS), F32),
            jax.ShapeDtypeStruct((shard, COLS), F32),
        ],
        in_specs=[smem()] + [vmem()] * 3,
        out_specs=[vmem()] * 6,
        compiler_params=limit(12),
        cost_estimate=cost(2),
        name="pack",
    )(tile, *sums, sum_gu)


def unpack_kernel(shard, ff_own, tile_ref, tx_ref, ty_ref, gu_ref, down_ref, unit_ref, wgu_ref, wdown_ref, wqkv_ref):
    one = 2 * shard + ff_own
    share = gu_ref.shape[1]
    groups = share // ff_own
    gus = [
        gu_ref[...],
        tx_ref[0:shard, :].astype(F32),
        ty_ref[0:shard, :].astype(F32),
        ty_ref[one : one + shard, :].astype(F32),
    ]
    downs = [
        down_ref[...],
        tx_ref[2 * shard : 2 * shard + ff_own, :COLS].astype(F32),
        ty_ref[shard : shard + ff_own, :COLS].astype(F32),
        ty_ref[one + shard : one + shard + ff_own, :COLS].astype(F32),
    ]
    units = [
        unit_ref[...],
        tx_ref[2 * shard + 2 * ff_own :, :COLS].astype(F32),
        ty_ref[shard + ff_own : one, :COLS].astype(F32),
    ]
    for tile in range(4):

        @pl.when(tile_ref[0] == tile)
        def _(tile=tile):
            for source in range(4):
                flip = source ^ tile
                wdown_ref[ff_own * source : ff_own * (source + 1), :] = downs[flip]
                for group in range(groups):
                    at = share * group + ff_own * source
                    wgu_ref[:, at : at + ff_own] = gus[flip][:, ff_own * group : ff_own * (group + 1)]
            for k in range(3):
                wqkv_ref[:, COLS * k : COLS * (k + 1)] = units[SLOTS[tile][k]]


def unpack(tile, from_tx, from_ty, kept, shard, ff_own):
    share = kept[0].shape[1]
    return pl.pallas_call(
        functools.partial(unpack_kernel, shard, ff_own),
        out_shape=[
            jax.ShapeDtypeStruct((shard, 4 * share), F32),
            jax.ShapeDtypeStruct((4 * ff_own, COLS), F32),
            jax.ShapeDtypeStruct((shard, 3 * COLS), F32),
        ],
        in_specs=[smem()] + [vmem()] * 5,
        out_specs=[vmem()] * 3,
        compiler_params=limit(12),
        cost_estimate=cost(2),
        name="unpack",
    )(tile, from_tx, from_ty, *kept)


def ada_kernel(tile_ref, mod_ref, w_ref, silu_ref, ada_ref, bias_ref, cond_ref):
    count, wide = mod_ref.shape
    width = w_ref.shape[1]
    share = width // 4
    for tile in range(4):

        @pl.when(tile_ref[0] == tile)
        def _(tile=tile):
            ada_ref[...] = dot_tn(silu_ref[...], mod_ref[:, share * tile : share * (tile + 1)])

    rows = [mod_ref[k : k + 1, :].astype(F32) for k in range(count)]
    while len(rows) > 1:
        rows = [rows[k] + rows[k + 1] for k in range(0, len(rows), 2)]
    bias_ref[...] = rows[0]
    cond_ref[...] = dot_nt(mod_ref[:, :width], w_ref[...])


def ada_back(tile, mod_all, w_ada, silu_rows):
    count, wide = mod_all.shape
    shard, width = w_ada.shape
    return pl.pallas_call(
        ada_kernel,
        out_shape=[
            jax.ShapeDtypeStruct((shard, width // 4), F32),
            jax.ShapeDtypeStruct((1, wide), F32),
            jax.ShapeDtypeStruct((count, shard), F32),
        ],
        in_specs=[smem()] + [vmem()] * 3,
        out_specs=[vmem()] * 3,
        cost_estimate=cost(3.5),
        compiler_params=limit(12),
        name="ada_back",
    )(tile, mod_all, w_ada, silu_rows)


def reorder_kernel(index_ref, rows_ref, out_ref):
    for k in range(rows_ref.shape[0]):
        out_ref[k : k + 1, :] = rows_ref[pl.ds(index_ref[k], 1), :]


def reorder(index, rows):
    return pl.pallas_call(
        reorder_kernel,
        out_shape=jax.ShapeDtypeStruct(rows.shape, rows.dtype),
        in_specs=[smem(), vmem()],
        out_specs=vmem(),
        cost_estimate=cost(1.3),
        compiler_params=limit(4),
        name="reorder",
    )(index, rows)


def lane_matrix():
    matrix = np.zeros((HEAD, LANES), np.float32)
    for index in range(HEAD):
        matrix[index, head_lane(index)] = 1.0
    return matrix


def rope_lanes(tile_rows, tile_cols):
    freqs = (10000.0 ** (-np.arange(QUARTER, dtype=np.float64) / QUARTER)).astype(np.float32)
    freq = np.zeros((LANES,), np.float32)
    part = np.zeros((LANES,), np.int32)
    sign = np.zeros((LANES,), np.float32)
    for index in range(HEAD):
        lane = head_lane(index)
        freq[lane] = freqs[index % QUARTER]
        part[lane] = index // 36
        sign[lane] = 1.0 if lane >= 64 else -1.0
    per_tile = tile_rows * tile_cols
    ids = np.arange(4 * per_tile)
    flips = np.array(FLIPS)[ids // per_tile]
    ty = lax.axis_index("ty") ^ jnp.asarray(flips >> 1, jnp.int32)
    tx = lax.axis_index("tx") ^ jnp.asarray(flips & 1, jnp.int32)
    rows = (ty * tile_rows + jnp.asarray(ids % per_tile // tile_cols, jnp.int32)).astype(F32)
    cols = (tx * tile_cols + jnp.asarray(ids % tile_cols, jnp.int32)).astype(F32)
    angle = jnp.where(jnp.asarray(part)[None] == 0, rows[:, None], cols[:, None]) * jnp.asarray(freq)[None]
    live = jnp.asarray((sign != 0).astype(np.float32))[None]
    return jnp.cos(angle) * live, jnp.sin(angle) * jnp.asarray(sign)[None]


def gain_lanes(gain):
    return jnp.sum(jnp.asarray(lane_matrix()) * gain[:, None], axis=0, keepdims=True)


def gain_back(lanes):
    return jnp.sum(jnp.asarray(lane_matrix()) * lanes[None, :], axis=1)


def tile_pair(far):
    return (far[0].astype(F32) + swap(far[1], "tx").astype(F32)).astype(BF16)


def tile_sum_parts(pair, near):
    return near[0], swap(near[1], "tx"), swap(pair, "ty")


def body(
    count, tokens, cond, live_count, w_qkv, w_out, w_gu, w_down, w_ada, ada_bias, q_gain, k_gain, cotangent
):
    _, tile_rows, tile_cols, width = tokens.shape
    per_tile = tile_rows * tile_cols
    img, ty, tx = lax.axis_index("img"), lax.axis_index("ty"), lax.axis_index("tx")
    tile = ty * 2 + tx
    tile_word = tile[None].astype(jnp.int32)
    live = (live_count[0] > 0).astype(F32)
    shard = width // count
    ff_shard = FF // count
    ff_own = ff_shard // TILES
    hidden_own = FF // TILES
    out_width = width // TILES
    spread = jnp.asarray(spread_matrices(), BF16)

    first = jnp.concatenate(
        [lax.dynamic_slice_in_dim(w_qkv, p * width + tile * COLS, COLS, 1) for p in range(3)]
        + [lax.dynamic_slice_in_dim(w_out, tile * out_width, out_width, 1)],
        axis=1,
    )
    down_own = lax.dynamic_slice_in_dim(w_down, tile * ff_own, ff_own, 0)
    gu_own = lax.dynamic_slice_in_dim(w_gu.reshape(shard, 2 * count, ff_shard), tile * ff_own, ff_own, 2)
    gu_own = gu_own.reshape(shard, 2 * hidden_own)

    x_own = tokens.reshape(per_tile, width)
    dy_own = cotangent.reshape(per_tile, width)
    x_tiles = gather_tiles(x_own)
    dy_tiles = gather_tiles(dy_own)

    cond_float = cond.astype(F32)
    bits = [1 << k for k in range(count.bit_length() - 1)]
    store = {}

    def gather_step(v, bit):
        return jnp.concatenate([v, lax.ppermute(v, "img", flip_perm(count, bit))])

    def scatter_step(v, bit):
        return v[:bit] + lax.ppermute(v[bit:], "img", flip_perm(count, bit))

    silu_some = jax.nn.silu(cond_float).astype(BF16)
    for bit in bits[:-1]:
        silu_some = gather_step(silu_some, bit)

    def rows_step(_):
        store["silu_rows"] = lax.dynamic_slice_in_dim(gather_step(silu_some, bits[-1]), img * shard, shard, 1)
        return store["silu_rows"]

    beside = [rows_step, lambda v: scatter_step(dot(v, w_ada), bits[-1])]
    beside += [lambda v, bit=bit: scatter_step(v, bit) for bit in bits[-2::-1]]
    early, late = beside[1], beside[2]
    beside[1] = lambda v: after(early(v), x_tiles[0])
    beside[2] = lambda v: after(late(v), dy_tiles[0], x_tiles)

    ring = use_ring(count, math.gcd(shard, ff_own))
    if ring:
        own = after(jnp.concatenate([first, down_own]), silu_some)
        pieces, modulation = ring_gather(own, count, beside)
        full_first, full_down, out_own = assemble(
            own,
            pieces,
            [(width, width), (hidden_own, width), (COLS, width)],
            [(0, shard, 0, shard, 0, 0, 0, width), (1, ff_own, shard, ff_own, 0, 0, 0, width)],
            count,
            True,
        )
        full_gu = lax.all_gather(after(gu_own, pieces[GU_AFTER]), "img", axis=0, tiled=True)
    else:
        full_first, full_down, full_gu = [
            lax.all_gather(a, "img", axis=0, tiled=True) for a in (first, down_own, gu_own)
        ]
        out_own = out_share(out_pick(), full_first)
        modulation = None
        for step in beside:
            modulation = step(modulation)
    silu_rows = store["silu_rows"]
    modulation = modulation + ada_bias
    mod = jnp.concatenate([modulation.reshape(6, width), jnp.broadcast_to(live, (2, width))])

    cos, sin = rope_lanes(tile_rows, tile_cols)
    gq, gk = gain_lanes(q_gain), gain_lanes(k_gain)
    attn_in, qraw, kraw, q0, q1, k0, k1, v0, v1 = project(
        x_tiles, mod, full_first, cos, sin, gq, gk, spread
    )
    out_far = swap(out_own, "ty")
    out_far = after(out_far, attn_in)
    full_out, out_rows = out_weight(
        tile_word, [out_far, swap(out_far, "tx"), out_own, swap(out_own, "tx")]
    )
    q0, mixedp0, mixed0 = attend(q0, k0, v0, spread)
    mixed = gather_tiles(mixed0)
    q1, mixedp1, mixed1 = attend(after(q1, full_out, mixed0), k1, v1, spread)
    mixed += gather_tiles(mixed1)

    weights = (tile_word, mod, full_out, full_gu, full_down, x_tiles, dy_tiles, mixed)
    far = mlp((0, 1), *weights, ())
    grad_pair = tile_pair(far[6:8])
    cut = per_tile // 2
    part_0, part_1 = swap(grad_pair[:cut], "ty"), swap(grad_pair[cut:], "ty")
    beside_tile = mlp((3,), *weights, after(far[:4], grad_pair))
    own_tile = mlp((2,), *weights, after(beside_tile[:4], part_0))
    mlp_in, hidden, grad_gu, grad_branch = own_tile[:4]
    attended = own_tile[6]

    grad_att, grad_mid, mid_sums = middle(
        (own_tile[5], swap(beside_tile[5], "tx"), part_0, part_1), attended, x_own, dy_own, mod
    )
    g_gu = weight_grad(mlp_in, after(grad_gu, grad_att), 5)
    g_down = weight_grad(hidden, after(grad_branch, g_gu), 3)
    att_far = after(swap(grad_att, "ty"), g_gu, g_down)
    grad_att_tiles = [att_far, swap(att_far, "tx"), grad_att, swap(grad_att, "tx")]

    grad_qkv, gains = attention_backward(
        grad_att_tiles, out_rows, qraw, kraw, (q0, q1), (k0, k1), (v0, v1), (mixedp0, mixedp1),
        cos, sin, gq, gk, spread,
    )
    branch_parts = tile_sum_parts(tile_pair(far[4:6]), (own_tile[4], beside_tile[4]))
    output, out_sums = output_tile(after(branch_parts, grad_qkv), attended, x_own, dy_own, mod)
    w_back = full_first[:, : 3 * COLS]
    back_far = dot_nt(grad_qkv[: 2 * per_tile], w_back).astype(BF16)
    halves = lambda rows: (rows[:per_tile], rows[per_tile:])
    back_pair = tile_pair(halves(back_far))
    late_qkv = after(grad_qkv, back_pair)
    back_near = dot_nt(late_qkv[2 * per_tile :], w_back).astype(BF16)
    g_first = first_grad(tile_word, grad_att_tiles, mixed, attn_in, late_qkv)

    wide = 6 * width

    def token_step():
        parts = tile_sum_parts(back_pair, halves(back_near))
        store["grad_tokens"], tok_sums = tokens_back(parts, x_own, grad_mid, mod)
        return jnp.concatenate(
            [tok_sums[0], tok_sums[1], mid_sums[0], mid_sums[1], mid_sums[2], out_sums[0], gains[0], gains[1]]
        )[None]

    def low_step(grad_mod):
        return jnp.concatenate([grad_mod[:, :wide].astype(BF16), *three_parts(grad_mod[:, wide:])], axis=1)

    def ada_step(mod_all):
        store["grad_ada"], store["sums"], grad_silu = ada_back(tile_word, mod_all, w_ada, silu_rows)
        return grad_silu

    steps = [None, lambda _: token_step(), lambda v: low_step(sum_tiles(v))]
    steps += [lambda v, bit=bit: gather_step(v, bit) for bit in bits]
    steps.append(lambda v: flip_exchange(ada_step(v), count, bits[-1:]))
    steps.append(lambda v: flip_exchange(v, count, bits[-2::-1]))

    if ring:
        s_gu = lax.psum_scatter(g_gu, "img", scatter_dimension=0, tiled=True)
        s_all, grad_silu = ring_scatter([g_first, g_down], count, steps)
    else:
        grad_silu = None
        for step in steps:
            grad_silu = step(grad_silu) if step else None
    grad_tokens, grad_ada, sums = store["grad_tokens"], store["grad_ada"], store["sums"]
    grad_bias = sums[0, :wide]
    gain_sums = (sums[:, wide : wide + 256] + sums[:, wide + 256 : wide + 512]) + sums[:, wide + 512 :]
    flips = (jnp.arange(count, dtype=jnp.int32) ^ img).astype(jnp.int32)
    grad_silu = reorder(flips, grad_silu).reshape(1, width)
    sigmoid_c = jax.nn.sigmoid(cond_float)
    grad_cond = (grad_silu * sigmoid_c * (1.0 + cond_float * (1.0 - sigmoid_c))).astype(BF16)
    if ring:
        to_tx, to_ty, *kept, grad_w_out = pack(tile_word, s_all, s_gu, shard, ff_own)
        from_tx = swap(to_tx, "tx")
        to_ty = jnp.concatenate(
            [to_ty, from_tx[shard : 2 * shard], from_tx[2 * shard + ff_own : 2 * shard + 2 * ff_own]]
        )
        grad_w_gu, grad_down, grad_w_qkv = unpack(tile_word, from_tx, swap(to_ty, "ty"), kept, shard, ff_own)
    else:
        sums_of = lambda grad: lax.psum_scatter(grad, "img", scatter_dimension=0, tiled=True)
        s_first, s_down, s_gu = sums_of(g_first).astype(F32), sums_of(g_down), sums_of(g_gu)
        gu_cols = 2 * hidden_own // TILES
        got = exchange_tiles(lambda t: lax.dynamic_slice_in_dim(s_gu, t * gu_cols, gu_cols, 1))
        grad_w_out = s_first[:, 3 * COLS :].astype(F32)
        s_qkv = s_first.astype(BF16)

        grad_down = jnp.concatenate(
            exchange_tiles(lambda t: lax.dynamic_slice_in_dim(s_down, t * out_width, out_width, 1))
        ).astype(F32)
        grad_w_gu = jnp.concatenate(
            [got[s][:, ff_own * g : ff_own * (g + 1)] for g in range(gu_cols // ff_own) for s in range(4)],
            axis=1,
        ).astype(F32)
        units = [s_qkv[:, COLS * p : COLS * (p + 1)] for p in range(3)]

        def choose(options, table):
            result = options[table[0]]
            for t in range(1, 4):
                if table[t] != table[0]:
                    result = jnp.where(tile == t, options[table[t]], result)
            return result

        slots = [
            choose(units, KEPT),
            swap(choose(units, TO_TX), "tx"),
            swap(choose(units, TO_TY), "ty"),
        ]
        grad_w_qkv = jnp.concatenate(
            [choose(slots, [SLOTS[t][k] for t in range(4)]) for k in range(3)], axis=1
        ).astype(F32)

    return (
        output.reshape(tokens.shape),
        grad_tokens.reshape(tokens.shape),
        grad_cond,
        grad_w_qkv,
        grad_w_out,
        grad_w_gu,
        grad_down,
        grad_ada,
        gain_back(gain_sums[0, :LANES]),
        gain_back(gain_sums[0, LANES:]),
        grad_bias,
    )


def solution(mesh):
    tiled = P("img", "ty", "tx", None)
    rows = P("img", None)
    cut = P("img", ("ty", "tx"))
    in_specs = (tiled, rows, P("img"), rows, rows, rows, rows, rows, P(), P(), P(), tiled)
    out_specs = (tiled, tiled, rows, cut, cut, cut, cut, cut, P(), P(), P())
    return jax.shard_map(
        functools.partial(body, mesh.shape["img"]),
        mesh=mesh,
        in_specs=in_specs,
        out_specs=out_specs,
        check_vma=False,
    )
```

time: 653 us -> 402 us (0.62)
  other arithmetic: 85.4 us -> 10.4 us
  starting transfers between devices: 147 us -> 76.2 us
  local copies, waits for them, and re-layouts: 105 us -> 53.7 us
  Pallas kernels: 64.5 us -> 113 us
  matrix products: 51.8 us -> 4.78 us
  between operations: 46.1 us -> 16.6 us
  waiting for transfers between devices: 143 us -> 120 us
    ppermute x115 -> x40, starting transfers between devices: 128 us -> 59.8 us  [the longest x14 25.2 us: ring_scatter(): lax.ppermute(sums[k], 'img', ring_perm(count, sign))]
    pallas_call x4 -> x18, Pallas kernels: 33.3 us -> 80.1 us  [the longest x3 28.6 us: mlp(): pl.pallas_call(functools.partial(mlp_kernel, places), grid=(1,), out_shap...]
    unnamed x208 -> x247, local copies, waits for them, and re-layouts: 16.3 us -> 48.1 us
    ppermute x115 -> x40, waiting for transfers between devices: 112 us -> 84.4 us  [the longest x14 41.4 us: ring_scatter(): lax.ppermute(sums[k], 'img', ring_perm(count, sign))]
    convert_element_type x52 -> x18, other arithmetic: 32.1 us -> 5.7 us  [the longest x3 3.42 us: tile_pair(): return (far[0].astype(F32) + swap(far[1], 'tx').astype(F32)).astype(BF16)]
    slice x37 -> x21, local copies, waits for them, and re-layouts: 26.6 us -> 1.16 us  [the longest x1 0.68 us: body(): grad_bias = sums[0, :wide]]
    dot_general x5 -> x0, matrix products: 16.8 us -> none  [dot_tn(): lax.dot_general(left, right, (((0,), (0,)), ((), ())), preferred_element_...]
    dynamic_slice x20 -> x4, local copies, waits for them, and re-layouts: 16.3 us -> 0.24 us  [the longest x3 0.22 us: part(): lax.dynamic_slice_in_dim(grad, owner * rows + low - base, high - low, 0)]
  transfers between devices with their start and end apart: 142 -> 74, of which waited for: 57 -> 35; matrix products, arithmetic and copies ran while one was open for 27% -> 5% of each run, Pallas kernels for 5% -> 25%
where the time goes in v2:
time: 402 us; the launch traced here: 395 us
  waiting for transfers between devices  120 us (30%)
  Pallas kernels  113 us (28%)
  starting transfers between devices  76.2 us (19%)
  local copies, waits for them, and re-layouts  53.7 us (13%)
  between operations  16.6 us (4%)
  other arithmetic  10.4 us (3%)
  matrix products  4.78 us (1%)
    unnamed x247, local copies, waits for them, and re-layouts  48.1 us
    ppermute x14, waiting for transfers between devices, ring_scatter(): lax.ppermute(sums[k], 'img', ring_perm(count, sign))  41.4 us
    ppermute x32, waiting for transfers between devices, swap(): return lax.ppermute(values, axis, [(0, 1), (1, 0)])  35.9 us
    pallas_call x1, Pallas kernels, attention_backward(): pl.pallas_call(attention_back_kernel, out_shape=[jax.ShapeDtypeStruct((to...  32.9 us
    pallas_call x3, Pallas kernels, mlp(): pl.pallas_call(functools.partial(mlp_kernel, places), grid=(1,), out_shap...  28.6 us
    ppermute x14, starting transfers between devices, ring_scatter(): lax.ppermute(sums[k], 'img', ring_perm(count, sign))  25.2 us
    ppermute x7, waiting for transfers between devices, ring_gather(): b = lax.ppermute(b, 'img', ring_perm(count, -1))  23.5 us
    ppermute x32, starting transfers between devices, swap(): return lax.ppermute(values, axis, [(0, 1), (1, 0)])  16.4 us
  transfers between devices with their start and end apart: 74, of which 35 were waited for; matrix products, arithmetic and copies ran while one was open for 5% of the time, Pallas kernels for 25%

profile of v2, /device:TPU:0, one launch (start us, length us, event | category | flops | bytes accessed | tf_op | source)
XLA Modules:
  0.0 395.1 jit_solution(9585973811180748014)
XLA Ops:
  22.2 4.5 %collective-permute-done.4 = bf16[4,1152]{1,0:T(4,128)(2,1)S(1)} collective-permute-done((bf16[4,1152]{1,0:T(4,128)(2,1)S(1)}, bf16[4,1152]{1,0:T(4,128)(2,1)S(1)}, u32[]{:S(2)}, u32[]{:S(2)}) %collective-permute-start.4) | collective-permute-done | bytes 9248 | tf_op jit(solution)/shard_map/ppermute | solution.py:1016
  36.0 5.1 %collective-permute-done.8.x0_ref.refs_0_ = bf16[256,1152]{1,0:T(8,128)(2,1)S(1)} collective-permute-done((bf16[256,1152]{1,0:T(8,128)(2,1)S(1)}, bf16[256,1152]{1,0:T(8,128)(2,1)S(1)}, u32[]{:S(2)}, u32[]{:S(2)}) %collective-permute-start.8) | collective-permute-done | bytes 589856 | tf_op jit(solution)/shard_map/ppermute | solution.py:66
  47.6 10.5 %collective-permute-done.12.refs_2_ = bf16[256,1152]{1,0:T(8,128)(2,1)S(1)} collective-permute-done((bf16[256,1152]{1,0:T(8,128)(2,1)}, bf16[256,1152]{1,0:T(8,128)(2,1)S(1)}, u32[]{:S(2)}, u32[]{:S(2)}) %collective-permute-start.12) | collective-permute-done | bytes 589856 | tf_op jit(solution)/shard_map/ppermute | solution.py:66
  64.1 4.6 %collective-permute-done.16.refs_11_ = bf16[112,1152]{1,0:T(8,128)(2,1)} collective-permute-done((bf16[112,1152]{1,0:T(8,128)(2,1)S(1)}, bf16[112,1152]{1,0:T(8,128)(2,1)}, u32[]{:S(2)}, u32[]{:S(2)}) %collective-permute-start.16) | collective-permute-done | bytes 258080 | tf_op jit(solution)/shard_map/ppermute | solution.py:152
  88.2 12.6 %collective-permute-done.23.refs_14_ = bf16[112,1152]{1,0:T(8,128)(2,1)} collective-permute-done((bf16[112,1152]{1,0:T(8,128)(2,1)}, bf16[112,1152]{1,0:T(8,128)(2,1)}, u32[]{:S(2)}, u32[]{:S(2)}) %collective-permute-start.23) | collective-permute-done | bytes 258080 | tf_op jit(solution)/shard_map/ppermute | solution.py:152
  100.8 6.0 %assemble_first.1 = (bf16[1152,1152]{1,0:T(8,128)(2,1)}, bf16[768,1152]{1,0:T(8,128)(2,1)}, bf16[288,1152]{1,0:T(8,128)(2,1)}) custom-call(s32[15]{0:T(128)} %compare_select_fusion.2.index_ref, bf16[288,384]{1,0:T(8,128)(2,1)} %constant.269.clone.pick_ref, bf16[240,1152]{1,0:T(8,128)(2,1)} %copy-done.95, bf16[128,1152]{1,0:T(8,128)(2,1)} %copy-done.113, ...), custom_call_target="tpu_custom_call" | custom-call | flops 5500000256 | bytes 15000000 | tf_op jit(solution)/shard_map/assemble_first/pallas_call | solution.py:195
  112.1 9.5 %project.1 = (bf16[1024,1152]{1,0:T(8,128)(2,1)S(1)}, f32[1024,512]{1,0:T(8,128)S(1)}, f32[1024,512]{1,0:T(8,128)S(1)}, bf16[1024,256]{1,0:T(8,128)(2,1)S(1)}, b...) custom-call(bf16[256,1152]{1,0:T(8,128)(2,1)S(1)} %copy-done.21, ...), custom_call_target="tpu_custom_call" | custom-call | flops 17600000000 | bytes 48000000 | tf_op jit(solution)/shard_map/project/pallas_call | solution.py:345
  122.4 4.1 %attend.2 = (bf16[1024,256]{1,0:T(8,128)(2,1)S(1)}, bf16[1024,256]{1,0:T(8,128)(2,1)S(1)}, bf16[144,1024]{1,0:T(8,128)(2,1)S(1)}) custom-call(bf16[1024,256]{1,0:T(8,128)(2,1)S(1)} %get-tuple-element.146.qin_ref, bf16[1024,256]{1,0:T(8,128)(2,1)S(1)} %get-tuple-element.147.k_ref.k0_ref, bf16[1024,256]{1,0:T(8,128)(2,1)S(1)} %get-tuple-element.148.v_ref.v0_ref, ...), custom_call_target="tpu_custom_call" | custom-call | flops 4510000128 | bytes 12299999 | tf_op jit(solution)/shard_map/attend/pallas_call | solution.py:382
  130.0 4.7 %attend.3 = (bf16[1024,256]{1,0:T(8,128)(2,1)S(1)}, bf16[1024,256]{1,0:T(8,128)(2,1)S(1)}, bf16[144,1024]{1,0:T(8,128)(2,1)S(1)}) custom-call(bf16[1024,256]{1,0:T(8,128)(2,1)S(1)} %get-tuple-element.151.qin_ref, bf16[1024,256]{1,0:T(8,128)(2,1)S(1)} %get-tuple-element.152.k_ref.k1_ref, bf16[1024,256]{1,0:T(8,128)(2,1)S(1)} %get-tuple-element.153.v_ref.v1_ref, ...), custom_call_target="tpu_custom_call" | custom-call | flops 4510000128 | bytes 12299999 | tf_op jit(solution)/shard_map/attend/pallas_call | solution.py:382
  140.0 5.7 %collective-permute-done.30.refs_8_.refs_6_.refs_4_ = bf16[144,1024]{1,0:T(8,128)(2,1)S(1)} collective-permute-done((bf16[144,1024]{1,0:T(8,128)(2,1)S(1)}, bf16[144,1024]{1,0:T(8,128)(2,1)S(1)}, u32[]{:S(2)}, u32[]{:S(2)}) %collective-permute-start.30) | collective-permute-done | bytes 294944 | tf_op jit(solution)/shard_map/ppermute | solution.py:66
  161.1 13.3 %mlp.3 = (bf16[1024,1152]{1,0:T(8,128)(2,1)}, bf16[1024,768]{1,0:T(8,128)(2,1)S(1)}, bf16[1024,1536]{1,0:T(8,128)(2,1)}, bf16[1024,1152]{1,0:T(8,128)(2,1)}, bf1...) custom-call(s32[1]{0:T(128)} %bitcast.tile_ref, ...), custom_call_target="tpu_custom_call" | custom-call | flops 15399999488 | bytes 42000000 | tf_op jit(solution)/shard_map/mlp/pallas_call | solution.py:596
  184.7 7.8 %mlp.4 = (bf16[1024,1152]{1,0:T(8,128)(2,1)}, bf16[1024,768]{1,0:T(8,128)(2,1)S(1)}, bf16[1024,1536]{1,0:T(8,128)(2,1)}, bf16[1024,1152]{1,0:T(8,128)(2,1)}, bf1...) custom-call(s32[1]{0:T(128)} %bitcast.tile_ref, ...), custom_call_target="tpu_custom_call", output_to_operand_aliasing={{0}: (15, {}), {1}: (16, {}), {2}: (17, {}), {3}: (18, {})} | custom-call | flops 7699999744 | bytes 21000000 | tf_op jit(solution)/shard_map/mlp/pallas_call | solution.py:596
  195.8 7.5 %mlp.5 = (bf16[1024,1152]{1,0:T(8,128)(2,1)}, bf16[1024,768]{1,0:T(8,128)(2,1)S(1)}, bf16[1024,1536]{1,0:T(8,128)(2,1)}, bf16[1024,1152]{1,0:T(8,128)(2,1)}, bf1...) custom-call(s32[1]{0:T(128)} %bitcast.tile_ref, ...), custom_call_target="tpu_custom_call", output_to_operand_aliasing={{0}: (15, {}), {1}: (16, {}), {2}: (17, {}), {3}: (18, {})} | custom-call | flops 7699999744 | bytes 21000000 | tf_op jit(solution)/shard_map/mlp/pallas_call | solution.py:596
  205.3 3.8 middle.1
  211.6 5.7 %weight_grad.2 = bf16[1152,1536]{1,0:T(8,128)(2,1)} custom-call(bf16[1024,1152]{1,0:T(8,128)(2,1)S(1)} %copy-done.67, bf16[1024,1536]{1,0:T(8,128)(2,1)S(1)} %copy-done.65), custom_call_target="tpu_custom_call" | custom-call | flops 5500000256 | bytes 15000000 | tf_op jit(solution)/shard_map/weight_grad/pallas_call | solution.py:752
  229.7 32.9 %attention_backward.1 = (bf16[1024,864]{1,0:T(8,128)(2,1)}, f32[8,128]{1,0:T(8,128)}) custom-call(bf16[256,1152]{1,0:T(8,128)(2,1)} %collective-permute-done.42.g0_ref, bf16[256,1152]{1,0:T(8,128)(2,1)} %collective-permute-done.43.g1_ref, bf16[256,1152]{1,0:T(8,128)(2,1)} %get-tuple-element.180.g2_ref, bf16[256,1152]{1,0:T(8,128)(2,1)} %collective-permute-done.44.g3_ref, ...), custom_call_target="tpu_custom_call" | custom-call | flops 35200000000 | bytes 96000000 | tf_op jit(solution)/shard_map/attention_backward/pallas_call | solution.py:479
  272.6 5.7 %first_grad.1 = bf16[1152,1152]{1,0:T(8,128)(2,1)S(1)} custom-call(s32[1]{0:T(128)} %bitcast.tile_ref, bf16[256,1152]{1,0:T(8,128)(2,1)} %collective-permute-done.42.g0_ref, bf16[256,1152]{1,0:T(8,128)(2,1)} %collective-permute-done.43.g1_ref, bf16[256,1152]{1,0:T(8,128)(2,1)} %get-tuple-element.180.g2_ref, ...), custom_call_target="tpu_custom_call" | custom-call | flops 8800000000 | bytes 24000000 | tf_op jit(solution)/shard_map/first_grad/pallas_call | solution.py:733
  282.1 5.7 %collective-permute-done.50 = bf16[112,1152]{1,0:T(8,128)(2,1)S(1)} collective-permute-done((bf16[112,1152]{1,0:T(8,128)(2,1)S(1)}, bf16[112,1152]{1,0:T(8,128)(2,1)S(1)}, u32[]{:S(2)}, u32[]{:S(2)}) %collective-permute-start.50) | collective-permute-done | bytes 258080 | tf_op jit(solution)/shard_map/ppermute | solution.py:238
  295.0 6.6 %collective-permute-done.51 = bf16[112,1152]{1,0:T(8,128)(2,1)S(1)} collective-permute-done((bf16[112,1152]{1,0:T(8,128)(2,1)S(1)}, bf16[112,1152]{1,0:T(8,128)(2,1)S(1)}, u32[]{:S(2)}, u32[]{:S(2)}) %collective-permute-start.51) | collective-permute-done | bytes 258080 | tf_op jit(solution)/shard_map/ppermute | solution.py:238
  304.7 6.7 %collective-permute-start.53 = (bf16[112,1152]{1,0:T(8,128)(2,1)S(1)}, bf16[112,1152]{1,0:T(8,128)(2,1)S(1)}, u32[]{:S(2)}, u32[]{:S(2)}) collective-permute-start(bf16[112,1152]{1,0:T(8,128)(2,1)S(1)} %add_convert_fusion.13), channel_id=1, source_target_pairs={{0,4},{8,0},{16,8},{24,16},{28,24},{20,28},{12,20},{4,12},{1,5},{9... | collective-permute-start | bytes 774152 | tf_op jit(solution)/shard_map/ppermute | solution.py:238
  324.7 4.5 %collective-permute-done.57 = bf16[112,1152]{1,0:T(8,128)(2,1)S(1)} collective-permute-done((bf16[112,1152]{1,0:T(8,128)(2,1)S(1)}, bf16[112,1152]{1,0:T(8,128)(2,1)S(1)}, u32[]{:S(2)}, u32[]{:S(2)}) %collective-permute-start.57) | collective-permute-done | bytes 258080 | tf_op jit(solution)/shard_map/ppermute | solution.py:238
  349.9 3.6 collective-permute-done.63
  361.3 3.6 collective-permute-done.67
  375.6 9.8 %collective-permute-done.71.ty_ref = bf16[624,384]{1,0:T(8,128)(2,1)S(1)} collective-permute-done((bf16[624,384]{1,0:T(8,128)(2,1)S(1)}, bf16[624,384]{1,0:T(8,128)(2,1)S(1)}, u32[]{:S(2)}, u32[]{:S(2)}) %collective-permute-start.71) | collective-permute-done | bytes 479264 | tf_op jit(solution)/shard_map/ppermute | solution.py:66
  (477 shorter events, 193.8 us)
Async XLA Ops:
  7.2 142.9 %all-gather.2.cloned.1.call-start = ((), (), s32[]{:S(2)}) async-start(), calls=%async_computation.1 | async-start | bytes 3981312 | tf_op jit(solution)/shard_map/all_gather | solution.py:1047
  29.2 11.8 %collective-permute-start.8 = (bf16[256,1152]{1,0:T(8,128)(2,1)S(1)}, bf16[256,1152]{1,0:T(8,128)(2,1)S(1)}, u32[]{:S(2)}, u32[]{:S(2)}) collective-permute-start(bf16[256,1152]{1,0:T(8,128)(2,1)S(1)} %bitcast.25), channel_id=1, source_target_pairs={{0,2},{2,0},{1,3},{3,1},{4,6},{6,4},{5,7},{7,5},{8,10},{10,8},{9,1... | collective-permute-start | bytes 1769480 | tf_op jit(solution)/shard_map/ppermute | solution.py:66
  42.1 16.0 %collective-permute-start.12 = (bf16[256,1152]{1,0:T(8,128)(2,1)}, bf16[256,1152]{1,0:T(8,128)(2,1)S(1)}, u32[]{:S(2)}, u32[]{:S(2)}) collective-permute-start(bf16[256,1152]{1,0:T(8,128)(2,1)} %bitcast.2.refs_1_.dy_ref), channel_id=1, source_target_pairs={{0,2},{2,0},{1,3},{3,1},{4,6},{6,4},{5,7},{7,5},{8,10},{10,8},{9,1... | collective-permute-start | bytes 1769480 | tf_op jit(solution)/shard_map/ppermute | solution.py:66
  43.6 14.5 %collective-permute-start.13 = (bf16[256,1152]{1,0:T(8,128)(2,1)S(1)}, bf16[256,1152]{1,0:T(8,128)(2,1)S(1)}, u32[]{:S(2)}, u32[]{:S(2)}) collective-permute-start(bf16[256,1152]{1,0:T(8,128)(2,1)S(1)} %collective-permute-done.8.x0_ref.refs_0_), channel_id=1, source_target_pairs={{0,1},{1,0},{2,3},{3,2},{4,5},{5,4},{6,7},{7,6},{8,9},{9,8},{10,11... | collective-permute-start | bytes 1769480 | tf_op jit(solution)/shard_map/ppermute | solution.py:66
  44.7 15.1 %collective-permute-start.9 = (bf16[128,1152]{1,0:T(8,128)(2,1)S(1)}, bf16[128,1152]{1,0:T(8,128)(2,1)S(1)}, u32[]{:S(2)}, u32[]{:S(2)}) collective-permute-start(bf16[128,1152]{1,0:T(8,128)(2,1)S(1)} %collective-permute-done.5.refs_2_), channel_id=1, source_target_pairs={{0,8},{8,16},{16,24},{24,28},{28,20},{20,12},{12,4},{4,0},{1,9},{9... | collective-permute-start | bytes 884744 | tf_op jit(solution)/shard_map/ppermute | solution.py:151
  45.7 14.0 %collective-permute-start.10 = (bf16[112,1152]{1,0:T(8,128)(2,1)S(1)}, bf16[112,1152]{1,0:T(8,128)(2,1)S(1)}, u32[]{:S(2)}, u32[]{:S(2)}) collective-permute-start(bf16[112,1152]{1,0:T(8,128)(2,1)S(1)} %collective-permute-done.6.refs_9_), channel_id=1, source_target_pairs={{0,4},{8,0},{16,8},{24,16},{28,24},{20,28},{12,20},{4,12},{1,5},{9... | collective-permute-start | bytes 774152 | tf_op jit(solution)/shard_map/ppermute | solution.py:152
  77.3 288.7 %reduce-scatter.2.cloned.1.call-start = ((), (), s32[]{:S(2)}) async-start(), calls=%async_computation.2 | async-start | bytes 3981312 | tf_op jit(solution)/shard_map/reduce_scatter | solution.py:1129
  84.3 16.5 %collective-permute-start.23 = (bf16[112,1152]{1,0:T(8,128)(2,1)}, bf16[112,1152]{1,0:T(8,128)(2,1)}, u32[]{:S(2)}, u32[]{:S(2)}) collective-permute-start(bf16[112,1152]{1,0:T(8,128)(2,1)} %collective-permute-done.22.refs_13_), channel_id=1, source_target_pairs={{0,4},{8,0},{16,8},{24,16},{28,24},{20,28},{12,20},{4,12},{1,5},{9... | collective-permute-start | bytes 774152 | tf_op jit(solution)/shard_map/ppermute | solution.py:152
  85.7 15.2 %collective-permute-start.20 = (bf16[128,1152]{1,0:T(8,128)(2,1)}, bf16[128,1152]{1,0:T(8,128)(2,1)}, u32[]{:S(2)}, u32[]{:S(2)}) collective-permute-start(bf16[128,1152]{1,0:T(8,128)(2,1)} %collective-permute-done.19.refs_6_), channel_id=1, source_target_pairs={{0,8},{8,16},{16,24},{24,28},{28,20},{20,12},{12,4},{4,0},{1,9},{9... | collective-permute-start | bytes 884744 | tf_op jit(solution)/shard_map/ppermute | solution.py:151
  106.9 14.7 %collective-permute-start.24 = (bf16[288,1152]{1,0:T(8,128)(2,1)}, bf16[288,1152]{1,0:T(8,128)(2,1)S(1)}, u32[]{:S(2)}, u32[]{:S(2)}) collective-permute-start(bf16[288,1152]{1,0:T(8,128)(2,1)} %get-tuple-element.139.p2_ref), channel_id=1, source_target_pairs={{0,2},{2,0},{1,3},{3,1},{4,6},{6,4},{5,7},{7,5},{8,10},{10,8},{9,1... | collective-permute-start | bytes 1990664 | tf_op jit(solution)/shard_map/ppermute | solution.py:66
  108.4 18.3 %collective-permute-start.26 = (bf16[288,1152]{1,0:T(8,128)(2,1)}, bf16[288,1152]{1,0:T(8,128)(2,1)S(1)}, u32[]{:S(2)}, u32[]{:S(2)}) collective-permute-start(bf16[288,1152]{1,0:T(8,128)(2,1)} %get-tuple-element.139.p2_ref), channel_id=1, source_target_pairs={{0,1},{1,0},{2,3},{3,2},{4,5},{5,4},{6,7},{7,6},{8,9},{9,8},{10,11... | collective-permute-start | bytes 1990664 | tf_op jit(solution)/shard_map/ppermute | solution.py:66
  122.3 24.1 %collective-permute-start.34 = (bf16[256,1152]{1,0:T(8,128)(2,1)S(1)}, bf16[256,1152]{1,0:T(8,128)(2,1)S(1)}, u32[]{:S(2)}, u32[]{:S(2)}) collective-permute-start(bf16[256,1152]{1,0:T(8,128)(2,1)S(1)} %copy-done.24), channel_id=1, source_target_pairs={{0,1},{1,0},{2,3},{3,2},{4,5},{5,4},{6,7},{7,6},{8,9},{9,8},{10,11... | collective-permute-start | bytes 1769480 | tf_op jit(solution)/shard_map/ppermute | solution.py:66
  177.0 48.9 %collective-permute-start.38 = (bf16[256,1152]{1,0:T(8,128)(2,1)}, bf16[256,1152]{1,0:T(8,128)(2,1)}, u32[]{:S(2)}, u32[]{:S(2)}) collective-permute-start(bf16[256,1152]{1,0:T(8,128)(2,1)} %copy-done.19), channel_id=1, source_target_pairs={{0,1},{1,0},{2,3},{3,2},{4,5},{5,4},{6,7},{7,6},{8,9},{9,8},{10,11... | collective-permute-start | bytes 1769480 | tf_op jit(solution)/shard_map/ppermute | solution.py:66
  180.2 14.1 %collective-permute-start.36 = (bf16[128,1152]{1,0:T(8,128)(2,1)S(1)}, bf16[128,1152]{1,0:T(8,128)(2,1)S(1)}, u32[]{:S(2)}, u32[]{:S(2)}) collective-permute-start(bf16[128,1152]{1,0:T(8,128)(2,1)S(1)} %get-tuple-element.292), channel_id=1, source_target_pairs={{0,2},{2,0},{1,3},{3,1},{4,6},{6,4},{5,7},{7,5},{8,10},{10,8},{9,1... | collective-permute-start | bytes 884744 | tf_op jit(solution)/shard_map/ppermute | solution.py:66
  193.7 11.6 %collective-permute-start.40 = (bf16[256,1152]{1,0:T(8,128)(2,1)S(1)}, bf16[256,1152]{1,0:T(8,128)(2,1)S(1)}, u32[]{:S(2)}, u32[]{:S(2)}) collective-permute-start(bf16[256,1152]{1,0:T(8,128)(2,1)S(1)} %get-tuple-element.178), channel_id=1, source_target_pairs={{0,1},{1,0},{2,3},{3,2},{4,5},{5,4},{6,7},{7,6},{8,9},{9,8},{10,11... | collective-permute-start | bytes 1769480 | tf_op jit(solution)/shard_map/ppermute | solution.py:66
  210.2 15.7 %collective-permute-start.42 = (bf16[256,1152]{1,0:T(8,128)(2,1)}, bf16[256,1152]{1,0:T(8,128)(2,1)}, u32[]{:S(2)}, u32[]{:S(2)}) collective-permute-start(bf16[256,1152]{1,0:T(8,128)(2,1)} %get-tuple-element.180.g2_ref), channel_id=1, source_target_pairs={{0,2},{2,0},{1,3},{3,1},{4,6},{6,4},{5,7},{7,5},{8,10},{10,8},{9,1... | collective-permute-start | bytes 1769480 | tf_op jit(solution)/shard_map/ppermute | solution.py:66
  211.6 18.0 %collective-permute-start.44 = (bf16[256,1152]{1,0:T(8,128)(2,1)}, bf16[256,1152]{1,0:T(8,128)(2,1)}, u32[]{:S(2)}, u32[]{:S(2)}) collective-permute-start(bf16[256,1152]{1,0:T(8,128)(2,1)} %get-tuple-element.180.g2_ref), channel_id=1, source_target_pairs={{0,1},{1,0},{2,3},{3,2},{4,5},{5,4},{6,7},{7,6},{8,9},{9,8},{10,11... | collective-permute-start | bytes 1769480 | tf_op jit(solution)/shard_map/ppermute | solution.py:66
  227.9 38.2 %collective-permute-start.39 = (bf16[256,1152]{1,0:T(8,128)(2,1)}, bf16[256,1152]{1,0:T(8,128)(2,1)S(1)}, u32[]{:S(2)}, u32[]{:S(2)}) collective-permute-start(bf16[256,1152]{1,0:T(8,128)(2,1)} %add_convert_fusion.1), channel_id=1, source_target_pairs={{0,2},{2,0},{1,3},{3,1},{4,6},{6,4},{5,7},{7,5},{8,10},{10,8},{9,1... | collective-permute-start | bytes 1769480 | tf_op jit(solution)/shard_map/ppermute | solution.py:66
  229.4 36.7 %collective-permute-start.37 = (bf16[256,1152]{1,0:T(8,128)(2,1)S(1)}, bf16[256,1152]{1,0:T(8,128)(2,1)}, u32[]{:S(2)}, u32[]{:S(2)}) collective-permute-start(bf16[256,1152]{1,0:T(8,128)(2,1)S(1)} %get-tuple-element.174), channel_id=1, source_target_pairs={{0,1},{1,0},{2,3},{3,2},{4,5},{5,4},{6,7},{7,6},{8,9},{9,8},{10,11... | collective-permute-start | bytes 1769480 | tf_op jit(solution)/shard_map/ppermute | solution.py:66
  270.3 21.5 %collective-permute-start.47 = (bf16[256,1152]{1,0:T(8,128)(2,1)S(1)}, bf16[256,1152]{1,0:T(8,128)(2,1)S(1)}, u32[]{:S(2)}, u32[]{:S(2)}) collective-permute-start(bf16[256,1152]{1,0:T(8,128)(2,1)S(1)} %add_convert_fusion), channel_id=1, source_target_pairs={{0,2},{2,0},{1,3},{3,1},{4,6},{6,4},{5,7},{7,5},{8,10},{10,8},{9,1... | collective-permute-start | bytes 1769480 | tf_op jit(solution)/shard_map/ppermute | solution.py:66
  287.9 13.7 %collective-permute-start.51 = (bf16[112,1152]{1,0:T(8,128)(2,1)S(1)}, bf16[112,1152]{1,0:T(8,128)(2,1)S(1)}, u32[]{:S(2)}, u32[]{:S(2)}) collective-permute-start(bf16[112,1152]{1,0:T(8,128)(2,1)S(1)} %add_convert_fusion.14), channel_id=1, source_target_pairs={{0,4},{8,0},{16,8},{24,16},{28,24},{20,28},{12,20},{4,12},{1,5},{9... | collective-permute-start | bytes 774152 | tf_op jit(solution)/shard_map/ppermute | solution.py:238
  291.4 13.2 %collective-permute-start.49 = (bf16[128,1152]{1,0:T(8,128)(2,1)S(1)}, bf16[128,1152]{1,0:T(8,128)(2,1)S(1)}, u32[]{:S(2)}, u32[]{:S(2)}) collective-permute-start(bf16[128,1152]{1,0:T(8,128)(2,1)S(1)} %add_convert_fusion.8), channel_id=1, source_target_pairs={{0,8},{8,16},{16,24},{24,28},{28,20},{20,12},{12,4},{4,0},{1,9},{9... | collective-permute-start | bytes 884744 | tf_op jit(solution)/shard_map/ppermute | solution.py:238
  304.7 13.4 %collective-permute-start.53 = (bf16[112,1152]{1,0:T(8,128)(2,1)S(1)}, bf16[112,1152]{1,0:T(8,128)(2,1)S(1)}, u32[]{:S(2)}, u32[]{:S(2)}) collective-permute-start(bf16[112,1152]{1,0:T(8,128)(2,1)S(1)} %add_convert_fusion.13), channel_id=1, source_target_pairs={{0,4},{8,0},{16,8},{24,16},{28,24},{20,28},{12,20},{4,12},{1,5},{9... | collective-permute-start | bytes 774152 | tf_op jit(solution)/shard_map/ppermute | solution.py:238
  373.7 11.7 %collective-permute-start.71 = (bf16[624,384]{1,0:T(8,128)(2,1)S(1)}, bf16[624,384]{1,0:T(8,128)(2,1)S(1)}, u32[]{:S(2)}, u32[]{:S(2)}) collective-permute-start(bf16[624,384]{1,0:T(8,128)(2,1)S(1)} %pad_maximum_fusion.1), channel_id=1, source_target_pairs={{0,2},{2,0},{1,3},{3,1},{4,6},{6,4},{5,7},{7,5},{8,10},{10,8},{9,1... | collective-permute-start | bytes 1437704 | tf_op jit(solution)/shard_map/ppermute | solution.py:66
  (169 other events, 1181.1 us)
Sparse Core Ops, SparseCore 0:
  77.4 67.6 all-gather.1
  229.8 85.5 reduce-scatter.1

commit v3 on v2

--- a/solution.py
+++ b/solution.py
@@ -260,6 +260,10 @@
     )
 
 
+def hbm():
+    return pl.BlockSpec(memory_space=pltpu.HBM)
+
+
 def lane_ids(rows):
     return lax.broadcasted_iota(jnp.int32, (rows, LANES), 1)
 
@@ -269,6 +273,22 @@
     rest = column - high.astype(F32)
     mid = rest.astype(BF16)
     return high, mid, (rest - mid.astype(F32)).astype(BF16)
+
+
+def head_sums(values):
+    lanes = values.shape[1]
+    row = lax.broadcasted_iota(jnp.int32, (PAIR, PAIR), 0) // LANES
+    col = lax.broadcasted_iota(jnp.int32, (PAIR, PAIR), 1) // LANES
+    ones = jnp.where(row == col, 1.0, 0.0).astype(BF16)
+    high = values.astype(BF16)
+    rest = (values - high.astype(F32)).astype(BF16)
+    return jnp.concatenate(
+        [
+            dot(high[:, at : at + PAIR], ones) + dot(rest[:, at : at + PAIR], ones)
+            for at in range(0, lanes, PAIR)
+        ],
+        axis=1,
+    )
 
 
 def put_lanes(values, first, parts):
@@ -362,10 +382,8 @@
 def attend_kernel(qin_ref, k_ref, v_ref, spread_ref, q_ref, mixedp_ref, mixed_ref):
     tokens = qin_ref.shape[0]
     block = 256
-
-    @pl.loop(0, tokens // block)
-    def _(i):
-        rows = pl.ds(pl.multiple_of(i * block, block), block)
+    for i in range(tokens // block):
+        rows = slice(block * i, block * (i + 1))
         for head in range(2):
             at = slice(LANES * head, LANES * (head + 1))
             query = qin_ref[rows, at]
@@ -397,7 +415,14 @@
 def attention_back_kernel(
     g0_ref, g1_ref, g2_ref, g3_ref, wout_ref, qraw_ref, kraw_ref, q0_ref, q1_ref, k0_ref, k1_ref, v0_ref, v1_ref,
     m0_ref, m1_ref, cos_ref, sin_ref, gq_ref, gk_ref, spread_ref, out_ref, gains_ref, do_ref, dq_ref, dk_ref, pad_ref,
+    *scratch
 ):
+    sems = scratch[-1]
+    late = (q0_ref, k0_ref, v0_ref, q1_ref, k1_ref, v1_ref, cos_ref, sin_ref, qraw_ref, kraw_ref)
+    copies = [pltpu.make_async_copy(src, dst, sems.at[n]) for n, (src, dst) in enumerate(zip(late, scratch))]
+    for copy in copies:
+        copy.start()
+    q0_ref, k0_ref, v0_ref, q1_ref, k1_ref, v1_ref, cos_ref, sin_ref, qraw_ref, kraw_ref = scratch[:-1]
     block = g0_ref.shape[0]
     tokens = 4 * block
     root = 1.0 / math.sqrt(HEAD)
@@ -406,23 +431,23 @@
         rows = slice(block * place, block * (place + 1))
         grad_mixed = dot(g_ref[...], wout_ref[...]).astype(BF16)
         wide = dot(grad_mixed, spread_ref[3, :COLS, :])
+        mixed = jnp.concatenate([m0_ref[rows, :], m1_ref[rows, :]], axis=1).astype(F32)
+        row_dot = head_sums(wide * mixed)
         for head in range(OWN):
             at = slice(LANES * head, LANES * (head + 1))
-            part = wide[:, at]
-            pair_at = slice(LANES * (head % 2), LANES * (head % 2 + 1))
-            mixed = (m0_ref, m1_ref)[head // 2][rows, pair_at].astype(F32)
-            row_dot = jnp.sum(part * mixed, axis=-1, keepdims=True)
-            do_ref[rows, at] = put_lanes(part.astype(BF16), V_SPARE, three_parts(-row_dot))
+            do_ref[rows, at] = put_lanes(wide[:, at].astype(BF16), V_SPARE, three_parts(-row_dot[:, at]))
 
     for head in range(OWN):
         at = slice(LANES * head, LANES * (head + 1))
         pair_at = slice(LANES * (head % 2), LANES * (head % 2 + 1))
         q_ref, k_ref, v_ref = ((q0_ref, k0_ref, v0_ref), (q1_ref, k1_ref, v1_ref))[head // 2]
+        if head % 2 == 0:
+            for copy in copies[3 * (head // 2) : 3 * (head // 2) + 3]:
+                copy.wait()
         dq_ref[at, :] = jnp.zeros((LANES, tokens), F32)
 
-        @pl.loop(0, tokens // block)
-        def _(i, at=at, pair_at=pair_at, q_ref=q_ref, k_ref=k_ref, v_ref=v_ref, head=head):
-            rows = pl.ds(pl.multiple_of(i * block, block), block)
+        for i in range(tokens // block):
+            rows = slice(block * i, block * (i + 1))
             query, grad = q_ref[:, pair_at], do_ref[:, at]
             key = k_ref[rows, pair_at]
             probs = jnp.exp2(dot_nt(key, query))
@@ -433,6 +458,8 @@
             dk_ref[rows, at] = dot(slope, query) * LN2
             dq_ref[at, :] += dot(key.astype(F32).T.astype(BF16), slope)
 
+    for copy in copies[6:]:
+        copy.wait()
     gains_ref[...] = jnp.zeros_like(gains_ref)
 
     @pl.loop(0, tokens // block)
@@ -440,24 +467,24 @@
         rows = pl.ds(pl.multiple_of(i * block, block), block)
         cos, sin = cos_ref[rows, :], sin_ref[rows, :]
         for which, raw_ref, gain_ref in ((0, qraw_ref, gq_ref), (1, kraw_ref, gk_ref)):
-            gained = jnp.zeros((1, LANES), F32)
+            raw = raw_ref[rows, :]
+            inv = lax.rsqrt(head_sums(raw * raw) / HEAD + EPSILON)
+            hat = raw * inv
+            turned = []
             for head in range(OWN):
                 at = slice(LANES * head, LANES * (head + 1))
-                raw = raw_ref[rows, at]
-                inv = lax.rsqrt(jnp.sum(raw * raw, axis=-1, keepdims=True) / HEAD + EPSILON)
-                hat = raw * inv
-                if which == 0:
-                    grad = dq_ref[at, rows].T * root
-                else:
-                    grad = dk_ref[rows, at]
-                turned = grad * cos - pltpu.roll(grad, 64, 1) * sin
-                product = turned * hat
-                gained += jnp.sum(product, axis=0, keepdims=True)
-                mean = jnp.sum(product * gain_ref[...], axis=-1, keepdims=True) / HEAD
-                pad_ref[rows, PADDED * which + LANES * head : PADDED * which + LANES * (head + 1)] = (
-                    inv * (turned * gain_ref[...] - hat * mean)
-                ).astype(BF16)
-            gains_ref[which : which + 1, :] += gained
+                grad = dq_ref[at, rows].T * root if which == 0 else dk_ref[rows, at]
+                turned.append(grad * cos - pltpu.roll(grad, 64, 1) * sin)
+            gain = jnp.concatenate([gain_ref[...]] * OWN, axis=1)
+            product = jnp.concatenate(turned, axis=1) * hat
+            gained = jnp.sum(product, axis=0, keepdims=True)
+            gains_ref[which : which + 1, :] += sum(
+                gained[:, LANES * head : LANES * (head + 1)] for head in range(OWN)
+            )
+            mean = head_sums(product * gain) / HEAD
+            pad_ref[rows, PADDED * which : PADDED * (which + 1)] = (
+                inv * (jnp.concatenate(turned, axis=1) * gain - hat * mean)
+            ).astype(BF16)
         compact = [
             dot_nt(pad_ref[rows, PADDED * w : PADDED * (w + 1)], spread_ref[w]).astype(BF16)
             for w in range(3)
@@ -482,15 +509,19 @@
             jax.ShapeDtypeStruct((tokens, 3 * COLS), BF16),
             jax.ShapeDtypeStruct((8, LANES), F32),
         ],
-        in_specs=[vmem()] * 20,
+        in_specs=[vmem()] * 5 + [hbm()] * 8 + [vmem()] * 2 + [hbm()] * 2 + [vmem()] * 3,
         out_specs=[vmem()] * 2,
         scratch_shapes=[
             pltpu.VMEM((tokens, PADDED), BF16),
             pltpu.VMEM((PADDED, tokens), F32),
             pltpu.VMEM((tokens, PADDED), F32),
             pltpu.VMEM((tokens, 3 * PADDED), BF16),
-        ],
-        cost_estimate=cost(32),
+        ]
+        + [pltpu.VMEM((tokens, PAIR), BF16)] * 6
+        + [pltpu.VMEM((tokens, LANES), F32)] * 2
+        + [pltpu.VMEM((tokens, PADDED), F32)] * 2
+        + [pltpu.SemaphoreType.DMA((10,))],
+        cost_estimate=cost(K5_COST),
         compiler_params=limit(58),
         name="attention_backward",
     )(*grads, w_rows, qraw, kraw, *q, *k, *v, *mixedp, cos, sin, gq, gk, spread)
@@ -544,9 +575,10 @@
     for n, (place, x_ref, dy_ref, branch_ref, gmlp_ref) in enumerate(
         zip(places, x_refs, dy_refs, branch_refs, gmlp_refs)
     ):
-        here = slice(block * n, block * (n + 1))
+        at = slice(block * n, block * (n + 1))
+        here = slice(0, block) if number == 1 else slice(block * place, block * (place + 1))
         attended = lax.dot_general(
-            mixed_ref[:, here], wout_ref[...], (((0,), (1,)), ((), ())), preferred_element_type=F32
+            mixed_ref[:, at], wout_ref[...], (((0,), (1,)), ((), ())), preferred_element_type=F32
         )
         if place == 2:
             refs[-2][...] = attended
@@ -578,9 +610,10 @@
     block, width = x_tiles[0].shape
     hidden = w_down.shape[0]
     one = pl.Buffered(1)
-    row_block = lambda cols: pl.BlockSpec(
-        (number * block, cols), lambda i: (places[0] // number, 0), pipeline_mode=one
-    )
+    if number == 1:
+        row_block = lambda cols: pl.BlockSpec((block, cols), lambda i: (places[0], 0), pipeline_mode=one)
+    else:
+        row_block = lambda cols: pl.BlockSpec((4 * block, cols), lambda i: (0, 0), pipeline_mode=one)
     whole = lambda rows, cols: pl.BlockSpec((rows, cols), lambda i: (0, 0), pipeline_mode=one)
     args = [mod, w_out, w_gu, w_down]
     args += [x_tiles[p] for p in places] + [dy_tiles[p] for p in places] + list(mixed)
@@ -590,7 +623,7 @@
     for k, array in enumerate(kept):
         aliases[len(args)] = k
         args.append(array)
-        in_specs.append(pl.BlockSpec(memory_space=pl.ANY))
+        in_specs.append(hbm())
     shapes = [(4 * block, width), (4 * block, hidden), (4 * block, 2 * hidden), (4 * block, width)]
     attended = [jax.ShapeDtypeStruct((block, width), F32)] if 2 in places else []
     return pl.pallas_call(
@@ -604,15 +637,14 @@
         + [whole(block, width)] * (2 * number + len(attended)),
         scratch_shapes=[pltpu.VMEM((width, number * block), BF16)],
         input_output_aliases=aliases,
-        compiler_params=limit(44),
+        compiler_params=limit(58),
         cost_estimate=cost(7 * number),
         name="mlp",
     )(*args)
 
 
-def middle_kernel(a_ref, b_ref, c0_ref, c1_ref, attended_ref, x_ref, dy_ref, mod_ref, gatt_ref, gmid_ref, sums_ref):
-    far = jnp.concatenate([c0_ref[...], c1_ref[...]]).astype(F32)
-    grad_in = a_ref[...].astype(F32) + b_ref[...].astype(F32) + far
+def middle_kernel(a_ref, b_ref, c_ref, attended_ref, x_ref, dy_ref, mod_ref, gatt_ref, gmid_ref, sums_ref):
+    grad_in = a_ref[...].astype(F32) + b_ref[...].astype(F32) + c_ref[...].astype(F32)
     attended = attended_ref[...]
     x_mid = x_ref[...].astype(F32) + mod_ref[2:3, :] * attended
     inv = inverse_rms(x_mid)
@@ -639,7 +671,7 @@
             jax.ShapeDtypeStruct((block, width), F32),
             jax.ShapeDtypeStruct((8, width), F32),
         ],
-        in_specs=[vmem()] * 8,
+        in_specs=[vmem()] * 7,
         out_specs=[vmem()] * 3,
         cost_estimate=cost(4.6),
         compiler_params=limit(14),
@@ -760,16 +792,17 @@
     )(left, right)
 
 
-GU_AFTER = 4
+GU_AFTER = 5
+K5_COST = 32
+GU_BY = 3
 TO_TX = (1, 0, 2, 1)
 TO_TY = (2, 2, 0, 0)
 KEPT = (0, 1, 1, 2)
 SLOTS = ((0, 1, 2), (2, 1, 0), (0, 1, 2), (2, 1, 0))
 
 
-def pack_kernel(shard, ff_own, tile_ref, a_ref, b_ref, sgu_ref, tx_ref, ty_ref, gu_ref, down_ref, unit_ref, out_ref):
+def pack_kernel(shard, ff_own, tile_ref, a_ref, b_ref, tx_ref, ty_ref, down_ref, unit_ref, out_ref):
     cut = a_ref.shape[0]
-    share = sgu_ref.shape[1] // 4
 
     def rows(first, last, lanes):
         pieces = []
@@ -779,9 +812,6 @@
             pieces.append(b_ref[max(first, cut) - cut : last - cut, lanes])
         return pieces[0] if len(pieces) == 1 else jnp.concatenate(pieces)
 
-    def gu(tile):
-        return sgu_ref[:, share * tile : share * (tile + 1)]
-
     def down(tile):
         return rows(shard, shard + ff_own, slice(COLS * tile, COLS * (tile + 1)))
 
@@ -793,63 +823,50 @@
 
         @pl.when(tile_ref[0] == tile)
         def _(tile=tile):
-            at = 0
             for ref, pieces in (
-                (tx_ref, (gu(tile ^ 1), gu(tile ^ 3), down(tile ^ 1), down(tile ^ 3), unit(TO_TX[tile]))),
-                (ty_ref, (gu(tile ^ 2), down(tile ^ 2), unit(TO_TY[tile]))),
+                (tx_ref, (down(tile ^ 1), down(tile ^ 3), unit(TO_TX[tile]))),
+                (ty_ref, (down(tile ^ 2), unit(TO_TY[tile]))),
             ):
                 at = 0
                 for piece in pieces:
-                    ref[at : at + piece.shape[0], : piece.shape[1]] = piece.astype(BF16)
+                    ref[at : at + piece.shape[0], :COLS] = piece.astype(BF16)
                     at += piece.shape[0]
-            gu_ref[...] = gu(tile).astype(F32)
             down_ref[...] = down(tile)
             unit_ref[...] = unit(KEPT[tile])
 
 
-def pack(tile, sums, sum_gu, shard, ff_own):
-    share = sum_gu.shape[1] // 4
-    both = 3 * shard + 2 * ff_own
-    one = 2 * shard + ff_own
+def pack(tile, sums, shard, ff_own):
     return pl.pallas_call(
         functools.partial(pack_kernel, shard, ff_own),
         out_shape=[
-            jax.ShapeDtypeStruct((both, share), BF16),
-            jax.ShapeDtypeStruct((one, share), BF16),
-            jax.ShapeDtypeStruct((shard, share), F32),
+            jax.ShapeDtypeStruct((shard + 2 * ff_own, WINDOW), BF16),
+            jax.ShapeDtypeStruct((shard + ff_own, WINDOW), BF16),
             jax.ShapeDtypeStruct((ff_own, COLS), F32),
             jax.ShapeDtypeStruct((shard, COLS), F32),
             jax.ShapeDtypeStruct((shard, COLS), F32),
         ],
-        in_specs=[smem()] + [vmem()] * 3,
-        out_specs=[vmem()] * 6,
+        in_specs=[smem()] + [vmem()] * 2,
+        out_specs=[vmem()] * 5,
         compiler_params=limit(12),
         cost_estimate=cost(2),
         name="pack",
-    )(tile, *sums, sum_gu)
-
-
-def unpack_kernel(shard, ff_own, tile_ref, tx_ref, ty_ref, gu_ref, down_ref, unit_ref, wgu_ref, wdown_ref, wqkv_ref):
-    one = 2 * shard + ff_own
-    share = gu_ref.shape[1]
+    )(tile, *sums)
+
+
+def unpack_kernel(
+    shard, ff_own, tile_ref, tx_ref, ty_ref, on_ref, down_ref, unit_ref, sgu_ref, gutx_ref, guty_ref,
+    wgu_ref, wdown_ref, wqkv_ref,
+):
+    share = sgu_ref.shape[1] // 4
     groups = share // ff_own
-    gus = [
-        gu_ref[...],
-        tx_ref[0:shard, :].astype(F32),
-        ty_ref[0:shard, :].astype(F32),
-        ty_ref[one : one + shard, :].astype(F32),
-    ]
+    gus = [None, gutx_ref[:shard, :], guty_ref[:shard, :], guty_ref[shard:, :]]
     downs = [
         down_ref[...],
-        tx_ref[2 * shard : 2 * shard + ff_own, :COLS].astype(F32),
-        ty_ref[shard : shard + ff_own, :COLS].astype(F32),
-        ty_ref[one + shard : one + shard + ff_own, :COLS].astype(F32),
+        tx_ref[:ff_own, :COLS].astype(F32),
+        ty_ref[:ff_own, :COLS].astype(F32),
+        on_ref[:, :COLS].astype(F32),
     ]
-    units = [
-        unit_ref[...],
-        tx_ref[2 * shard + 2 * ff_own :, :COLS].astype(F32),
-        ty_ref[shard + ff_own : one, :COLS].astype(F32),
-    ]
+    units = [unit_ref[...], tx_ref[2 * ff_own :, :COLS].astype(F32), ty_ref[ff_own:, :COLS].astype(F32)]
     for tile in range(4):
 
         @pl.when(tile_ref[0] == tile)
@@ -857,28 +874,28 @@
             for source in range(4):
                 flip = source ^ tile
                 wdown_ref[ff_own * source : ff_own * (source + 1), :] = downs[flip]
+                piece = sgu_ref[:, share * tile : share * (tile + 1)] if flip == 0 else gus[flip]
                 for group in range(groups):
                     at = share * group + ff_own * source
-                    wgu_ref[:, at : at + ff_own] = gus[flip][:, ff_own * group : ff_own * (group + 1)]
+                    wgu_ref[:, at : at + ff_own] = piece[:, ff_own * group : ff_own * (group + 1)].astype(F32)
             for k in range(3):
                 wqkv_ref[:, COLS * k : COLS * (k + 1)] = units[SLOTS[tile][k]]
 
 
-def unpack(tile, from_tx, from_ty, kept, shard, ff_own):
-    share = kept[0].shape[1]
+def unpack(tile, from_tx, from_ty, passed_on, kept, gus, shard, ff_own):
     return pl.pallas_call(
         functools.partial(unpack_kernel, shard, ff_own),
         out_shape=[
-            jax.ShapeDtypeStruct((shard, 4 * share), F32),
+            jax.ShapeDtypeStruct(gus[0].shape, F32),
             jax.ShapeDtypeStruct((4 * ff_own, COLS), F32),
             jax.ShapeDtypeStruct((shard, 3 * COLS), F32),
         ],
-        in_specs=[smem()] + [vmem()] * 5,
+        in_specs=[smem()] + [vmem()] * 8,
         out_specs=[vmem()] * 3,
         compiler_params=limit(12),
         cost_estimate=cost(2),
         name="unpack",
-    )(tile, from_tx, from_ty, *kept)
+    )(tile, from_tx, from_ty, passed_on, *kept, *gus)
 
 
 def ada_kernel(tile_ref, mod_ref, w_ref, silu_ref, ada_ref, bias_ref, cond_ref):
@@ -1028,9 +1045,9 @@
 
     beside = [rows_step, lambda v: scatter_step(dot(v, w_ada), bits[-1])]
     beside += [lambda v, bit=bit: scatter_step(v, bit) for bit in bits[-2::-1]]
-    early, late = beside[1], beside[2]
-    beside[1] = lambda v: after(early(v), x_tiles[0])
-    beside[2] = lambda v: after(late(v), dy_tiles[0], x_tiles)
+    early = beside[2]
+    beside[2] = lambda v: after(early(v), x_tiles)
+    beside.append(lambda v: after(v, dy_tiles))
 
     ring = use_ring(count, math.gcd(shard, ff_own))
     if ring:
@@ -1073,17 +1090,15 @@
     mixed += gather_tiles(mixed1)
 
     weights = (tile_word, mod, full_out, full_gu, full_down, x_tiles, dy_tiles, mixed)
-    far = mlp((0, 1), *weights, ())
-    grad_pair = tile_pair(far[6:8])
-    cut = per_tile // 2
-    part_0, part_1 = swap(grad_pair[:cut], "ty"), swap(grad_pair[cut:], "ty")
-    beside_tile = mlp((3,), *weights, after(far[:4], grad_pair))
-    own_tile = mlp((2,), *weights, after(beside_tile[:4], part_0))
+    others = mlp((1, 0, 3), *weights, ())
+    grad_pair = tile_pair((others[8], others[7]))
+    grad_far = swap(grad_pair, "ty")
+    own_tile = mlp((2,), *weights, after(others[:4], grad_pair))
     mlp_in, hidden, grad_gu, grad_branch = own_tile[:4]
     attended = own_tile[6]
 
     grad_att, grad_mid, mid_sums = middle(
-        (own_tile[5], swap(beside_tile[5], "tx"), part_0, part_1), attended, x_own, dy_own, mod
+        (own_tile[5], swap(others[9], "tx"), grad_far), attended, x_own, dy_own, mod
     )
     g_gu = weight_grad(mlp_in, after(grad_gu, grad_att), 5)
     g_down = weight_grad(hidden, after(grad_branch, g_gu), 3)
@@ -1094,8 +1109,8 @@
         grad_att_tiles, out_rows, qraw, kraw, (q0, q1), (k0, k1), (v0, v1), (mixedp0, mixedp1),
         cos, sin, gq, gk, spread,
     )
-    branch_parts = tile_sum_parts(tile_pair(far[4:6]), (own_tile[4], beside_tile[4]))
-    output, out_sums = output_tile(after(branch_parts, grad_qkv), attended, x_own, dy_own, mod)
+    branch_parts = tile_sum_parts(tile_pair((others[5], others[4])), (own_tile[4], others[6]))
+    grad_qkv = after(grad_qkv, branch_parts)
     w_back = full_first[:, : 3 * COLS]
     back_far = dot_nt(grad_qkv[: 2 * per_tile], w_back).astype(BF16)
     halves = lambda rows: (rows[:per_tile], rows[per_tile:])
@@ -1106,11 +1121,17 @@
 
     wide = 6 * width
 
+    def output_step():
+        store["output"], store["out_sums"] = output_tile(
+            branch_parts, attended, x_own, dy_own, mod
+        )
+        return store["out_sums"]
+
     def token_step():
         parts = tile_sum_parts(back_pair, halves(back_near))
         store["grad_tokens"], tok_sums = tokens_back(parts, x_own, grad_mid, mod)
         return jnp.concatenate(
-            [tok_sums[0], tok_sums[1], mid_sums[0], mid_sums[1], mid_sums[2], out_sums[0], gains[0], gains[1]]
+            [tok_sums[0], tok_sums[1], mid_sums[0], mid_sums[1], mid_sums[2], store["out_sums"][0], gains[0], gains[1]]
         )[None]
 
     def low_step(grad_mod):
@@ -1120,13 +1141,28 @@
         store["grad_ada"], store["sums"], grad_silu = ada_back(tile_word, mod_all, w_ada, silu_rows)
         return grad_silu
 
-    steps = [None, lambda _: token_step(), lambda v: low_step(sum_tiles(v))]
+    steps = [lambda _: output_step(), lambda _: token_step(), lambda v: low_step(sum_tiles(v))]
     steps += [lambda v, bit=bit: gather_step(v, bit) for bit in bits]
     steps.append(lambda v: flip_exchange(ada_step(v), count, bits[-1:]))
-    steps.append(lambda v: flip_exchange(v, count, bits[-2::-1]))
 
     if ring:
         s_gu = lax.psum_scatter(g_gu, "img", scatter_dimension=0, tiled=True)
+        gu_cols = 2 * hidden_own // TILES
+
+        def gu_piece(flip):
+            return lax.dynamic_slice_in_dim(s_gu, tile_at(flip) * gu_cols, gu_cols, 1)
+
+        def gu_tx_step(v):
+            store["gu_tx"] = swap(jnp.concatenate([gu_piece(1), gu_piece(3)]), "tx")
+            return after(v, store["gu_tx"])
+
+        def gu_ty_step(v):
+            store["gu_ty"] = swap(jnp.concatenate([gu_piece(2), store["gu_tx"][shard:]]), "ty")
+            return after(v, store["gu_ty"])
+
+        first_half, second_half = steps[GU_BY], steps[GU_BY + 1]
+        steps[GU_BY] = lambda v: gu_tx_step(first_half(v))
+        steps[GU_BY + 1] = lambda v: gu_ty_step(second_half(v))
         s_all, grad_silu = ring_scatter([g_first, g_down], count, steps)
     else:
         grad_silu = None
@@ -1135,17 +1171,15 @@
     grad_tokens, grad_ada, sums = store["grad_tokens"], store["grad_ada"], store["sums"]
     grad_bias = sums[0, :wide]
     gain_sums = (sums[:, wide : wide + 256] + sums[:, wide + 256 : wide + 512]) + sums[:, wide + 512 :]
-    flips = (jnp.arange(count, dtype=jnp.int32) ^ img).astype(jnp.int32)
-    grad_silu = reorder(flips, grad_silu).reshape(1, width)
-    sigmoid_c = jax.nn.sigmoid(cond_float)
-    grad_cond = (grad_silu * sigmoid_c * (1.0 + cond_float * (1.0 - sigmoid_c))).astype(BF16)
     if ring:
-        to_tx, to_ty, *kept, grad_w_out = pack(tile_word, s_all, s_gu, shard, ff_own)
+        to_tx, to_ty, *kept, grad_w_out = pack(tile_word, s_all, shard, ff_own)
         from_tx = swap(to_tx, "tx")
-        to_ty = jnp.concatenate(
-            [to_ty, from_tx[shard : 2 * shard], from_tx[2 * shard + ff_own : 2 * shard + 2 * ff_own]]
+        passed_on = swap(from_tx[ff_own : 2 * ff_own], "ty")
+        from_ty = swap(to_ty, "ty")
+        grad_w_gu, grad_down, grad_w_qkv = unpack(
+            tile_word, from_tx, from_ty, passed_on, kept, (s_gu, store["gu_tx"], store["gu_ty"]), shard, ff_own
         )
-        grad_w_gu, grad_down, grad_w_qkv = unpack(tile_word, from_tx, swap(to_ty, "ty"), kept, shard, ff_own)
+        grad_silu = after(grad_silu, from_tx)
     else:
         sums_of = lambda grad: lax.psum_scatter(grad, "img", scatter_dimension=0, tiled=True)
         s_first, s_down, s_gu = sums_of(g_first).astype(F32), sums_of(g_down), sums_of(g_gu)
@@ -1179,8 +1213,14 @@
             [choose(slots, [SLOTS[t][k] for t in range(4)]) for k in range(3)], axis=1
         ).astype(F32)
 
+    flips = (jnp.arange(count, dtype=jnp.int32) ^ img).astype(jnp.int32)
+    grad_silu = flip_exchange(grad_silu, count, bits[-2::-1])
+    grad_silu = reorder(flips, grad_silu).reshape(1, width)
+    sigmoid_c = jax.nn.sigmoid(cond_float)
+    grad_cond = (grad_silu * sigmoid_c * (1.0 + cond_float * (1.0 - sigmoid_c))).astype(BF16)
+
     return (
-        output.reshape(tokens.shape),
+        store["output"].reshape(tokens.shape),
         grad_tokens.reshape(tokens.shape),
         grad_cond,
         grad_w_qkv,

time: 402 us -> 371 us (0.923)
  local copies, waits for them, and re-layouts: 53.7 us -> 29.4 us
  Pallas kernels: 113 us -> 104 us
  starting transfers between devices: 76.2 us -> 69.8 us
  other arithmetic: 10.4 us -> 15.1 us
    unnamed x247 -> x237, local copies, waits for them, and re-layouts: 48.1 us -> 20.6 us
    ppermute x14, starting transfers between devices: 25.2 us -> 14.5 us  [ring_scatter(): lax.ppermute(sums[k], 'img', ring_perm(count, sign))]
    pallas_call x1, Pallas kernels: 32.9 us -> 24.9 us  [attention_backward(): pl.pallas_call(attention_back_kernel, out_shape=[jax.ShapeDtypeStruct((to...]
    ppermute x32 -> x34, waiting for transfers between devices: 35.9 us -> 28.1 us  [swap(): return lax.ppermute(values, axis, [(0, 1), (1, 0)])]
    ppermute x7, waiting for transfers between devices: 23.5 us -> 30.5 us  [ring_gather(): b = lax.ppermute(b, 'img', ring_perm(count, -1))]
    all_gather x1, waiting for transfers between devices: 0.01 us -> 5.6 us  [body(): lax.all_gather(after(gu_own, pieces[GU_AFTER]), 'img', axis=0, tiled=True)]
    pallas_call x3 -> x2, Pallas kernels: 28.6 us -> 30.1 us  [mlp(): pl.pallas_call(functools.partial(mlp_kernel, places), grid=(1,), out_shap...]
    ppermute x32 -> x34, starting transfers between devices: 16.4 us -> 17.1 us  [swap(): return lax.ppermute(values, axis, [(0, 1), (1, 0)])]
  transfers between devices with their start and end apart: 74 -> 76, of which waited for: 35 -> 41; matrix products, arithmetic and copies ran while one was open for 5% -> 7% of each run, Pallas kernels for 25% -> 22%
where the time goes in v3:
time: 371 us; the launch traced here: 364 us
  waiting for transfers between devices  124 us (33%)
  Pallas kernels  104 us (28%)
  starting transfers between devices  69.8 us (19%)
  local copies, waits for them, and re-layouts  29.4 us (8%)
  between operations  17.3 us (5%)
  other arithmetic  15.1 us (4%)
  matrix products  4.74 us (1%)
    ppermute x14, waiting for transfers between devices, ring_scatter(): lax.ppermute(sums[k], 'img', ring_perm(count, sign))  41.7 us
    ppermute x7, waiting for transfers between devices, ring_gather(): b = lax.ppermute(b, 'img', ring_perm(count, -1))  30.5 us
    pallas_call x2, Pallas kernels, mlp(): pl.pallas_call(functools.partial(mlp_kernel, places), grid=(1,), out_shap...  30.1 us
    ppermute x34, waiting for transfers between devices, swap(): return lax.ppermute(values, axis, [(0, 1), (1, 0)])  28.1 us
    pallas_call x1, Pallas kernels, attention_backward(): pl.pallas_call(attention_back_kernel, out_shape=[jax.ShapeDtypeStruct((to...  24.9 us
    unnamed x237, local copies, waits for them, and re-layouts  20.6 us
    ppermute x34, starting transfers between devices, swap(): return lax.ppermute(values, axis, [(0, 1), (1, 0)])  17.1 us
    ppermute x6, starting transfers between devices, gather_step(): return jnp.concatenate([v, lax.ppermute(v, 'img', flip_perm(count, bit))])  16.7 us
  transfers between devices with their start and end apart: 76, of which 41 were waited for; matrix products, arithmetic and copies ran while one was open for 7% of the time, Pallas kernels for 22%

profile of v3, /device:TPU:0, one launch (start us, length us, event | category | flops | bytes accessed | tf_op | source)
XLA Modules:
  0.0 364.2 jit_solution(7461998254362645056)
XLA Ops:
  22.8 4.5 %collective-permute-done.4 = bf16[4,1152]{1,0:T(4,128)(2,1)S(1)} collective-permute-done((bf16[4,1152]{1,0:T(4,128)(2,1)S(1)}, bf16[4,1152]{1,0:T(4,128)(2,1)S(1)}, u32[]{:S(2)}, u32[]{:S(2)}) %collective-permute-start.4) | collective-permute-done | bytes 9248 | tf_op jit(solution)/shard_map/ppermute | solution.py:1033
  36.0 3.4 collective-permute-done.6.refs_9_
  45.8 6.0 %collective-permute-done.9.refs_10_ = bf16[112,1152]{1,0:T(8,128)(2,1)S(1)} collective-permute-done((bf16[112,1152]{1,0:T(8,128)(2,1)S(1)}, bf16[112,1152]{1,0:T(8,128)(2,1)S(1)}, u32[]{:S(2)}, u32[]{:S(2)}) %collective-permute-start.9) | collective-permute-done | bytes 258080 | tf_op jit(solution)/shard_map/ppermute | solution.py:152
  57.5 8.2 %collective-permute-done.15.refs_11_ = bf16[112,1152]{1,0:T(8,128)(2,1)S(1)} collective-permute-done((bf16[112,1152]{1,0:T(8,128)(2,1)S(1)}, bf16[112,1152]{1,0:T(8,128)(2,1)S(1)}, u32[]{:S(2)}, u32[]{:S(2)}) %collective-permute-start.15) | collective-permute-done | bytes 258080 | tf_op jit(solution)/shard_map/ppermute | solution.py:152
  67.8 6.6 %collective-permute-done.18.refs_12_ = bf16[112,1152]{1,0:T(8,128)(2,1)} collective-permute-done((bf16[112,1152]{1,0:T(8,128)(2,1)S(1)}, bf16[112,1152]{1,0:T(8,128)(2,1)}, u32[]{:S(2)}, u32[]{:S(2)}) %collective-permute-start.18) | collective-permute-done | bytes 258080 | tf_op jit(solution)/shard_map/ppermute | solution.py:152
  78.7 3.6 collective-permute-done.24.refs_13_
  91.5 4.7 %collective-permute-done.23.refs_7_ = bf16[128,1152]{1,0:T(8,128)(2,1)S(1)} collective-permute-done((bf16[128,1152]{1,0:T(8,128)(2,1)}, bf16[128,1152]{1,0:T(8,128)(2,1)S(1)}, u32[]{:S(2)}, u32[]{:S(2)}) %collective-permute-start.23) | collective-permute-done | bytes 294944 | tf_op jit(solution)/shard_map/ppermute | solution.py:151
  97.0 6.1 %assemble_first.1 = (bf16[1152,1152]{1,0:T(8,128)(2,1)}, bf16[768,1152]{1,0:T(8,128)(2,1)}, bf16[288,1152]{1,0:T(8,128)(2,1)}) custom-call(s32[15]{0:T(128)} %compare_select_fusion.2.index_ref, bf16[288,384]{1,0:T(8,128)(2,1)} %constant.271.clone.pick_ref, bf16[240,1152]{1,0:T(8,128)(2,1)} %copy-done.75, bf16[128,1152]{1,0:T(8,128)(2,1)} %collective-permute-done.2.refs_1_, ...), custom_call_target="tpu_custom_call" | custom-call | flops 5500000256 | bytes 15000000 | tf_op jit(solution)/shard_map/assemble_first/pallas_call | solution.py:195
  106.5 9.2 %project.1 = (bf16[1024,1152]{1,0:T(8,128)(2,1)S(1)}, f32[1024,512]{1,0:T(8,128)S(1)}, f32[1024,512]{1,0:T(8,128)S(1)}, bf16[1024,256]{1,0:T(8,128)(2,1)S(1)}, b...) custom-call(bf16[256,1152]{1,0:T(8,128)(2,1)S(1)} %copy-done.24, ...), custom_call_target="tpu_custom_call" | custom-call | flops 17600000000 | bytes 48000000 | tf_op jit(solution)/shard_map/project/pallas_call | solution.py:365
  116.3 3.5 attend.2
  124.9 3.5 attend.3
  130.9 8.0 %collective-permute-done.32.refs_10_.refs_6_.refs_4_ = bf16[144,1024]{1,0:T(8,128)(2,1)S(1)} collective-permute-done((bf16[144,1024]{1,0:T(8,128)(2,1)S(1)}, bf16[144,1024]{1,0:T(8,128)(2,1)S(1)}, u32[]{:S(2)}, u32[]{:S(2)}) %collective-permute-start.32) | collective-permute-done | bytes 294944 | tf_op jit(solution)/shard_map/ppermute | solution.py:66
  140.5 5.6 %all-gather.2.cloned.1.call-done.wgu_ref = bf16[1152,1536]{1,0:T(8,128)(2,1)} async-done(((bf16[144,1536]{1,0:T(8,128)(2,1)}), bf16[1152,1536]{1,0:T(8,128)(2,1)}) %all-gather.2.cloned.1.call-update) | async-done | bytes 3538960 | tf_op jit(solution)/shard_map/all_gather | solution.py:1064
  146.1 20.0 %mlp.2 = (bf16[1024,1152]{1,0:T(8,128)(2,1)}, bf16[1024,768]{1,0:T(8,128)(2,1)}, bf16[1024,1536]{1,0:T(8,128)(2,1)}, bf16[1024,1152]{1,0:T(8,128)(2,1)}, bf16[25...) custom-call(s32[1]{0:T(128)} %bitcast.tile_ref, ...), custom_call_target="tpu_custom_call" | custom-call | flops 23100000256 | bytes 63000000 | tf_op jit(solution)/shard_map/mlp/pallas_call | solution.py:629
  171.2 10.0 %mlp.3 = (bf16[1024,1152]{1,0:T(8,128)(2,1)}, bf16[1024,768]{1,0:T(8,128)(2,1)}, bf16[1024,1536]{1,0:T(8,128)(2,1)}, bf16[1024,1152]{1,0:T(8,128)(2,1)}, bf16[25...) custom-call(s32[1]{0:T(128)} %bitcast.tile_ref, ...), custom_call_target="tpu_custom_call", output_to_operand_aliasing={{0}: (15, {}), {1}: (16, {}), {2}: (17, {}), {3}: (18, {})} | custom-call | flops 7699999744 | bytes 21000000 | tf_op jit(solution)/shard_map/mlp/pallas_call | solution.py:629
  181.2 3.9 %collective-permute-done.40.c_ref = bf16[256,1152]{1,0:T(8,128)(2,1)S(1)} collective-permute-done((bf16[256,1152]{1,0:T(8,128)(2,1)S(1)}, bf16[256,1152]{1,0:T(8,128)(2,1)S(1)}, u32[]{:S(2)}, u32[]{:S(2)}) %collective-permute-start.40) | collective-permute-done | bytes 589856 | tf_op jit(solution)/shard_map/ppermute | solution.py:66
  192.2 5.9 %weight_grad.2 = bf16[1152,1536]{1,0:T(8,128)(2,1)} custom-call(bf16[1024,1152]{1,0:T(8,128)(2,1)S(1)} %copy-done.54, bf16[1024,1536]{1,0:T(8,128)(2,1)S(1)} %copy-done.52), custom_call_target="tpu_custom_call" | custom-call | flops 5500000256 | bytes 15000000 | tf_op jit(solution)/shard_map/weight_grad/pallas_call | solution.py:784
  209.6 24.9 %attention_backward.1 = (bf16[1024,864]{1,0:T(8,128)(2,1)}, f32[8,128]{1,0:T(8,128)}) custom-call(bf16[256,1152]{1,0:T(8,128)(2,1)} %collective-permute-done.41.g0_ref, bf16[256,1152]{1,0:T(8,128)(2,1)} %collective-permute-done.42.g1_ref, bf16[256,1152]{1,0:T(8,128)(2,1)} %get-tuple-element.173.g2_ref, bf16[256,1152]{1,0:T(8,128)(2,1)} %collective-permute-done.43.g3_ref, ...), custom_call_target="tpu_custom_call" | custom-call | flops 35200000000 | bytes 96000000 | tf_op jit(solution)/shard_map/attention_backward/pallas_call | solution.py:506
  243.1 6.2 %first_grad.1 = bf16[1152,1152]{1,0:T(8,128)(2,1)S(1)} custom-call(s32[1]{0:T(128)} %bitcast.tile_ref, bf16[256,1152]{1,0:T(8,128)(2,1)} %collective-permute-done.41.g0_ref, bf16[256,1152]{1,0:T(8,128)(2,1)} %collective-permute-done.42.g1_ref, bf16[256,1152]{1,0:T(8,128)(2,1)} %get-tuple-element.173.g2_ref, ...), custom_call_target="tpu_custom_call" | custom-call | flops 8800000000 | bytes 24000000 | tf_op jit(solution)/shard_map/first_grad/pallas_call | solution.py:765
  254.0 6.9 %collective-permute-done.48 = bf16[112,1152]{1,0:T(8,128)(2,1)S(1)} collective-permute-done((bf16[112,1152]{1,0:T(8,128)(2,1)S(1)}, bf16[112,1152]{1,0:T(8,128)(2,1)S(1)}, u32[]{:S(2)}, u32[]{:S(2)}) %collective-permute-start.48) | collective-permute-done | bytes 258080 | tf_op jit(solution)/shard_map/ppermute | solution.py:238
  260.9 3.7 %collective-permute-done.47 = bf16[128,1152]{1,0:T(8,128)(2,1)S(1)} collective-permute-done((bf16[128,1152]{1,0:T(8,128)(2,1)S(1)}, bf16[128,1152]{1,0:T(8,128)(2,1)S(1)}, u32[]{:S(2)}, u32[]{:S(2)}) %collective-permute-start.47) | collective-permute-done | bytes 294944 | tf_op jit(solution)/shard_map/ppermute | solution.py:238
  279.7 11.6 %collective-permute-done.52 = bf16[112,1152]{1,0:T(8,128)(2,1)S(1)} collective-permute-done((bf16[112,1152]{1,0:T(8,128)(2,1)S(1)}, bf16[112,1152]{1,0:T(8,128)(2,1)S(1)}, u32[]{:S(2)}, u32[]{:S(2)}) %collective-permute-start.52) | collective-permute-done | bytes 258080 | tf_op jit(solution)/shard_map/ppermute | solution.py:238
  291.3 4.9 %collective-permute-start.57 = (bf16[1,7680]{1,0:T(2,128)(2,1)}, bf16[1,7680]{1,0:T(2,128)(2,1)}, u32[]{:S(2)}, u32[]{:S(2)}) collective-permute-start(bf16[1,7680]{1,0:T(2,128)(2,1)} %pad_maximum_fusion.6), channel_id=1, source_target_pairs={{0,4},{4,0},{8,12},{12,8},{16,20},{20,16},{24,28},{28,24},{1,5},{5... | collective-permute-start | bytes 46088 | tf_op jit(solution)/shard_map/ppermute | solution.py:1033
  312.7 3.3 collective-permute-done.60
  (471 shorter events, 173.1 us)
Async XLA Ops:
  7.2 138.9 %all-gather.2.cloned.1.call-start = ((), (), s32[]{:S(2)}) async-start(), calls=%async_computation.1 | async-start | bytes 3981312 | tf_op jit(solution)/shard_map/all_gather | solution.py:1064
  29.3 11.9 %collective-permute-start.11 = (bf16[256,1152]{1,0:T(8,128)(2,1)S(1)}, bf16[256,1152]{1,0:T(8,128)(2,1)S(1)}, u32[]{:S(2)}, u32[]{:S(2)}) collective-permute-start(bf16[256,1152]{1,0:T(8,128)(2,1)S(1)} %bitcast.31), channel_id=1, source_target_pairs={{0,2},{2,0},{1,3},{3,1},{4,6},{6,4},{5,7},{7,5},{8,10},{10,8},{9,1... | collective-permute-start | bytes 1769480 | tf_op jit(solution)/shard_map/ppermute | solution.py:66
  39.7 15.7 %collective-permute-start.19 = (bf16[256,1152]{1,0:T(8,128)(2,1)S(1)}, bf16[256,1152]{1,0:T(8,128)(2,1)S(1)}, u32[]{:S(2)}, u32[]{:S(2)}) collective-permute-start(bf16[256,1152]{1,0:T(8,128)(2,1)S(1)} %bitcast.26), channel_id=1, source_target_pairs={{0,2},{2,0},{1,3},{3,1},{4,6},{6,4},{5,7},{7,5},{8,10},{10,8},{9,1... | collective-permute-start | bytes 1769480 | tf_op jit(solution)/shard_map/ppermute | solution.py:66
  52.6 15.2 %collective-permute-start.21 = (bf16[256,1152]{1,0:T(8,128)(2,1)S(1)}, bf16[256,1152]{1,0:T(8,128)(2,1)S(1)}, u32[]{:S(2)}, u32[]{:S(2)}) collective-permute-start(bf16[256,1152]{1,0:T(8,128)(2,1)S(1)} %bitcast.27), channel_id=1, source_target_pairs={{0,1},{1,0},{2,3},{3,2},{4,5},{5,4},{6,7},{7,6},{8,9},{9,8},{10,11... | collective-permute-start | bytes 1769480 | tf_op jit(solution)/shard_map/ppermute | solution.py:66
  55.4 12.4 %collective-permute-start.20 = (bf16[256,1152]{1,0:T(8,128)(2,1)S(1)}, bf16[256,1152]{1,0:T(8,128)(2,1)S(1)}, u32[]{:S(2)}, u32[]{:S(2)}) collective-permute-start(bf16[256,1152]{1,0:T(8,128)(2,1)S(1)} %collective-permute-done.19.refs_4_), channel_id=1, source_target_pairs={{0,1},{1,0},{2,3},{3,2},{4,5},{5,4},{6,7},{7,6},{8,9},{9,8},{10,11... | collective-permute-start | bytes 1769480 | tf_op jit(solution)/shard_map/ppermute | solution.py:66
  55.4 10.3 %collective-permute-start.14 = (bf16[128,1152]{1,0:T(8,128)(2,1)S(1)}, bf16[128,1152]{1,0:T(8,128)(2,1)S(1)}, u32[]{:S(2)}, u32[]{:S(2)}) collective-permute-start(bf16[128,1152]{1,0:T(8,128)(2,1)S(1)} %collective-permute-done.8.refs_3_), channel_id=1, source_target_pairs={{0,8},{8,16},{16,24},{24,28},{28,20},{20,12},{12,4},{4,0},{1,9},{9... | collective-permute-start | bytes 884744 | tf_op jit(solution)/shard_map/ppermute | solution.py:151
  82.3 217.5 %reduce-scatter.2.cloned.1.call-start = ((), (), s32[]{:S(2)}) async-start(), calls=%async_computation.2 | async-start | bytes 3981312 | tf_op jit(solution)/shard_map/reduce_scatter | solution.py:1149
  85.9 10.3 %collective-permute-start.23 = (bf16[128,1152]{1,0:T(8,128)(2,1)}, bf16[128,1152]{1,0:T(8,128)(2,1)S(1)}, u32[]{:S(2)}, u32[]{:S(2)}) collective-permute-start(bf16[128,1152]{1,0:T(8,128)(2,1)} %copy-done.107), channel_id=1, source_target_pairs={{0,8},{8,16},{16,24},{24,28},{28,20},{20,12},{12,4},{4,0},{1,9},{9... | collective-permute-start | bytes 884744 | tf_op jit(solution)/shard_map/ppermute | solution.py:151
  103.1 12.7 %collective-permute-start.26 = (bf16[288,1152]{1,0:T(8,128)(2,1)}, bf16[288,1152]{1,0:T(8,128)(2,1)S(1)}, u32[]{:S(2)}, u32[]{:S(2)}) collective-permute-start(bf16[288,1152]{1,0:T(8,128)(2,1)} %get-tuple-element.139.p2_ref), channel_id=1, source_target_pairs={{0,2},{2,0},{1,3},{3,1},{4,6},{6,4},{5,7},{7,5},{8,10},{10,8},{9,1... | collective-permute-start | bytes 1990664 | tf_op jit(solution)/shard_map/ppermute | solution.py:66
  103.1 18.7 %collective-permute-start.28 = (bf16[288,1152]{1,0:T(8,128)(2,1)}, bf16[288,1152]{1,0:T(8,128)(2,1)S(1)}, u32[]{:S(2)}, u32[]{:S(2)}) collective-permute-start(bf16[288,1152]{1,0:T(8,128)(2,1)} %get-tuple-element.139.p2_ref), channel_id=1, source_target_pairs={{0,1},{1,0},{2,3},{3,2},{4,5},{5,4},{6,7},{7,6},{8,9},{9,8},{10,11... | collective-permute-start | bytes 1990664 | tf_op jit(solution)/shard_map/ppermute | solution.py:66
  119.8 10.5 %collective-permute-start.29 = (bf16[144,1024]{1,0:T(8,128)(2,1)S(1)}, bf16[144,1024]{1,0:T(8,128)(2,1)S(1)}, u32[]{:S(2)}, u32[]{:S(2)}) collective-permute-start(bf16[144,1024]{1,0:T(8,128)(2,1)S(1)} %get-tuple-element.149.refs_8_.refs_4_.refs_2_), channel_id=1, source_target_pairs={{0,2},{2,0},{1,3},{3,1},{4,6},{6,4},{5,7},{7,5},{8,10},{10,8},{9,1... | collective-permute-start | bytes 884744 | tf_op jit(solution)/shard_map/ppermute | solution.py:66
  166.8 14.4 %collective-permute-start.39 = (bf16[256,1152]{1,0:T(8,128)(2,1)}, bf16[256,1152]{1,0:T(8,128)(2,1)S(1)}, u32[]{:S(2)}, u32[]{:S(2)}) collective-permute-start(bf16[256,1152]{1,0:T(8,128)(2,1)} %get-tuple-element.172), channel_id=1, source_target_pairs={{0,1},{1,0},{2,3},{3,2},{4,5},{5,4},{6,7},{7,6},{8,9},{9,8},{10,11... | collective-permute-start | bytes 1769480 | tf_op jit(solution)/shard_map/ppermute | solution.py:66
  166.9 39.2 %collective-permute-start.37 = (bf16[256,1152]{1,0:T(8,128)(2,1)}, bf16[256,1152]{1,0:T(8,128)(2,1)}, u32[]{:S(2)}, u32[]{:S(2)}) collective-permute-start(bf16[256,1152]{1,0:T(8,128)(2,1)} %get-tuple-element.168), channel_id=1, source_target_pairs={{0,1},{1,0},{2,3},{3,2},{4,5},{5,4},{6,7},{7,6},{8,9},{9,8},{10,11... | collective-permute-start | bytes 1769480 | tf_op jit(solution)/shard_map/ppermute | solution.py:66
  169.6 15.4 %collective-permute-start.40 = (bf16[256,1152]{1,0:T(8,128)(2,1)S(1)}, bf16[256,1152]{1,0:T(8,128)(2,1)S(1)}, u32[]{:S(2)}, u32[]{:S(2)}) collective-permute-start(bf16[256,1152]{1,0:T(8,128)(2,1)S(1)} %add_convert_fusion.2), channel_id=1, source_target_pairs={{0,2},{2,0},{1,3},{3,1},{4,6},{6,4},{5,7},{7,5},{8,10},{10,8},{9,1... | collective-permute-start | bytes 1769480 | tf_op jit(solution)/shard_map/ppermute | solution.py:66
  190.7 14.9 %collective-permute-start.41 = (bf16[256,1152]{1,0:T(8,128)(2,1)}, bf16[256,1152]{1,0:T(8,128)(2,1)}, u32[]{:S(2)}, u32[]{:S(2)}) collective-permute-start(bf16[256,1152]{1,0:T(8,128)(2,1)} %get-tuple-element.173.g2_ref), channel_id=1, source_target_pairs={{0,2},{2,0},{1,3},{3,1},{4,6},{6,4},{5,7},{7,5},{8,10},{10,8},{9,1... | collective-permute-start | bytes 1769480 | tf_op jit(solution)/shard_map/ppermute | solution.py:66
  192.2 17.4 %collective-permute-start.43 = (bf16[256,1152]{1,0:T(8,128)(2,1)}, bf16[256,1152]{1,0:T(8,128)(2,1)}, u32[]{:S(2)}, u32[]{:S(2)}) collective-permute-start(bf16[256,1152]{1,0:T(8,128)(2,1)} %get-tuple-element.173.g2_ref), channel_id=1, source_target_pairs={{0,1},{1,0},{2,3},{3,2},{4,5},{5,4},{6,7},{7,6},{8,9},{9,8},{10,11... | collective-permute-start | bytes 1769480 | tf_op jit(solution)/shard_map/ppermute | solution.py:66
  205.6 28.9 %collective-permute-start.36 = (bf16[256,1152]{1,0:T(8,128)(2,1)}, bf16[256,1152]{1,0:T(8,128)(2,1)}, u32[]{:S(2)}, u32[]{:S(2)}) collective-permute-start(bf16[256,1152]{1,0:T(8,128)(2,1)} %get-tuple-element.166), channel_id=1, source_target_pairs={{0,1},{1,0},{2,3},{3,2},{4,5},{5,4},{6,7},{7,6},{8,9},{9,8},{10,11... | collective-permute-start | bytes 1769480 | tf_op jit(solution)/shard_map/ppermute | solution.py:66
  208.1 26.4 %collective-permute-start.38 = (bf16[256,1152]{1,0:T(8,128)(2,1)}, bf16[256,1152]{1,0:T(8,128)(2,1)}, u32[]{:S(2)}, u32[]{:S(2)}) collective-permute-start(bf16[256,1152]{1,0:T(8,128)(2,1)} %add_convert_fusion.1), channel_id=1, source_target_pairs={{0,2},{2,0},{1,3},{3,1},{4,6},{6,4},{5,7},{7,5},{8,10},{10,8},{9,1... | collective-permute-start | bytes 1769480 | tf_op jit(solution)/shard_map/ppermute | solution.py:66
  241.7 25.2 %collective-permute-start.46 = (bf16[256,1152]{1,0:T(8,128)(2,1)S(1)}, bf16[256,1152]{1,0:T(8,128)(2,1)S(1)}, u32[]{:S(2)}, u32[]{:S(2)}) collective-permute-start(bf16[256,1152]{1,0:T(8,128)(2,1)S(1)} %add_convert_fusion), channel_id=1, source_target_pairs={{0,2},{2,0},{1,3},{3,1},{4,6},{6,4},{5,7},{7,5},{8,10},{10,8},{9,1... | collective-permute-start | bytes 1769480 | tf_op jit(solution)/shard_map/ppermute | solution.py:66
  249.9 11.0 %collective-permute-start.48 = (bf16[112,1152]{1,0:T(8,128)(2,1)S(1)}, bf16[112,1152]{1,0:T(8,128)(2,1)S(1)}, u32[]{:S(2)}, u32[]{:S(2)}) collective-permute-start(bf16[112,1152]{1,0:T(8,128)(2,1)S(1)} %pad_maximum_fusion.1), channel_id=1, source_target_pairs={{0,4},{8,0},{16,8},{24,16},{28,24},{20,28},{12,20},{4,12},{1,5},{9... | collective-permute-start | bytes 774152 | tf_op jit(solution)/shard_map/ppermute | solution.py:238
  250.5 14.1 %collective-permute-start.47 = (bf16[128,1152]{1,0:T(8,128)(2,1)S(1)}, bf16[128,1152]{1,0:T(8,128)(2,1)S(1)}, u32[]{:S(2)}, u32[]{:S(2)}) collective-permute-start(bf16[128,1152]{1,0:T(8,128)(2,1)S(1)} %constant_dynamic-slice_fusion.18), channel_id=1, source_target_pairs={{0,8},{8,16},{16,24},{24,28},{28,20},{20,12},{12,4},{4,0},{1,9},{9... | collective-permute-start | bytes 884744 | tf_op jit(solution)/shard_map/ppermute | solution.py:238
  253.8 13.1 %collective-permute-start.45 = (bf16[256,1152]{1,0:T(8,128)(2,1)S(1)}, bf16[256,1152]{1,0:T(8,128)(2,1)S(1)}, u32[]{:S(2)}, u32[]{:S(2)}) collective-permute-start(bf16[256,1152]{1,0:T(8,128)(2,1)S(1)} %get-tuple-element.280), channel_id=1, source_target_pairs={{0,1},{1,0},{2,3},{3,2},{4,5},{5,4},{6,7},{7,6},{8,9},{9,8},{10,11... | collective-permute-start | bytes 1769480 | tf_op jit(solution)/shard_map/ppermute | solution.py:66
  273.8 17.5 %collective-permute-start.52 = (bf16[112,1152]{1,0:T(8,128)(2,1)S(1)}, bf16[112,1152]{1,0:T(8,128)(2,1)S(1)}, u32[]{:S(2)}, u32[]{:S(2)}) collective-permute-start(bf16[112,1152]{1,0:T(8,128)(2,1)S(1)} %add_convert_fusion.13), channel_id=1, source_target_pairs={{0,4},{8,0},{16,8},{24,16},{28,24},{20,28},{12,20},{4,12},{1,5},{9... | collective-permute-start | bytes 774152 | tf_op jit(solution)/shard_map/ppermute | solution.py:238
  275.2 16.1 %collective-permute-start.51 = (bf16[128,1152]{1,0:T(8,128)(2,1)S(1)}, bf16[128,1152]{1,0:T(8,128)(2,1)S(1)}, u32[]{:S(2)}, u32[]{:S(2)}) collective-permute-start(bf16[128,1152]{1,0:T(8,128)(2,1)S(1)} %add_convert_fusion.7), channel_id=1, source_target_pairs={{0,8},{8,16},{16,24},{24,28},{28,20},{20,12},{12,4},{4,0},{1,9},{9... | collective-permute-start | bytes 884744 | tf_op jit(solution)/shard_map/ppermute | solution.py:238
  (166 other events, 1447.5 us)
Sparse Core Ops, SparseCore 0:
  82.4 63.6 all-gather.1
  209.7 86.5 reduce-scatter.1

commit v4 on v3

--- a/solution.py
+++ b/solution.py
@@ -558,36 +558,75 @@
     )(tile, *pieces)
 
 
-def mlp_kernel(places, tile_ref, mod_ref, wout_ref, wgu_ref, wdown_ref, *refs):
-    number = len(places)
-    x_refs, dy_refs, mixed_refs = refs[:number], refs[number : 2 * number], refs[2 * number : 2 * number + 4 * PAIRS]
-    refs = refs[-(4 + 2 * number + (2 in places) + 1) :]
-    mlp_ref, hidden_ref, ggu_ref, gbranch_ref = refs[:4]
-    branch_refs, gmlp_refs, mixed_ref = refs[4 : 4 + number], refs[4 + number : 4 + 2 * number], refs[-1]
+def residual_kernel(tile_ref, mod_ref, wout_ref, *refs):
+    x_refs, mixed_refs = refs[:4], refs[4 : 4 + 4 * PAIRS]
+    mlp_ref, attended_ref, mixed_ref = refs[4 + 4 * PAIRS :]
     block = x_refs[0].shape[0]
-    half = wgu_ref.shape[1] // 2
     for k, m_ref in enumerate(mixed_refs):
         pair, source = k // 4, k % 4
         start = pl.multiple_of((tile_ref[0] ^ FLIPS[source]) * COLS + PAIR_COLS * pair, 16)
-        for n, place in enumerate(places):
+        for place in range(4):
             at = block * (place ^ FLIPS[source])
-            mixed_ref[pl.ds(start, PAIR_COLS), block * n : block * (n + 1)] = m_ref[:, at : at + block]
-    for n, (place, x_ref, dy_ref, branch_ref, gmlp_ref) in enumerate(
-        zip(places, x_refs, dy_refs, branch_refs, gmlp_refs)
-    ):
-        at = slice(block * n, block * (n + 1))
-        here = slice(0, block) if number == 1 else slice(block * place, block * (place + 1))
+            mixed_ref[pl.ds(start, PAIR_COLS), block * place : block * (place + 1)] = m_ref[:, at : at + block]
+    for place, x_ref in enumerate(x_refs):
+        here = slice(block * place, block * (place + 1))
         attended = lax.dot_general(
-            mixed_ref[:, at], wout_ref[...], (((0,), (1,)), ((), ())), preferred_element_type=F32
+            mixed_ref[:, here], wout_ref[...], (((0,), (1,)), ((), ())), preferred_element_type=F32
         )
         if place == 2:
-            refs[-2][...] = attended
+            attended_ref[...] = attended
         x_mid = x_ref[...].astype(F32) + mod_ref[2:3, :] * attended
         normed = x_mid * inverse_rms(x_mid)
-        mlp_in = (normed * (1.0 + mod_ref[4:5, :]) + mod_ref[3:4, :]).astype(BF16)
-        mlp_ref[here, :] = mlp_in
-        grad_branch = (mod_ref[5:6, :] * (mod_ref[6:7, :] * dy_ref[...].astype(F32))).astype(BF16)
-        gbranch_ref[here, :] = grad_branch
+        mlp_ref[here, :] = (normed * (1.0 + mod_ref[4:5, :]) + mod_ref[3:4, :]).astype(BF16)
+
+
+def branch_kernel(mod_ref, dy0_ref, dy1_ref, dy2_ref, dy3_ref, out_ref):
+    block = dy0_ref.shape[0]
+    for place, dy_ref in enumerate((dy0_ref, dy1_ref, dy2_ref, dy3_ref)):
+        out_ref[block * place : block * (place + 1), :] = (
+            mod_ref[5:6, :] * (mod_ref[6:7, :] * dy_ref[...].astype(F32))
+        ).astype(BF16)
+
+
+def branch_grad(mod, dy_tiles):
+    block, width = dy_tiles[0].shape
+    return pl.pallas_call(
+        branch_kernel,
+        out_shape=jax.ShapeDtypeStruct((4 * block, width), BF16),
+        in_specs=[vmem()] * 5,
+        out_specs=vmem(),
+        compiler_params=limit(12),
+        cost_estimate=cost(3),
+        name="branch_grad",
+    )(mod, *dy_tiles)
+
+
+def residual(tile, mod, w_out, x_tiles, mixed):
+    block, width = x_tiles[0].shape
+    return pl.pallas_call(
+        residual_kernel,
+        out_shape=[
+            jax.ShapeDtypeStruct((4 * block, width), BF16),
+            jax.ShapeDtypeStruct((block, width), F32),
+        ],
+        in_specs=[smem()] + [vmem()] * (6 + 4 * PAIRS),
+        out_specs=[vmem()] * 2,
+        scratch_shapes=[pltpu.VMEM((width, 4 * block), BF16)],
+        compiler_params=limit(58),
+        cost_estimate=cost(9),
+        name="residual",
+    )(tile, mod, w_out, *x_tiles, *mixed)
+
+
+def mlp_kernel(places, wgu_ref, wdown_ref, in_ref, gbranch_ref, *refs):
+    number = len(places)
+    refs = refs[-(2 + 2 * number) :]
+    hidden_ref, ggu_ref, branch_refs, gmlp_refs = refs[0], refs[1], refs[2 : 2 + number], refs[2 + number :]
+    block = branch_refs[0].shape[0]
+    half = wgu_ref.shape[1] // 2
+    for place, branch_ref, gmlp_ref in zip(places, branch_refs, gmlp_refs):
+        here = slice(0, block) if number == 1 else slice(block * place, block * (place + 1))
+        mlp_in, grad_branch = in_ref[here, :], gbranch_ref[here, :]
         gate = dot(mlp_in, wgu_ref[:, :half])
         up = dot(mlp_in, wgu_ref[:, half:])
         grad_hidden = dot_nt(grad_branch, wdown_ref[...])
@@ -605,9 +644,10 @@
         ).astype(BF16)
 
 
-def mlp(places, tile, mod, w_out, w_gu, w_down, x_tiles, dy_tiles, mixed, kept):
+def mlp(places, w_gu, w_down, mlp_in, grad_branch, kept):
     number = len(places)
-    block, width = x_tiles[0].shape
+    tokens, width = mlp_in.shape
+    block = tokens // 4
     hidden = w_down.shape[0]
     one = pl.Buffered(1)
     if number == 1:
@@ -615,30 +655,19 @@
     else:
         row_block = lambda cols: pl.BlockSpec((4 * block, cols), lambda i: (0, 0), pipeline_mode=one)
     whole = lambda rows, cols: pl.BlockSpec((rows, cols), lambda i: (0, 0), pipeline_mode=one)
-    args = [mod, w_out, w_gu, w_down]
-    args += [x_tiles[p] for p in places] + [dy_tiles[p] for p in places] + list(mixed)
-    in_specs = [smem()] + [whole(*arg.shape) for arg in args]
-    args = [tile] + args
-    aliases = {}
-    for k, array in enumerate(kept):
-        aliases[len(args)] = k
-        args.append(array)
-        in_specs.append(hbm())
-    shapes = [(4 * block, width), (4 * block, hidden), (4 * block, 2 * hidden), (4 * block, width)]
-    attended = [jax.ShapeDtypeStruct((block, width), F32)] if 2 in places else []
+    args = [w_gu, w_down, mlp_in, grad_branch, *kept]
+    shapes = [(tokens, hidden), (tokens, 2 * hidden)]
     return pl.pallas_call(
         functools.partial(mlp_kernel, places),
         grid=(1,),
         out_shape=[jax.ShapeDtypeStruct(shape, BF16) for shape in shapes]
-        + [jax.ShapeDtypeStruct((block, width), BF16)] * (2 * number)
-        + attended,
-        in_specs=in_specs,
-        out_specs=[row_block(shape[1]) for shape in shapes]
-        + [whole(block, width)] * (2 * number + len(attended)),
-        scratch_shapes=[pltpu.VMEM((width, number * block), BF16)],
-        input_output_aliases=aliases,
+        + [jax.ShapeDtypeStruct((block, width), BF16)] * (2 * number),
+        in_specs=[whole(*w_gu.shape), whole(*w_down.shape), row_block(width), row_block(width)]
+        + [hbm()] * len(kept),
+        out_specs=[row_block(shape[1]) for shape in shapes] + [whole(block, width)] * (2 * number),
+        input_output_aliases={4 + k: k for k in range(len(kept))},
         compiler_params=limit(58),
-        cost_estimate=cost(7 * number),
+        cost_estimate=cost(12 if number == 2 else 0.3),
         name="mlp",
     )(*args)
 
@@ -768,8 +797,8 @@
         in_specs=[smem()] + [vmem()] * (6 + 4 * PAIRS),
         out_specs=vmem(),
         scratch_shapes=[pltpu.VMEM((grad_qkv.shape[0], COLS), BF16)],
-        compiler_params=limit(24),
-        cost_estimate=cost(8),
+        compiler_params=limit(58),
+        cost_estimate=cost(FIRST_COST),
         name="first_grad",
     )(tile, *grads, *mixed, attn_in, grad_qkv)
 
@@ -793,8 +822,10 @@
 
 
 GU_AFTER = 5
-K5_COST = 32
+K5_COST = 1
 GU_BY = 3
+TIE_BY = 1
+FIRST_COST = 1
 TO_TX = (1, 0, 2, 1)
 TO_TY = (2, 2, 0, 0)
 KEPT = (0, 1, 1, 2)
@@ -1023,7 +1054,6 @@
     x_own = tokens.reshape(per_tile, width)
     dy_own = cotangent.reshape(per_tile, width)
     x_tiles = gather_tiles(x_own)
-    dy_tiles = gather_tiles(dy_own)
 
     cond_float = cond.astype(F32)
     bits = [1 << k for k in range(count.bit_length() - 1)]
@@ -1035,19 +1065,23 @@
     def scatter_step(v, bit):
         return v[:bit] + lax.ppermute(v[bit:], "img", flip_perm(count, bit))
 
-    silu_some = jax.nn.silu(cond_float).astype(BF16)
-    for bit in bits[:-1]:
-        silu_some = gather_step(silu_some, bit)
-
-    def rows_step(_):
-        store["silu_rows"] = lax.dynamic_slice_in_dim(gather_step(silu_some, bits[-1]), img * shard, shard, 1)
+    silu_some = gather_step(jax.nn.silu(cond_float).astype(BF16), bits[0])
+
+    def rows_step(v):
+        store["silu_rows"] = lax.dynamic_slice_in_dim(gather_step(v, bits[-1]), img * shard, shard, 1)
         return store["silu_rows"]
 
-    beside = [rows_step, lambda v: scatter_step(dot(v, w_ada), bits[-1])]
+    def dy_step(v):
+        store["dy"] = gather_tiles(after(dy_own, v))
+        return v
+
+    beside = [lambda _, bit=bit: gather_step(silu_some if _ is None else _, bit) for bit in bits[1:-1]]
+    beside += [rows_step, lambda v: scatter_step(dot(v, w_ada), bits[-1])]
     beside += [lambda v, bit=bit: scatter_step(v, bit) for bit in bits[-2::-1]]
-    early = beside[2]
+    early, middle_step, late = beside[2], beside[3], beside[-1]
     beside[2] = lambda v: after(early(v), x_tiles)
-    beside.append(lambda v: after(v, dy_tiles))
+    beside[3] = lambda v: middle_step(dy_step(v))
+    beside.append(lambda v: after(v, store["dy"]))
 
     ring = use_ring(count, math.gcd(shard, ff_own))
     if ring:
@@ -1071,6 +1105,7 @@
         for step in beside:
             modulation = step(modulation)
     silu_rows = store["silu_rows"]
+    dy_tiles = store["dy"]
     modulation = modulation + ada_bias
     mod = jnp.concatenate([modulation.reshape(6, width), jnp.broadcast_to(live, (2, width))])
 
@@ -1089,16 +1124,18 @@
     q1, mixedp1, mixed1 = attend(after(q1, full_out, mixed0), k1, v1, spread)
     mixed += gather_tiles(mixed1)
 
-    weights = (tile_word, mod, full_out, full_gu, full_down, x_tiles, dy_tiles, mixed)
-    others = mlp((1, 0, 3), *weights, ())
-    grad_pair = tile_pair((others[8], others[7]))
+    grad_branch = branch_grad(mod, after(dy_tiles, mixed1))
+    mlp_in, attended = residual(tile_word, mod, full_out, after(x_tiles, grad_branch), mixed)
+    weights = (full_gu, full_down, mlp_in, grad_branch)
+    far = mlp((1, 0), *weights, ())
+    grad_pair = tile_pair((far[5], far[4]))
     grad_far = swap(grad_pair, "ty")
-    own_tile = mlp((2,), *weights, after(others[:4], grad_pair))
-    mlp_in, hidden, grad_gu, grad_branch = own_tile[:4]
-    attended = own_tile[6]
+    beside_tile = mlp((3,), *weights, after(far[:2], grad_pair))
+    own_tile = mlp((2,), *weights, beside_tile[:2])
+    hidden, grad_gu = own_tile[:2]
 
     grad_att, grad_mid, mid_sums = middle(
-        (own_tile[5], swap(others[9], "tx"), grad_far), attended, x_own, dy_own, mod
+        (own_tile[3], swap(beside_tile[3], "tx"), grad_far), attended, x_own, dy_own, mod
     )
     g_gu = weight_grad(mlp_in, after(grad_gu, grad_att), 5)
     g_down = weight_grad(hidden, after(grad_branch, g_gu), 3)
@@ -1109,15 +1146,15 @@
         grad_att_tiles, out_rows, qraw, kraw, (q0, q1), (k0, k1), (v0, v1), (mixedp0, mixedp1),
         cos, sin, gq, gk, spread,
     )
-    branch_parts = tile_sum_parts(tile_pair((others[5], others[4])), (own_tile[4], others[6]))
+    branch_parts = tile_sum_parts(tile_pair((far[3], far[2])), (own_tile[2], beside_tile[2]))
     grad_qkv = after(grad_qkv, branch_parts)
     w_back = full_first[:, : 3 * COLS]
-    back_far = dot_nt(grad_qkv[: 2 * per_tile], w_back).astype(BF16)
+    g_first = first_grad(tile_word, grad_att_tiles, mixed, attn_in, grad_qkv)
+    back_qkv = after(grad_qkv, g_first)
+    back_far = dot_nt(back_qkv[: 2 * per_tile], w_back).astype(BF16)
     halves = lambda rows: (rows[:per_tile], rows[per_tile:])
     back_pair = tile_pair(halves(back_far))
-    late_qkv = after(grad_qkv, back_pair)
-    back_near = dot_nt(late_qkv[2 * per_tile :], w_back).astype(BF16)
-    g_first = first_grad(tile_word, grad_att_tiles, mixed, attn_in, late_qkv)
+    back_near = dot_nt(after(back_qkv, back_pair)[2 * per_tile :], w_back).astype(BF16)
 
     wide = 6 * width
 
@@ -1160,6 +1197,8 @@
             store["gu_ty"] = swap(jnp.concatenate([gu_piece(2), store["gu_tx"][shard:]]), "ty")
             return after(v, store["gu_ty"])
 
+        tied = steps[TIE_BY]
+        steps[TIE_BY] = lambda v: after(tied(v), s_gu)
         first_half, second_half = steps[GU_BY], steps[GU_BY + 1]
         steps[GU_BY] = lambda v: gu_tx_step(first_half(v))
         steps[GU_BY + 1] = lambda v: gu_ty_step(second_half(v))

time: 371 us -> 362 us (0.976)
  waiting for transfers between devices: 124 us -> 103 us
  Pallas kernels: 104 us -> 114 us
  local copies, waits for them, and re-layouts: 29.4 us -> 34.4 us
    ppermute x14, waiting for transfers between devices: 41.7 us -> 26.5 us  [ring_scatter(): lax.ppermute(sums[k], 'img', ring_perm(count, sign))]
    ppermute x7, waiting for transfers between devices: 30.5 us -> 20.3 us  [ring_gather(): b = lax.ppermute(b, 'img', ring_perm(count, -1))]
    pallas_call x0 -> x2, Pallas kernels: none -> 9.43 us  [the longest x1 8.87 us: residual(): pl.pallas_call(residual_kernel, out_shape=[jax.ShapeDtypeStruct((4 * bloc...]
    all_gather x1, waiting for transfers between devices: 5.6 us -> 0.01 us  [body(): lax.all_gather(after(gu_own, pieces[GU_AFTER]), 'img', axis=0, tiled=True)]
    ppermute x34, waiting for transfers between devices: 28.1 us -> 33.2 us  [swap(): return lax.ppermute(values, axis, [(0, 1), (1, 0)])]
    ppermute x6, starting transfers between devices: 16.7 us -> 12.1 us  [gather_step(): return jnp.concatenate([v, lax.ppermute(v, 'img', flip_perm(count, bit))])]
    pallas_call x2 -> x3, Pallas kernels: 30.1 us -> 26.2 us  [mlp(): pl.pallas_call(functools.partial(mlp_kernel, places), grid=(1,), out_shap...]
    unnamed x237 -> x219, local copies, waits for them, and re-layouts: 20.6 us -> 24.4 us
  transfers between devices with their start and end apart: 76 -> 76, of which waited for: 41 -> 41; matrix products, arithmetic and copies ran while one was open for 7% -> 7% of each run, Pallas kernels for 22% -> 28%
where the time goes in v4:
time: 362 us; the launch traced here: 355 us
  Pallas kernels  114 us (31%)
  waiting for transfers between devices  103 us (28%)
  starting transfers between devices  71.6 us (20%)
  local copies, waits for them, and re-layouts  34.4 us (10%)
  between operations  16.5 us (5%)
  other arithmetic  12.6 us (3%)
    ppermute x34, waiting for transfers between devices, swap(): return lax.ppermute(values, axis, [(0, 1), (1, 0)])  33.2 us
    ppermute x14, waiting for transfers between devices, ring_scatter(): lax.ppermute(sums[k], 'img', ring_perm(count, sign))  26.5 us
    pallas_call x3, Pallas kernels, mlp(): pl.pallas_call(functools.partial(mlp_kernel, places), grid=(1,), out_shap...  26.2 us
    pallas_call x1, Pallas kernels, attention_backward(): pl.pallas_call(attention_back_kernel, out_shape=[jax.ShapeDtypeStruct((to...  24.9 us
    unnamed x219, local copies, waits for them, and re-layouts  24.4 us
    ppermute x7, waiting for transfers between devices, ring_gather(): b = lax.ppermute(b, 'img', ring_perm(count, -1))  20.3 us
    ppermute x34, starting transfers between devices, swap(): return lax.ppermute(values, axis, [(0, 1), (1, 0)])  18.7 us
    ppermute x14, starting transfers between devices, ring_scatter(): lax.ppermute(sums[k], 'img', ring_perm(count, sign))  15 us
  transfers between devices with their start and end apart: 76, of which 41 were waited for; matrix products, arithmetic and copies ran while one was open for 7% of the time, Pallas kernels for 28%

profile of v4, /device:TPU:0, one launch (start us, length us, event | category | flops | bytes accessed | tf_op | source)
XLA Modules:
  0.0 355.2 jit_solution(6878817376060236393)
XLA Ops:
  16.9 5.3 %collective-permute-done.3 = bf16[2,1152]{1,0:T(2,128)(2,1)S(1)} collective-permute-done((bf16[2,1152]{1,0:T(2,128)(2,1)S(1)}, bf16[2,1152]{1,0:T(2,128)(2,1)S(1)}, u32[]{:S(2)}, u32[]{:S(2)}) %collective-permute-start.3) | collective-permute-done | bytes 4640 | tf_op jit(solution)/shard_map/ppermute | solution.py:1063
  41.5 4.7 %collective-permute-done.8.refs_10_ = bf16[112,1152]{1,0:T(8,128)(2,1)S(1)} collective-permute-done((bf16[112,1152]{1,0:T(8,128)(2,1)S(1)}, bf16[112,1152]{1,0:T(8,128)(2,1)S(1)}, u32[]{:S(2)}, u32[]{:S(2)}) %collective-permute-start.8) | collective-permute-done | bytes 258080 | tf_op jit(solution)/shard_map/ppermute | solution.py:152
  52.5 4.3 %collective-permute-done.14.refs_11_ = bf16[112,1152]{1,0:T(8,128)(2,1)S(1)} collective-permute-done((bf16[112,1152]{1,0:T(8,128)(2,1)S(1)}, bf16[112,1152]{1,0:T(8,128)(2,1)S(1)}, u32[]{:S(2)}, u32[]{:S(2)}) %collective-permute-start.14) | collective-permute-done | bytes 258080 | tf_op jit(solution)/shard_map/ppermute | solution.py:152
  64.9 3.4 collective-permute-done.17.refs_12_
  73.5 5.0 %collective-permute-done.20.refs_13_ = bf16[112,1152]{1,0:T(8,128)(2,1)} collective-permute-done((bf16[112,1152]{1,0:T(8,128)(2,1)}, bf16[112,1152]{1,0:T(8,128)(2,1)}, u32[]{:S(2)}, u32[]{:S(2)}) %collective-permute-start.20) | collective-permute-done | bytes 258080 | tf_op jit(solution)/shard_map/ppermute | solution.py:152
  90.2 6.1 %assemble_first.1 = (bf16[1152,1152]{1,0:T(8,128)(2,1)}, bf16[768,1152]{1,0:T(8,128)(2,1)}, bf16[288,1152]{1,0:T(8,128)(2,1)}) custom-call(s32[15]{0:T(128)} %compare_select_fusion.2.index_ref, bf16[288,384]{1,0:T(8,128)(2,1)} %constant.271.clone.pick_ref, bf16[240,1152]{1,0:T(8,128)(2,1)} %copy-done.60, bf16[128,1152]{1,0:T(8,128)(2,1)} %collective-permute-done.1.refs_1_, ...), custom_call_target="tpu_custom_call" | custom-call | flops 5500000256 | bytes 15000000 | tf_op jit(solution)/shard_map/assemble_first/pallas_call | solution.py:195
  101.8 10.6 %project.1 = (bf16[1024,1152]{1,0:T(8,128)(2,1)S(1)}, f32[1024,512]{1,0:T(8,128)S(1)}, f32[1024,512]{1,0:T(8,128)S(1)}, bf16[1024,256]{1,0:T(8,128)(2,1)S(1)}, b...) custom-call(bf16[256,1152]{1,0:T(8,128)(2,1)} %collective-permute-do, ...), custom_call_target="tpu_custom_call" | custom-call | flops 17600000000 | bytes 48000000 | tf_op jit(solution)/shard_map/project/pallas_call | solution.py:365
  113.9 3.5 attend.2
  122.1 3.5 attend.3
  127.5 7.6 %collective-permute-done.32.refs_8_.refs_4_ = bf16[144,1024]{1,0:T(8,128)(2,1)S(1)} collective-permute-done((bf16[144,1024]{1,0:T(8,128)(2,1)S(1)}, bf16[144,1024]{1,0:T(8,128)(2,1)S(1)}, u32[]{:S(2)}, u32[]{:S(2)}) %collective-permute-start.32) | collective-permute-done | bytes 294944 | tf_op jit(solution)/shard_map/ppermute | solution.py:66
  138.8 8.9 %residual.1 = (bf16[1024,1152]{1,0:T(8,128)(2,1)}, f32[256,1152]{1,0:T(8,128)}) custom-call(s32[1]{0:T(128)} %bitcast.2.tile_ref, f32[8,1152]{1,0:T(8,128)} %copy-done.30, bf16[1152,1152]{1,0:T(8,128)(2,1)} %copy-done.54, bf16[256,1152]{1,0:T(8,128)(2,1)} %collective-permute-done.10.x0_ref.refs_0_, bf16[256,1152]{1,0:T(8,128)(2,1)} %copy-done.43, ...), custom_call_target="tpu_custom_call" | custom-call | flops 9900000256 | bytes 27000000 | tf_op jit(solution)/shard_map/residual/pallas_call | solution.py:606
  147.7 12.3 %mlp.3 = (bf16[1024,768]{1,0:T(8,128)(2,1)}, bf16[1024,1536]{1,0:T(8,128)(2,1)}, bf16[256,1152]{1,0:T(8,128)(2,1)}, bf16[256,1152]{1,0:T(8,128)(2,1)}, bf16[256,...) custom-call(bf16[1152,1536]{1,0:T(8,128)(2,1)} %all-gather.2.cloned.1.call-done.wgu_ref, ...), custom_call_target="tpu_custom_call" | custom-call | flops 13200000000 | bytes 36000000 | tf_op jit(solution)/shard_map/mlp/pallas_call | solution.py:660
  164.1 6.9 %mlp.4 = (bf16[1024,768]{1,0:T(8,128)(2,1)}, bf16[1024,1536]{1,0:T(8,128)(2,1)}, bf16[256,1152]{1,0:T(8,128)(2,1)}, bf16[256,1152]{1,0:T(8,128)(2,1)}) custom-call(bf16[1152,1536]{1,0:T(8,128)(2,1)} %all-gather.2.cloned.1.call-done.wgu_ref, bf16[768,1152]{1,0:T(8,128)(2,1)} %get-tuple-element.154.wdown_ref, ...), custom_call_target="tpu_custom_call", output_to_operand_aliasing={{0}: (4, {}), {1}: (5, {})} | custom-call | flops 330000000 | bytes 900000 | tf_op jit(solution)/shard_map/mlp/pallas_call | solution.py:660
  171.5 7.0 %mlp.5 = (bf16[1024,768]{1,0:T(8,128)(2,1)}, bf16[1024,1536]{1,0:T(8,128)(2,1)}, bf16[256,1152]{1,0:T(8,128)(2,1)}, bf16[256,1152]{1,0:T(8,128)(2,1)}) custom-call(bf16[1152,1536]{1,0:T(8,128)(2,1)} %all-gather.2.cloned.1.call-done.wgu_ref, bf16[768,1152]{1,0:T(8,128)(2,1)} %get-tuple-element.154.wdown_ref, ...), custom_call_target="tpu_custom_call", output_to_operand_aliasing={{0}: (4, {}), {1}: (5, {})} | custom-call | flops 330000000 | bytes 900000 | tf_op jit(solution)/shard_map/mlp/pallas_call | solution.py:660
  180.2 3.5 middle.1
  185.7 4.1 %weight_grad.2 = bf16[1152,1536]{1,0:T(8,128)(2,1)S(1)} custom-call(bf16[1024,1152]{1,0:T(8,128)(2,1)S(1)} %copy-done.5, bf16[1024,1536]{1,0:T(8,128)(2,1)S(1)} %copy-done.2), custom_call_target="tpu_custom_call" | custom-call | flops 5500000256 | bytes 15000000 | tf_op jit(solution)/shard_map/weight_grad/pallas_call | solution.py:813
  204.7 24.9 %attention_backward.1 = (bf16[1024,864]{1,0:T(8,128)(2,1)}, f32[8,128]{1,0:T(8,128)}) custom-call(bf16[256,1152]{1,0:T(8,128)(2,1)} %collective-permute-done.41.g0_ref, bf16[256,1152]{1,0:T(8,128)(2,1)} %collective-permute-done.42.g1_ref, bf16[256,1152]{1,0:T(8,128)(2,1)} %get-tuple-element.195.g2_ref, bf16[256,1152]{1,0:T(8,128)(2,1)} %collective-permute-done.43.g3_ref, ...), custom_call_target="tpu_custom_call" | custom-call | flops 1100000000 | bytes 3000000 | tf_op jit(solution)/shard_map/attention_backward/pallas_call | solution.py:506
  229.7 9.5 %first_grad.1 = bf16[1152,1152]{1,0:T(8,128)(2,1)} custom-call(s32[1]{0:T(128)} %bitcast.2.tile_ref, bf16[256,1152]{1,0:T(8,128)(2,1)} %collective-permute-done.41.g0_ref, bf16[256,1152]{1,0:T(8,128)(2,1)} %collective-permute-done.42.g1_ref, bf16[256,1152]{1,0:T(8,128)(2,1)} %get-tuple-element.195.g2_ref, bf16[256,1152]{1,0:T(8,128)(2,1)} %collective-permute-done.43.g3_ref, ...), custom_call_target="tpu_custom_call" | custom-call | flops 1100000000 | bytes 3000000 | tf_op jit(solution)/shard_map/first_grad/pallas_call | solution.py:794
  248.8 4.2 %collective-permute-done.48 = bf16[112,1152]{1,0:T(8,128)(2,1)S(1)} collective-permute-done((bf16[112,1152]{1,0:T(8,128)(2,1)S(1)}, bf16[112,1152]{1,0:T(8,128)(2,1)S(1)}, u32[]{:S(2)}, u32[]{:S(2)}) %collective-permute-start.48) | collective-permute-done | bytes 258080 | tf_op jit(solution)/shard_map/ppermute | solution.py:238
  260.3 7.7 %collective-permute-done.46.c_ref = bf16[256,1152]{1,0:T(8,128)(2,1)S(1)} collective-permute-done((bf16[256,1152]{1,0:T(8,128)(2,1)S(1)}, bf16[256,1152]{1,0:T(8,128)(2,1)S(1)}, u32[]{:S(2)}, u32[]{:S(2)}) %collective-permute-start.46) | collective-permute-done | bytes 589856 | tf_op jit(solution)/shard_map/ppermute | solution.py:66
  285.4 5.9 %collective-permute-done.51 = bf16[128,1152]{1,0:T(8,128)(2,1)S(1)} collective-permute-done((bf16[128,1152]{1,0:T(8,128)(2,1)S(1)}, bf16[128,1152]{1,0:T(8,128)(2,1)S(1)}, u32[]{:S(2)}, u32[]{:S(2)}) %collective-permute-start.51) | collective-permute-done | bytes 294944 | tf_op jit(solution)/shard_map/ppermute | solution.py:238
  295.6 4.2 %collective-permute-done.56 = bf16[112,1152]{1,0:T(8,128)(2,1)S(1)} collective-permute-done((bf16[112,1152]{1,0:T(8,128)(2,1)S(1)}, bf16[112,1152]{1,0:T(8,128)(2,1)S(1)}, u32[]{:S(2)}, u32[]{:S(2)}) %collective-permute-start.56) | collective-permute-done | bytes 258080 | tf_op jit(solution)/shard_map/ppermute | solution.py:238
  305.4 3.6 %collective-permute-done.60 = bf16[112,1152]{1,0:T(8,128)(2,1)S(1)} collective-permute-done((bf16[112,1152]{1,0:T(8,128)(2,1)S(1)}, bf16[112,1152]{1,0:T(8,128)(2,1)S(1)}, u32[]{:S(2)}, u32[]{:S(2)}) %collective-permute-start.60) | collective-permute-done | bytes 258080 | tf_op jit(solution)/shard_map/ppermute | solution.py:238
  315.6 3.6 %collective-permute-done.64 = bf16[112,1152]{1,0:T(8,128)(2,1)S(1)} collective-permute-done((bf16[112,1152]{1,0:T(8,128)(2,1)S(1)}, bf16[112,1152]{1,0:T(8,128)(2,1)S(1)}, u32[]{:S(2)}, u32[]{:S(2)}) %collective-permute-start.64) | collective-permute-done | bytes 258080 | tf_op jit(solution)/shard_map/ppermute | solution.py:238
  (456 shorter events, 178.5 us)
Async XLA Ops:
  7.2 140.5 %all-gather.2.cloned.1.call-start = ((), (), s32[]{:S(2)}) async-start(), calls=%async_computation.1 | async-start | bytes 3981312 | tf_op jit(solution)/shard_map/all_gather | solution.py:1098
  22.3 10.2 %collective-permute-start.4 = (bf16[128,1152]{1,0:T(8,128)(2,1)}, bf16[128,1152]{1,0:T(8,128)(2,1)}, u32[]{:S(2)}, u32[]{:S(2)}) collective-permute-start(bf16[128,1152]{1,0:T(8,128)(2,1)} %collective-permute-done.1.refs_1_), channel_id=1, source_target_pairs={{0,8},{8,16},{16,24},{24,28},{28,20},{20,12},{12,4},{4,0},{1,9},{9... | collective-permute-start | bytes 884744 | tf_op jit(solution)/shard_map/ppermute | solution.py:151
  24.4 13.2 %collective-permute-start.10 = (bf16[256,1152]{1,0:T(8,128)(2,1)}, bf16[256,1152]{1,0:T(8,128)(2,1)}, u32[]{:S(2)}, u32[]{:S(2)}) collective-permute-start(bf16[256,1152]{1,0:T(8,128)(2,1)} %bitcast.x2_ref.refs_2_.x_ref), channel_id=1, source_target_pairs={{0,2},{2,0},{1,3},{3,1},{4,6},{6,4},{5,7},{7,5},{8,10},{10,8},{9,1... | collective-permute-start | bytes 1769480 | tf_op jit(solution)/shard_map/ppermute | solution.py:66
  51.0 13.8 %collective-permute-start.21 = (bf16[256,1152]{1,0:T(8,128)(2,1)S(1)}, bf16[256,1152]{1,0:T(8,128)(2,1)S(1)}, u32[]{:S(2)}, u32[]{:S(2)}) collective-permute-start(bf16[256,1152]{1,0:T(8,128)(2,1)S(1)} %bitcast.25), channel_id=1, source_target_pairs={{0,2},{2,0},{1,3},{3,1},{4,6},{6,4},{5,7},{7,5},{8,10},{10,8},{9,1... | collective-permute-start | bytes 1769480 | tf_op jit(solution)/shard_map/ppermute | solution.py:66
  59.6 13.9 %collective-permute-start.23 = (bf16[256,1152]{1,0:T(8,128)(2,1)S(1)}, bf16[256,1152]{1,0:T(8,128)(2,1)S(1)}, u32[]{:S(2)}, u32[]{:S(2)}) collective-permute-start(bf16[256,1152]{1,0:T(8,128)(2,1)S(1)} %bitcast.26), channel_id=1, source_target_pairs={{0,1},{1,0},{2,3},{3,2},{4,5},{5,4},{6,7},{7,6},{8,9},{9,8},{10,11... | collective-permute-start | bytes 1769480 | tf_op jit(solution)/shard_map/ppermute | solution.py:66
  78.4 196.9 %reduce-scatter.2.cloned.1.call-start = ((), (), s32[]{:S(2)}) async-start(), calls=%async_computation.2 | async-start | bytes 3981312 | tf_op jit(solution)/shard_map/reduce_scatter | solution.py:1186
  96.3 22.7 %collective-permute-start.28 = (bf16[288,1152]{1,0:T(8,128)(2,1)}, bf16[288,1152]{1,0:T(8,128)(2,1)S(1)}, u32[]{:S(2)}, u32[]{:S(2)}) collective-permute-start(bf16[288,1152]{1,0:T(8,128)(2,1)} %get-tuple-element.156.p2_ref), channel_id=1, source_target_pairs={{0,1},{1,0},{2,3},{3,2},{4,5},{5,4},{6,7},{7,6},{8,9},{9,8},{10,11... | collective-permute-start | bytes 1990664 | tf_op jit(solution)/shard_map/ppermute | solution.py:66
  96.3 17.5 %collective-permute-start.26 = (bf16[288,1152]{1,0:T(8,128)(2,1)}, bf16[288,1152]{1,0:T(8,128)(2,1)S(1)}, u32[]{:S(2)}, u32[]{:S(2)}) collective-permute-start(bf16[288,1152]{1,0:T(8,128)(2,1)} %get-tuple-element.156.p2_ref), channel_id=1, source_target_pairs={{0,2},{2,0},{1,3},{3,1},{4,6},{6,4},{5,7},{7,5},{8,10},{10,8},{9,1... | collective-permute-start | bytes 1990664 | tf_op jit(solution)/shard_map/ppermute | solution.py:66
  126.5 10.6 %collective-permute-start.31 = (bf16[144,1024]{1,0:T(8,128)(2,1)S(1)}, bf16[144,1024]{1,0:T(8,128)(2,1)S(1)}, u32[]{:S(2)}, u32[]{:S(2)}) collective-permute-start(bf16[144,1024]{1,0:T(8,128)(2,1)S(1)} %get-tuple-element.165.refs_6_.refs_2_), channel_id=1, source_target_pairs={{0,1},{1,0},{2,3},{3,2},{4,5},{5,4},{6,7},{7,6},{8,9},{9,8},{10,11... | collective-permute-start | bytes 884744 | tf_op jit(solution)/shard_map/ppermute | solution.py:66
  127.0 10.2 %collective-permute-start.30 = (bf16[144,1024]{1,0:T(8,128)(2,1)S(1)}, bf16[144,1024]{1,0:T(8,128)(2,1)S(1)}, u32[]{:S(2)}, u32[]{:S(2)}) collective-permute-start(bf16[144,1024]{1,0:T(8,128)(2,1)S(1)} %collective-permute-done.29.refs_4_.refs_0_), channel_id=1, source_target_pairs={{0,1},{1,0},{2,3},{3,2},{4,5},{5,4},{6,7},{7,6},{8,9},{9,8},{10,11... | collective-permute-start | bytes 884744 | tf_op jit(solution)/shard_map/ppermute | solution.py:66
  127.0 10.2 %collective-permute-start.34 = (bf16[144,1024]{1,0:T(8,128)(2,1)S(1)}, bf16[144,1024]{1,0:T(8,128)(2,1)S(1)}, u32[]{:S(2)}, u32[]{:S(2)}) collective-permute-start(bf16[144,1024]{1,0:T(8,128)(2,1)S(1)} %get-tuple-element.169.refs_10_.refs_6_), channel_id=1, source_target_pairs={{0,1},{1,0},{2,3},{3,2},{4,5},{5,4},{6,7},{7,6},{8,9},{9,8},{10,11... | collective-permute-start | bytes 884744 | tf_op jit(solution)/shard_map/ppermute | solution.py:66
  163.5 15.7 %collective-permute-start.40 = (bf16[256,1152]{1,0:T(8,128)(2,1)S(1)}, bf16[256,1152]{1,0:T(8,128)(2,1)S(1)}, u32[]{:S(2)}, u32[]{:S(2)}) collective-permute-start(bf16[256,1152]{1,0:T(8,128)(2,1)S(1)} %add_convert_fusion.2), channel_id=1, source_target_pairs={{0,2},{2,0},{1,3},{3,1},{4,6},{6,4},{5,7},{7,5},{8,10},{10,8},{9,1... | collective-permute-start | bytes 1769480 | tf_op jit(solution)/shard_map/ppermute | solution.py:66
  171.1 28.8 %collective-permute-start.37 = (bf16[256,1152]{1,0:T(8,128)(2,1)}, bf16[256,1152]{1,0:T(8,128)(2,1)}, u32[]{:S(2)}, u32[]{:S(2)}) collective-permute-start(bf16[256,1152]{1,0:T(8,128)(2,1)} %get-tuple-element.190), channel_id=1, source_target_pairs={{0,1},{1,0},{2,3},{3,2},{4,5},{5,4},{6,7},{7,6},{8,9},{9,8},{10,11... | collective-permute-start | bytes 1769480 | tf_op jit(solution)/shard_map/ppermute | solution.py:66
  184.8 15.1 %collective-permute-start.41 = (bf16[256,1152]{1,0:T(8,128)(2,1)}, bf16[256,1152]{1,0:T(8,128)(2,1)}, u32[]{:S(2)}, u32[]{:S(2)}) collective-permute-start(bf16[256,1152]{1,0:T(8,128)(2,1)} %get-tuple-element.195.g2_ref), channel_id=1, source_target_pairs={{0,2},{2,0},{1,3},{3,1},{4,6},{6,4},{5,7},{7,5},{8,10},{10,8},{9,1... | collective-permute-start | bytes 1769480 | tf_op jit(solution)/shard_map/ppermute | solution.py:66
  191.6 13.1 %collective-permute-start.43 = (bf16[256,1152]{1,0:T(8,128)(2,1)}, bf16[256,1152]{1,0:T(8,128)(2,1)}, u32[]{:S(2)}, u32[]{:S(2)}) collective-permute-start(bf16[256,1152]{1,0:T(8,128)(2,1)} %get-tuple-element.195.g2_ref), channel_id=1, source_target_pairs={{0,1},{1,0},{2,3},{3,2},{4,5},{5,4},{6,7},{7,6},{8,9},{9,8},{10,11... | collective-permute-start | bytes 1769480 | tf_op jit(solution)/shard_map/ppermute | solution.py:66
  202.1 27.6 %collective-permute-start.38 = (bf16[256,1152]{1,0:T(8,128)(2,1)}, bf16[256,1152]{1,0:T(8,128)(2,1)S(1)}, u32[]{:S(2)}, u32[]{:S(2)}) collective-permute-start(bf16[256,1152]{1,0:T(8,128)(2,1)} %add_convert_fusion.1), channel_id=1, source_target_pairs={{0,2},{2,0},{1,3},{3,1},{4,6},{6,4},{5,7},{7,5},{8,10},{10,8},{9,1... | collective-permute-start | bytes 1769480 | tf_op jit(solution)/shard_map/ppermute | solution.py:66
  203.5 26.2 %collective-permute-start.36 = (bf16[256,1152]{1,0:T(8,128)(2,1)}, bf16[256,1152]{1,0:T(8,128)(2,1)S(1)}, u32[]{:S(2)}, u32[]{:S(2)}) collective-permute-start(bf16[256,1152]{1,0:T(8,128)(2,1)} %get-tuple-element.188), channel_id=1, source_target_pairs={{0,1},{1,0},{2,3},{3,2},{4,5},{5,4},{6,7},{7,6},{8,9},{9,8},{10,11... | collective-permute-start | bytes 1769480 | tf_op jit(solution)/shard_map/ppermute | solution.py:66
  240.2 12.9 %collective-permute-start.47 = (bf16[128,1152]{1,0:T(8,128)(2,1)S(1)}, bf16[128,1152]{1,0:T(8,128)(2,1)S(1)}, u32[]{:S(2)}, u32[]{:S(2)}) collective-permute-start(bf16[128,1152]{1,0:T(8,128)(2,1)S(1)} %constant_dynamic-slice_fusion.18), channel_id=1, source_target_pairs={{0,8},{8,16},{16,24},{24,28},{28,20},{20,12},{12,4},{4,0},{1,9},{9... | collective-permute-start | bytes 884744 | tf_op jit(solution)/shard_map/ppermute | solution.py:238
  242.6 10.5 %collective-permute-start.44 = (bf16[256,1152]{1,0:T(8,128)(2,1)S(1)}, bf16[256,1152]{1,0:T(8,128)(2,1)S(1)}, u32[]{:S(2)}, u32[]{:S(2)}) collective-permute-start(bf16[256,1152]{1,0:T(8,128)(2,1)S(1)} %slice.217), channel_id=1, source_target_pairs={{0,1},{1,0},{2,3},{3,2},{4,5},{5,4},{6,7},{7,6},{8,9},{9,8},{10,11... | collective-permute-start | bytes 1769480 | tf_op jit(solution)/shard_map/ppermute | solution.py:66
  253.2 14.8 %collective-permute-start.46 = (bf16[256,1152]{1,0:T(8,128)(2,1)S(1)}, bf16[256,1152]{1,0:T(8,128)(2,1)S(1)}, u32[]{:S(2)}, u32[]{:S(2)}) collective-permute-start(bf16[256,1152]{1,0:T(8,128)(2,1)S(1)} %add_convert_fusion), channel_id=1, source_target_pairs={{0,2},{2,0},{1,3},{3,1},{4,6},{6,4},{5,7},{7,5},{8,10},{10,8},{9,1... | collective-permute-start | bytes 1769480 | tf_op jit(solution)/shard_map/ppermute | solution.py:66
  257.1 19.4 %collective-permute-start.50 = (bf16[112,1152]{1,0:T(8,128)(2,1)S(1)}, bf16[112,1152]{1,0:T(8,128)(2,1)S(1)}, u32[]{:S(2)}, u32[]{:S(2)}) collective-permute-start(bf16[112,1152]{1,0:T(8,128)(2,1)S(1)} %add_convert_fusion.14), channel_id=1, source_target_pairs={{0,4},{8,0},{16,8},{24,16},{28,24},{20,28},{12,20},{4,12},{1,5},{9... | collective-permute-start | bytes 774152 | tf_op jit(solution)/shard_map/ppermute | solution.py:238
  259.2 17.3 %collective-permute-start.49 = (bf16[128,1152]{1,0:T(8,128)(2,1)S(1)}, bf16[128,1152]{1,0:T(8,128)(2,1)S(1)}, u32[]{:S(2)}, u32[]{:S(2)}) collective-permute-start(bf16[128,1152]{1,0:T(8,128)(2,1)S(1)} %add_convert_fusion.8), channel_id=1, source_target_pairs={{0,8},{8,16},{16,24},{24,28},{28,20},{20,12},{12,4},{4,0},{1,9},{9... | collective-permute-start | bytes 884744 | tf_op jit(solution)/shard_map/ppermute | solution.py:238
  281.6 9.7 %collective-permute-start.51 = (bf16[128,1152]{1,0:T(8,128)(2,1)S(1)}, bf16[128,1152]{1,0:T(8,128)(2,1)S(1)}, u32[]{:S(2)}, u32[]{:S(2)}) collective-permute-start(bf16[128,1152]{1,0:T(8,128)(2,1)S(1)} %add_convert_fusion.7), channel_id=1, source_target_pairs={{0,8},{8,16},{16,24},{24,28},{28,20},{20,12},{12,4},{4,0},{1,9},{9... | collective-permute-start | bytes 884744 | tf_op jit(solution)/shard_map/ppermute | solution.py:238
  283.6 21.8 %collective-permute-start.62 = (bf16[288,384]{1,0:T(8,128)(2,1)S(1)}, bf16[288,384]{1,0:T(8,128)(2,1)S(1)}, u32[]{:S(2)}, u32[]{:S(2)}) collective-permute-start(bf16[288,384]{1,0:T(8,128)(2,1)S(1)} %pad_maximum_fusion.3), channel_id=1, source_target_pairs={{0,2},{2,0},{1,3},{3,1},{4,6},{6,4},{5,7},{7,5},{8,10},{10,8},{9,1... | collective-permute-start | bytes 663560 | tf_op jit(solution)/shard_map/ppermute | solution.py:66
  (157 other events, 1338.7 us)
Sparse Core Ops, SparseCore 0:
  78.6 65.2 all-gather.1
  191.7 83.6 reduce-scatter.1

commit v5 on v4

--- a/solution.py
+++ b/solution.py
@@ -1139,14 +1139,15 @@
     )
     g_gu = weight_grad(mlp_in, after(grad_gu, grad_att), 5)
     g_down = weight_grad(hidden, after(grad_branch, g_gu), 3)
-    att_far = after(swap(grad_att, "ty"), g_gu, g_down)
+    branch_pair = tile_pair((far[3], far[2]))
+    att_far = after(swap(grad_att, "ty"), g_gu, g_down, branch_pair)
     grad_att_tiles = [att_far, swap(att_far, "tx"), grad_att, swap(grad_att, "tx")]
 
     grad_qkv, gains = attention_backward(
         grad_att_tiles, out_rows, qraw, kraw, (q0, q1), (k0, k1), (v0, v1), (mixedp0, mixedp1),
         cos, sin, gq, gk, spread,
     )
-    branch_parts = tile_sum_parts(tile_pair((far[3], far[2])), (own_tile[2], beside_tile[2]))
+    branch_parts = tile_sum_parts(branch_pair, (own_tile[2], beside_tile[2]))
     grad_qkv = after(grad_qkv, branch_parts)
     w_back = full_first[:, : 3 * COLS]
     g_first = first_grad(tile_word, grad_att_tiles, mixed, attn_in, grad_qkv)

time: 362 us -> 366 us (1.011)
    ppermute x14, waiting for transfers between devices: 26.5 us -> 33.5 us  [ring_scatter(): lax.ppermute(sums[k], 'img', ring_perm(count, sign))]
    ppermute x7, waiting for transfers between devices: 5.37 us -> 0.15 us  [ring_gather(): a = lax.ppermute(a, 'img', ring_perm(count, 1))]
    unnamed x219 -> x215, local copies, waits for them, and re-layouts: 24.4 us -> 25.3 us
  transfers between devices with their start and end apart: 76 -> 76, of which waited for: 41 -> 37; matrix products, arithmetic and copies ran while one was open for 7% -> 7% of each run, Pallas kernels for 28% -> 25%
where the time goes in v5:
time: 366 us; the launch traced here: 360 us
  Pallas kernels  114 us (31%)
  waiting for transfers between devices  105 us (29%)
  starting transfers between devices  71.1 us (19%)
  local copies, waits for them, and re-layouts  36.9 us (10%)
  between operations  16.4 us (4%)
  other arithmetic  12.5 us (3%)
    ppermute x34, waiting for transfers between devices, swap(): return lax.ppermute(values, axis, [(0, 1), (1, 0)])  34 us
    ppermute x14, waiting for transfers between devices, ring_scatter(): lax.ppermute(sums[k], 'img', ring_perm(count, sign))  33.5 us
    pallas_call x3, Pallas kernels, mlp(): pl.pallas_call(functools.partial(mlp_kernel, places), grid=(1,), out_shap...  26.2 us
    unnamed x215, local copies, waits for them, and re-layouts  25.3 us
    pallas_call x1, Pallas kernels, attention_backward(): pl.pallas_call(attention_back_kernel, out_shape=[jax.ShapeDtypeStruct((to...  24.7 us
    ppermute x7, waiting for transfers between devices, ring_gather(): b = lax.ppermute(b, 'img', ring_perm(count, -1))  22.4 us
    ppermute x34, starting transfers between devices, swap(): return lax.ppermute(values, axis, [(0, 1), (1, 0)])  20.5 us
    ppermute x14, starting transfers between devices, ring_scatter(): lax.ppermute(sums[k], 'img', ring_perm(count, sign))  17 us
  transfers between devices with their start and end apart: 76, of which 37 were waited for; matrix products, arithmetic and copies ran while one was open for 7% of the time, Pallas kernels for 25%

profile of v5, /device:TPU:0, one launch (start us, length us, event | category | flops | bytes accessed | tf_op | source)
XLA Modules:
  0.0 359.9 jit_solution(266513316153252231)
XLA Ops:
  16.9 5.3 %collective-permute-done.3 = bf16[2,1152]{1,0:T(2,128)(2,1)S(1)} collective-permute-done((bf16[2,1152]{1,0:T(2,128)(2,1)S(1)}, bf16[2,1152]{1,0:T(2,128)(2,1)S(1)}, u32[]{:S(2)}, u32[]{:S(2)}) %collective-permute-start.3) | collective-permute-done | bytes 4640 | tf_op jit(solution)/shard_map/ppermute | solution.py:1063
  41.5 5.8 %collective-permute-done.8.refs_10_ = bf16[112,1152]{1,0:T(8,128)(2,1)S(1)} collective-permute-done((bf16[112,1152]{1,0:T(8,128)(2,1)S(1)}, bf16[112,1152]{1,0:T(8,128)(2,1)S(1)}, u32[]{:S(2)}, u32[]{:S(2)}) %collective-permute-start.8) | collective-permute-done | bytes 258080 | tf_op jit(solution)/shard_map/ppermute | solution.py:152
  52.7 4.6 %collective-permute-done.14.refs_11_ = bf16[112,1152]{1,0:T(8,128)(2,1)S(1)} collective-permute-done((bf16[112,1152]{1,0:T(8,128)(2,1)S(1)}, bf16[112,1152]{1,0:T(8,128)(2,1)S(1)}, u32[]{:S(2)}, u32[]{:S(2)}) %collective-permute-start.14) | collective-permute-done | bytes 258080 | tf_op jit(solution)/shard_map/ppermute | solution.py:152
  60.3 4.7 %collective-permute-done.21.dy0_ref = bf16[256,1152]{1,0:T(8,128)(2,1)S(1)} collective-permute-done((bf16[256,1152]{1,0:T(8,128)(2,1)S(1)}, bf16[256,1152]{1,0:T(8,128)(2,1)S(1)}, u32[]{:S(2)}, u32[]{:S(2)}) %collective-permute-start.21) | collective-permute-done | bytes 589856 | tf_op jit(solution)/shard_map/ppermute | solution.py:66
  72.0 4.9 %collective-permute-done.20.refs_13_ = bf16[112,1152]{1,0:T(8,128)(2,1)} collective-permute-done((bf16[112,1152]{1,0:T(8,128)(2,1)}, bf16[112,1152]{1,0:T(8,128)(2,1)}, u32[]{:S(2)}, u32[]{:S(2)}) %collective-permute-start.20) | collective-permute-done | bytes 258080 | tf_op jit(solution)/shard_map/ppermute | solution.py:152
  82.8 4.5 %collective-permute-done.25.refs_14_ = bf16[112,1152]{1,0:T(8,128)(2,1)S(1)} collective-permute-done((bf16[112,1152]{1,0:T(8,128)(2,1)}, bf16[112,1152]{1,0:T(8,128)(2,1)S(1)}, u32[]{:S(2)}, u32[]{:S(2)}) %collective-permute-start.25) | collective-permute-done | bytes 258080 | tf_op jit(solution)/shard_map/ppermute | solution.py:152
  88.7 6.1 %assemble_first.1 = (bf16[1152,1152]{1,0:T(8,128)(2,1)}, bf16[768,1152]{1,0:T(8,128)(2,1)}, bf16[288,1152]{1,0:T(8,128)(2,1)}) custom-call(s32[15]{0:T(128)} %compare_select_fusion.2.index_ref, bf16[288,384]{1,0:T(8,128)(2,1)} %constant.271.clone.pick_ref, bf16[240,1152]{1,0:T(8,128)(2,1)} %copy-done.58, bf16[128,1152]{1,0:T(8,128)(2,1)} %collective-permute-done.1.refs_1_, ...), custom_call_target="tpu_custom_call" | custom-call | flops 5500000256 | bytes 15000000 | tf_op jit(solution)/shard_map/assemble_first/pallas_call | solution.py:195
  100.3 10.6 %project.1 = (bf16[1024,1152]{1,0:T(8,128)(2,1)S(1)}, f32[1024,512]{1,0:T(8,128)S(1)}, f32[1024,512]{1,0:T(8,128)S(1)}, bf16[1024,256]{1,0:T(8,128)(2,1)S(1)}, b...) custom-call(bf16[256,1152]{1,0:T(8,128)(2,1)} %collective-permute-do, ...), custom_call_target="tpu_custom_call" | custom-call | flops 17600000000 | bytes 48000000 | tf_op jit(solution)/shard_map/project/pallas_call | solution.py:365
  111.5 3.5 attend.2
  124.8 6.5 %collective-permute-done.32.refs_8_.refs_4_ = bf16[144,1024]{1,0:T(8,128)(2,1)S(1)} collective-permute-done((bf16[144,1024]{1,0:T(8,128)(2,1)S(1)}, bf16[144,1024]{1,0:T(8,128)(2,1)S(1)}, u32[]{:S(2)}, u32[]{:S(2)}) %collective-permute-start.32) | collective-permute-done | bytes 294944 | tf_op jit(solution)/shard_map/ppermute | solution.py:66
  135.1 8.9 %residual.1 = (bf16[1024,1152]{1,0:T(8,128)(2,1)}, f32[256,1152]{1,0:T(8,128)}) custom-call(s32[1]{0:T(128)} %bitcast.2.tile_ref, f32[8,1152]{1,0:T(8,128)} %copy-done.29, bf16[1152,1152]{1,0:T(8,128)(2,1)} %copy-done.51, bf16[256,1152]{1,0:T(8,128)(2,1)} %collective-permute-done.10.x0_ref.refs_0_, bf16[256,1152]{1,0:T(8,128)(2,1)} %copy-done.40, ...), custom_call_target="tpu_custom_call" | custom-call | flops 9900000256 | bytes 27000000 | tf_op jit(solution)/shard_map/residual/pallas_call | solution.py:606
  143.9 12.3 %mlp.3 = (bf16[1024,768]{1,0:T(8,128)(2,1)}, bf16[1024,1536]{1,0:T(8,128)(2,1)}, bf16[256,1152]{1,0:T(8,128)(2,1)}, bf16[256,1152]{1,0:T(8,128)(2,1)}, bf16[256,...) custom-call(bf16[1152,1536]{1,0:T(8,128)(2,1)} %all-gather.2.cloned.1.call-done.wgu_ref, ...), custom_call_target="tpu_custom_call" | custom-call | flops 13200000000 | bytes 36000000 | tf_op jit(solution)/shard_map/mlp/pallas_call | solution.py:660
  159.7 6.9 %mlp.4 = (bf16[1024,768]{1,0:T(8,128)(2,1)}, bf16[1024,1536]{1,0:T(8,128)(2,1)}, bf16[256,1152]{1,0:T(8,128)(2,1)}, bf16[256,1152]{1,0:T(8,128)(2,1)}) custom-call(bf16[1152,1536]{1,0:T(8,128)(2,1)} %all-gather.2.cloned.1.call-done.wgu_ref, bf16[768,1152]{1,0:T(8,128)(2,1)} %get-tuple-element.154.wdown_ref, ...), custom_call_target="tpu_custom_call", output_to_operand_aliasing={{0}: (4, {}), {1}: (5, {})} | custom-call | flops 330000000 | bytes 900000 | tf_op jit(solution)/shard_map/mlp/pallas_call | solution.py:660
  168.5 7.0 %mlp.5 = (bf16[1024,768]{1,0:T(8,128)(2,1)}, bf16[1024,1536]{1,0:T(8,128)(2,1)}, bf16[256,1152]{1,0:T(8,128)(2,1)}, bf16[256,1152]{1,0:T(8,128)(2,1)}) custom-call(bf16[1152,1536]{1,0:T(8,128)(2,1)} %all-gather.2.cloned.1.call-done.wgu_ref, bf16[768,1152]{1,0:T(8,128)(2,1)} %get-tuple-element.154.wdown_ref, ...), custom_call_target="tpu_custom_call", output_to_operand_aliasing={{0}: (4, {}), {1}: (5, {})} | custom-call | flops 330000000 | bytes 900000 | tf_op jit(solution)/shard_map/mlp/pallas_call | solution.py:660
  175.5 6.8 %collective-permute-done.40.c_ref = bf16[256,1152]{1,0:T(8,128)(2,1)S(1)} collective-permute-done((bf16[256,1152]{1,0:T(8,128)(2,1)S(1)}, bf16[256,1152]{1,0:T(8,128)(2,1)S(1)}, u32[]{:S(2)}, u32[]{:S(2)}) %collective-permute-start.40) | collective-permute-done | bytes 589856 | tf_op jit(solution)/shard_map/ppermute | solution.py:66
  183.4 3.5 middle.1
  189.5 4.1 %weight_grad.2 = bf16[1152,1536]{1,0:T(8,128)(2,1)S(1)} custom-call(bf16[1024,1152]{1,0:T(8,128)(2,1)S(1)} %copy-done.5, bf16[1024,1536]{1,0:T(8,128)(2,1)S(1)} %copy-done.2), custom_call_target="tpu_custom_call" | custom-call | flops 5500000256 | bytes 15000000 | tf_op jit(solution)/shard_map/weight_grad/pallas_call | solution.py:813
  208.1 24.7 %attention_backward.1 = (bf16[1024,864]{1,0:T(8,128)(2,1)}, f32[8,128]{1,0:T(8,128)}) custom-call(bf16[256,1152]{1,0:T(8,128)(2,1)} %collective-permute-done.41.g0_ref, bf16[256,1152]{1,0:T(8,128)(2,1)} %copy-done.57, bf16[256,1152]{1,0:T(8,128)(2,1)} %get-tuple-element.195.g2_ref, bf16[256,1152]{1,0:T(8,128)(2,1)} %collective-permute-done.43.g3_ref, ...), custom_call_target="tpu_custom_call" | custom-call | flops 1100000000 | bytes 3000000 | tf_op jit(solution)/shard_map/attention_backward/pallas_call | solution.py:506
  232.8 9.8 %first_grad.1 = bf16[1152,1152]{1,0:T(8,128)(2,1)} custom-call(s32[1]{0:T(128)} %bitcast.2.tile_ref, bf16[256,1152]{1,0:T(8,128)(2,1)} %collective-permute-done.41.g0_ref, bf16[256,1152]{1,0:T(8,128)(2,1)} %copy-done.57, bf16[256,1152]{1,0:T(8,128)(2,1)} %get-tuple-element.195.g2_ref, bf16[256,1152]{1,0:T(8,128)(2,1)} %collective-permute-done.43.g3_ref, ...), custom_call_target="tpu_custom_call" | custom-call | flops 1100000000 | bytes 3000000 | tf_op jit(solution)/shard_map/first_grad/pallas_call | solution.py:794
  264.6 7.1 %collective-permute-done.46.c_ref = bf16[256,1152]{1,0:T(8,128)(2,1)S(1)} collective-permute-done((bf16[256,1152]{1,0:T(8,128)(2,1)S(1)}, bf16[256,1152]{1,0:T(8,128)(2,1)S(1)}, u32[]{:S(2)}, u32[]{:S(2)}) %collective-permute-start.46) | collective-permute-done | bytes 589856 | tf_op jit(solution)/shard_map/ppermute | solution.py:66
  288.8 5.6 %collective-permute-done.51 = bf16[128,1152]{1,0:T(8,128)(2,1)S(1)} collective-permute-done((bf16[128,1152]{1,0:T(8,128)(2,1)S(1)}, bf16[128,1152]{1,0:T(8,128)(2,1)S(1)}, u32[]{:S(2)}, u32[]{:S(2)}) %collective-permute-start.51) | collective-permute-done | bytes 294944 | tf_op jit(solution)/shard_map/ppermute | solution.py:238
  298.7 4.0 %collective-permute-done.56 = bf16[112,1152]{1,0:T(8,128)(2,1)S(1)} collective-permute-done((bf16[112,1152]{1,0:T(8,128)(2,1)S(1)}, bf16[112,1152]{1,0:T(8,128)(2,1)S(1)}, u32[]{:S(2)}, u32[]{:S(2)}) %collective-permute-start.56) | collective-permute-done | bytes 258080 | tf_op jit(solution)/shard_map/ppermute | solution.py:238
  308.3 3.8 %collective-permute-done.60 = bf16[112,1152]{1,0:T(8,128)(2,1)S(1)} collective-permute-done((bf16[112,1152]{1,0:T(8,128)(2,1)S(1)}, bf16[112,1152]{1,0:T(8,128)(2,1)S(1)}, u32[]{:S(2)}, u32[]{:S(2)}) %collective-permute-start.60) | collective-permute-done | bytes 258080 | tf_op jit(solution)/shard_map/ppermute | solution.py:238
  329.4 4.2 %collective-permute-done.67 = bf16[112,1152]{1,0:T(8,128)(2,1)S(1)} collective-permute-done((bf16[112,1152]{1,0:T(8,128)(2,1)S(1)}, bf16[112,1152]{1,0:T(8,128)(2,1)S(1)}, u32[]{:S(2)}, u32[]{:S(2)}) %collective-permute-start.67) | collective-permute-done | bytes 258080 | tf_op jit(solution)/shard_map/ppermute | solution.py:238
  (452 shorter events, 178.4 us)
Async XLA Ops:
  7.2 136.7 %all-gather.2.cloned.1.call-start = ((), (), s32[]{:S(2)}) async-start(), calls=%async_computation.1 | async-start | bytes 3981312 | tf_op jit(solution)/shard_map/all_gather | solution.py:1098
  13.0 9.3 %collective-permute-start.1 = (bf16[128,1152]{1,0:T(8,128)(2,1)S(1)}, bf16[128,1152]{1,0:T(8,128)(2,1)}, u32[]{:S(2)}, u32[]{:S(2)}) collective-permute-start(bf16[128,1152]{1,0:T(8,128)(2,1)S(1)} %slice.165), channel_id=1, source_target_pairs={{0,8},{8,16},{16,24},{24,28},{28,20},{20,12},{12,4},{4,0},{1,9},{9... | collective-permute-start | bytes 884744 | tf_op jit(solution)/shard_map/ppermute | solution.py:151
  22.3 10.2 %collective-permute-start.4 = (bf16[128,1152]{1,0:T(8,128)(2,1)}, bf16[128,1152]{1,0:T(8,128)(2,1)}, u32[]{:S(2)}, u32[]{:S(2)}) collective-permute-start(bf16[128,1152]{1,0:T(8,128)(2,1)} %collective-permute-done.1.refs_1_), channel_id=1, source_target_pairs={{0,8},{8,16},{16,24},{24,28},{28,20},{20,12},{12,4},{4,0},{1,9},{9... | collective-permute-start | bytes 884744 | tf_op jit(solution)/shard_map/ppermute | solution.py:151
  24.4 13.2 %collective-permute-start.10 = (bf16[256,1152]{1,0:T(8,128)(2,1)}, bf16[256,1152]{1,0:T(8,128)(2,1)}, u32[]{:S(2)}, u32[]{:S(2)}) collective-permute-start(bf16[256,1152]{1,0:T(8,128)(2,1)} %bitcast.x2_ref.refs_2_.x_ref), channel_id=1, source_target_pairs={{0,2},{2,0},{1,3},{3,1},{4,6},{6,4},{5,7},{7,5},{8,10},{10,8},{9,1... | collective-permute-start | bytes 1769480 | tf_op jit(solution)/shard_map/ppermute | solution.py:66
  37.5 9.8 %collective-permute-start.7 = (bf16[128,1152]{1,0:T(8,128)(2,1)}, bf16[128,1152]{1,0:T(8,128)(2,1)S(1)}, u32[]{:S(2)}, u32[]{:S(2)}) collective-permute-start(bf16[128,1152]{1,0:T(8,128)(2,1)} %collective-permute-done.4.refs_2_), channel_id=1, source_target_pairs={{0,8},{8,16},{16,24},{24,28},{28,20},{20,12},{12,4},{4,0},{1,9},{9... | collective-permute-start | bytes 884744 | tf_op jit(solution)/shard_map/ppermute | solution.py:151
  51.2 13.8 %collective-permute-start.21 = (bf16[256,1152]{1,0:T(8,128)(2,1)S(1)}, bf16[256,1152]{1,0:T(8,128)(2,1)S(1)}, u32[]{:S(2)}, u32[]{:S(2)}) collective-permute-start(bf16[256,1152]{1,0:T(8,128)(2,1)S(1)} %bitcast.25), channel_id=1, source_target_pairs={{0,2},{2,0},{1,3},{3,1},{4,6},{6,4},{5,7},{7,5},{8,10},{10,8},{9,1... | collective-permute-start | bytes 1769480 | tf_op jit(solution)/shard_map/ppermute | solution.py:66
  58.3 13.8 %collective-permute-start.23 = (bf16[256,1152]{1,0:T(8,128)(2,1)S(1)}, bf16[256,1152]{1,0:T(8,128)(2,1)S(1)}, u32[]{:S(2)}, u32[]{:S(2)}) collective-permute-start(bf16[256,1152]{1,0:T(8,128)(2,1)S(1)} %bitcast.26), channel_id=1, source_target_pairs={{0,1},{1,0},{2,3},{3,2},{4,5},{5,4},{6,7},{7,6},{8,9},{9,8},{10,11... | collective-permute-start | bytes 1769480 | tf_op jit(solution)/shard_map/ppermute | solution.py:66
  58.3 9.5 %collective-permute-start.16 = (bf16[128,1152]{1,0:T(8,128)(2,1)S(1)}, bf16[128,1152]{1,0:T(8,128)(2,1)}, u32[]{:S(2)}, u32[]{:S(2)}) collective-permute-start(bf16[128,1152]{1,0:T(8,128)(2,1)S(1)} %collective-permute-done.13.refs_4_), channel_id=1, source_target_pairs={{0,8},{8,16},{16,24},{24,28},{28,20},{20,12},{12,4},{4,0},{1,9},{9... | collective-permute-start | bytes 884744 | tf_op jit(solution)/shard_map/ppermute | solution.py:151
  77.0 200.2 %reduce-scatter.2.cloned.1.call-start = ((), (), s32[]{:S(2)}) async-start(), calls=%async_computation.2 | async-start | bytes 3981312 | tf_op jit(solution)/shard_map/reduce_scatter | solution.py:1187
  94.8 16.2 %collective-permute-start.26 = (bf16[288,1152]{1,0:T(8,128)(2,1)}, bf16[288,1152]{1,0:T(8,128)(2,1)S(1)}, u32[]{:S(2)}, u32[]{:S(2)}) collective-permute-start(bf16[288,1152]{1,0:T(8,128)(2,1)} %get-tuple-element.156.p2_ref), channel_id=1, source_target_pairs={{0,2},{2,0},{1,3},{3,1},{4,6},{6,4},{5,7},{7,5},{8,10},{10,8},{9,1... | collective-permute-start | bytes 1990664 | tf_op jit(solution)/shard_map/ppermute | solution.py:66
  96.3 19.3 %collective-permute-start.28 = (bf16[288,1152]{1,0:T(8,128)(2,1)}, bf16[288,1152]{1,0:T(8,128)(2,1)S(1)}, u32[]{:S(2)}, u32[]{:S(2)}) collective-permute-start(bf16[288,1152]{1,0:T(8,128)(2,1)} %get-tuple-element.156.p2_ref), channel_id=1, source_target_pairs={{0,1},{1,0},{2,3},{3,2},{4,5},{5,4},{6,7},{7,6},{8,9},{9,8},{10,11... | collective-permute-start | bytes 1990664 | tf_op jit(solution)/shard_map/ppermute | solution.py:66
  124.2 9.2 %collective-permute-start.31 = (bf16[144,1024]{1,0:T(8,128)(2,1)S(1)}, bf16[144,1024]{1,0:T(8,128)(2,1)S(1)}, u32[]{:S(2)}, u32[]{:S(2)}) collective-permute-start(bf16[144,1024]{1,0:T(8,128)(2,1)S(1)} %get-tuple-element.165.refs_6_.refs_2_), channel_id=1, source_target_pairs={{0,1},{1,0},{2,3},{3,2},{4,5},{5,4},{6,7},{7,6},{8,9},{9,8},{10,11... | collective-permute-start | bytes 884744 | tf_op jit(solution)/shard_map/ppermute | solution.py:66
  167.0 15.4 %collective-permute-start.40 = (bf16[256,1152]{1,0:T(8,128)(2,1)S(1)}, bf16[256,1152]{1,0:T(8,128)(2,1)S(1)}, u32[]{:S(2)}, u32[]{:S(2)}) collective-permute-start(bf16[256,1152]{1,0:T(8,128)(2,1)S(1)} %add_convert_fusion.2), channel_id=1, source_target_pairs={{0,2},{2,0},{1,3},{3,1},{4,6},{6,4},{5,7},{7,5},{8,10},{10,8},{9,1... | collective-permute-start | bytes 1769480 | tf_op jit(solution)/shard_map/ppermute | solution.py:66
  168.5 26.9 %collective-permute-start.37 = (bf16[256,1152]{1,0:T(8,128)(2,1)}, bf16[256,1152]{1,0:T(8,128)(2,1)}, u32[]{:S(2)}, u32[]{:S(2)}) collective-permute-start(bf16[256,1152]{1,0:T(8,128)(2,1)} %get-tuple-element.190), channel_id=1, source_target_pairs={{0,1},{1,0},{2,3},{3,2},{4,5},{5,4},{6,7},{7,6},{8,9},{9,8},{10,11... | collective-permute-start | bytes 1769480 | tf_op jit(solution)/shard_map/ppermute | solution.py:66
  187.9 15.4 %collective-permute-start.41 = (bf16[256,1152]{1,0:T(8,128)(2,1)}, bf16[256,1152]{1,0:T(8,128)(2,1)}, u32[]{:S(2)}, u32[]{:S(2)}) collective-permute-start(bf16[256,1152]{1,0:T(8,128)(2,1)} %get-tuple-element.195.g2_ref), channel_id=1, source_target_pairs={{0,2},{2,0},{1,3},{3,1},{4,6},{6,4},{5,7},{7,5},{8,10},{10,8},{9,1... | collective-permute-start | bytes 1769480 | tf_op jit(solution)/shard_map/ppermute | solution.py:66
  203.9 28.9 %collective-permute-start.38 = (bf16[256,1152]{1,0:T(8,128)(2,1)}, bf16[256,1152]{1,0:T(8,128)(2,1)S(1)}, u32[]{:S(2)}, u32[]{:S(2)}) collective-permute-start(bf16[256,1152]{1,0:T(8,128)(2,1)} %add_convert_fusion.1), channel_id=1, source_target_pairs={{0,2},{2,0},{1,3},{3,1},{4,6},{6,4},{5,7},{7,5},{8,10},{10,8},{9,1... | collective-permute-start | bytes 1769480 | tf_op jit(solution)/shard_map/ppermute | solution.py:66
  204.4 28.4 %collective-permute-start.36 = (bf16[256,1152]{1,0:T(8,128)(2,1)}, bf16[256,1152]{1,0:T(8,128)(2,1)S(1)}, u32[]{:S(2)}, u32[]{:S(2)}) collective-permute-start(bf16[256,1152]{1,0:T(8,128)(2,1)} %get-tuple-element.188), channel_id=1, source_target_pairs={{0,1},{1,0},{2,3},{3,2},{4,5},{5,4},{6,7},{7,6},{8,9},{9,8},{10,11... | collective-permute-start | bytes 1769480 | tf_op jit(solution)/shard_map/ppermute | solution.py:66
  244.3 12.9 %collective-permute-start.44 = (bf16[256,1152]{1,0:T(8,128)(2,1)S(1)}, bf16[256,1152]{1,0:T(8,128)(2,1)S(1)}, u32[]{:S(2)}, u32[]{:S(2)}) collective-permute-start(bf16[256,1152]{1,0:T(8,128)(2,1)S(1)} %slice.217), channel_id=1, source_target_pairs={{0,1},{1,0},{2,3},{3,2},{4,5},{5,4},{6,7},{7,6},{8,9},{9,8},{10,11... | collective-permute-start | bytes 1769480 | tf_op jit(solution)/shard_map/ppermute | solution.py:66
  257.3 14.3 %collective-permute-start.46 = (bf16[256,1152]{1,0:T(8,128)(2,1)S(1)}, bf16[256,1152]{1,0:T(8,128)(2,1)S(1)}, u32[]{:S(2)}, u32[]{:S(2)}) collective-permute-start(bf16[256,1152]{1,0:T(8,128)(2,1)S(1)} %add_convert_fusion), channel_id=1, source_target_pairs={{0,2},{2,0},{1,3},{3,1},{4,6},{6,4},{5,7},{7,5},{8,10},{10,8},{9,1... | collective-permute-start | bytes 1769480 | tf_op jit(solution)/shard_map/ppermute | solution.py:66
  261.4 16.9 %collective-permute-start.50 = (bf16[112,1152]{1,0:T(8,128)(2,1)S(1)}, bf16[112,1152]{1,0:T(8,128)(2,1)S(1)}, u32[]{:S(2)}, u32[]{:S(2)}) collective-permute-start(bf16[112,1152]{1,0:T(8,128)(2,1)S(1)} %add_convert_fusion.14), channel_id=1, source_target_pairs={{0,4},{8,0},{16,8},{24,16},{28,24},{20,28},{12,20},{4,12},{1,5},{9... | collective-permute-start | bytes 774152 | tf_op jit(solution)/shard_map/ppermute | solution.py:238
  263.7 14.6 %collective-permute-start.49 = (bf16[128,1152]{1,0:T(8,128)(2,1)S(1)}, bf16[128,1152]{1,0:T(8,128)(2,1)S(1)}, u32[]{:S(2)}, u32[]{:S(2)}) collective-permute-start(bf16[128,1152]{1,0:T(8,128)(2,1)S(1)} %add_convert_fusion.8), channel_id=1, source_target_pairs={{0,8},{8,16},{16,24},{24,28},{28,20},{20,12},{12,4},{4,0},{1,9},{9... | collective-permute-start | bytes 884744 | tf_op jit(solution)/shard_map/ppermute | solution.py:238
  278.9 9.9 %collective-permute-start.52 = (bf16[112,1152]{1,0:T(8,128)(2,1)S(1)}, bf16[112,1152]{1,0:T(8,128)(2,1)S(1)}, u32[]{:S(2)}, u32[]{:S(2)}) collective-permute-start(bf16[112,1152]{1,0:T(8,128)(2,1)S(1)} %add_convert_fusion.13), channel_id=1, source_target_pairs={{0,4},{8,0},{16,8},{24,16},{28,24},{20,28},{12,20},{4,12},{1,5},{9... | collective-permute-start | bytes 774152 | tf_op jit(solution)/shard_map/ppermute | solution.py:238
  283.8 10.6 %collective-permute-start.51 = (bf16[128,1152]{1,0:T(8,128)(2,1)S(1)}, bf16[128,1152]{1,0:T(8,128)(2,1)S(1)}, u32[]{:S(2)}, u32[]{:S(2)}) collective-permute-start(bf16[128,1152]{1,0:T(8,128)(2,1)S(1)} %add_convert_fusion.7), channel_id=1, source_target_pairs={{0,8},{8,16},{16,24},{24,28},{28,20},{20,12},{12,4},{4,0},{1,9},{9... | collective-permute-start | bytes 884744 | tf_op jit(solution)/shard_map/ppermute | solution.py:238
  287.0 21.2 %collective-permute-start.62 = (bf16[288,384]{1,0:T(8,128)(2,1)S(1)}, bf16[288,384]{1,0:T(8,128)(2,1)S(1)}, u32[]{:S(2)}, u32[]{:S(2)}) collective-permute-start(bf16[288,384]{1,0:T(8,128)(2,1)S(1)} %pad_maximum_fusion.3), channel_id=1, source_target_pairs={{0,2},{2,0},{1,3},{3,1},{4,6},{6,4},{5,7},{7,5},{8,10},{10,8},{9,1... | collective-permute-start | bytes 663560 | tf_op jit(solution)/shard_map/ppermute | solution.py:66
  (155 other events, 1294.3 us)
Sparse Core Ops, SparseCore 0:
  77.1 65.2 all-gather.1
  195.5 81.5 reduce-scatter.1
